TPU v7x, 256 devices: a whole 4x4x8 slice. The times are simulated.
256 devices in a mesh: hst: 16 (over x, y), chip: 16 (over z, core).
Axes of the slice: x: 4, y: 4, z: 8, core: 2. Of those that a mesh axis runs over, the one named last changes fastest.
Arguments:
- top_input: bfloat16 [32768, 2048], P(('hst', 'chip')), may hold values from -24 to 24
- grad_hidden: bfloat16 [32768, 2048], P(('hst', 'chip')), may hold values from -0.59765625 to 0.59765625
- w_in: bfloat16 [2048, 2048], replicated, may hold values from -0.125 to 0.125
- b_in: float32 [2048], replicated, may hold values from -3 to 3
- slice_map: int32 [16], replicated, may hold values from 0 to 15, as said below
- lookup_ids: int32 [16, 4, 32768], P('hst'), may hold values from 0 to 4095
- bag_len: int32 [16, 32768], P('hst'), may hold values from 1 to 4
Outputs:
- w_in_grad: float32 [2048, 2048], P(('hst', 'chip'))
- table_grad: float32 [16, 4096, 128], P('hst', 'chip')
Inputs may be any that keep to these rules, and one draw needn't show every extreme that they name: slice_map is a permutation; slice s holds half slice_map[s] % 2 of table slice_map[s] // 2, and two slices of one table have the same lookup_ids and bag_len.
All inputs are finite; a program needn't handle non-finite values.
Results may differ from a plain program's by a relative error of at most 0.0041.
Values may be sent and summed in bfloat16 or wider, within the bound.
No kernel may reach another device: no remote copies, remote signals or barrier semaphores. Data moves between devices by JAX's collectives and lax.ppermute only.
A program may use at most 128 MiB of HBM per device.

v0:
```python
import math

import jax
import jax.numpy as jnp
from jax import lax
from jax.sharding import PartitionSpec as P

ROWS_DEV = 256


def count_block(row_ids, bag_lens, first, rows):
    target = first + lax.iota(jnp.int32, rows)[:, None]
    total = jnp.zeros((rows, row_ids.shape[1]), jnp.float32)
    for slot in range(row_ids.shape[0]):
        hit = (row_ids[slot][None, :] == target) & (slot < bag_lens)[None, :]
        total = total + hit.astype(jnp.float32)
    return total.astype(jnp.bfloat16)


def body(top_input, grad_hidden, w_in, b_in, slice_map, lookup_ids, bag_len):
    hosts = lax.axis_size("hst")
    chips = lax.axis_size("chip")
    b_dev = top_input.shape[0]
    width = top_input.shape[1]
    slices = slice_map.shape[0]
    s_here = lookup_ids.shape[0]
    slot_count = lookup_ids.shape[1]
    slw = width // slices
    pre_act = jnp.dot(top_input, w_in, preferred_element_type=jnp.float32) + b_in
    gate_sig = jax.nn.sigmoid(pre_act)
    grad_pre = (
        grad_hidden.astype(jnp.float32) * gate_sig * (1.0 + pre_act * (1.0 - gate_sig))
    ).astype(jnp.bfloat16)
    w_in_grad = lax.psum_scatter(
        lax.dot_general(
            top_input, grad_pre, (((0,), (0,)), ((), ())), preferred_element_type=jnp.float32
        ),
        ("hst", "chip"),
        scatter_dimension=0,
        tiled=True,
    )
    pooled = lax.dot_general(
        grad_pre, w_in, (((1,), (1,)), ((), ())), preferred_element_type=jnp.float32
    ).astype(jnp.bfloat16)
    selector = (slice_map[:, None] == lax.iota(jnp.int32, slices)[None, :]).astype(jnp.bfloat16)
    ordered = jnp.einsum(
        "bkc,sk->sbc",
        pooled.reshape(b_dev, slices, slw),
        selector,
        preferred_element_type=jnp.float32,
    ).astype(jnp.bfloat16)
    received = lax.all_to_all(ordered, "hst", split_axis=0, concat_axis=1, tiled=True)
    chip_index = lax.axis_index("chip")
    ids_all = (
        lookup_ids.reshape(s_here, slot_count, hosts, chips, b_dev)
        .transpose(0, 1, 3, 2, 4)
        .reshape(s_here, slot_count, hosts * chips * b_dev)
    )
    lens_all = (
        bag_len.reshape(s_here, hosts, chips, b_dev)
        .transpose(0, 2, 1, 3)
        .reshape(s_here, hosts * chips * b_dev)
    )
    row_base = chip_index * ROWS_DEV
    empty = jnp.zeros((s_here, ROWS_DEV, slw), jnp.float32)
    piece = lax.all_gather(received, "chip", axis=1, tiled=True)
    length = piece.shape[1]
    block = math.gcd(length, 2048)

    def add_block(step, acc):
        offset = step * block
        ids_block = lax.dynamic_slice_in_dim(ids_all[0], offset, block, 1)
        lens_block = lax.dynamic_slice_in_dim(lens_all[0], offset, block, 0)
        rows_block = lax.dynamic_slice_in_dim(piece[0], step * block, block, 0)
        counts = count_block(ids_block, lens_block, row_base, ROWS_DEV)
        return acc + jnp.dot(counts, rows_block, preferred_element_type=jnp.float32)

    outputs = [lax.fori_loop(0, length // block, add_block, empty[0])]
    table_grad = jnp.stack(outputs, axis=0)
    return (w_in_grad, table_grad)


def solution(mesh):
    in_specs = (
        P(("hst", "chip"), None),
        P(("hst", "chip"), None),
        P(),
        P(),
        P(),
        P("hst", None, None),
        P("hst", None),
    )
    out_specs = (P(("hst", "chip"), None), P("hst", "chip", None))
    return jax.shard_map(body, mesh=mesh, in_specs=in_specs, out_specs=out_specs, check_vma=False)
```

profile of v0, /device:TPU:1, one launch (start us, length us, event | category | flops | bytes accessed | tf_op | source)
XLA Modules:
  0.0 1364.6 jit_solution(10422284984876569110)
XLA Ops:
  8.0 0.0 copy-start
  8.0 0.0 copy-start.3
  8.0 0.0 all-gather.2.cloned.1.call-start
  8.1 1.0 copy-done
  9.0 0.0 copy-start.1
  9.0 4.8 convolution_add_fusion.1
  13.8 0.0 copy-done.3
  13.9 1.0 copy-done.1
  14.9 0.0 copy-start.6
  14.9 2.9 fusion.11
  17.8 0.1 copy.21
  17.9 0.0 copy-done.6
  17.9 0.3 convolution_convert_fusion.1
  18.3 0.1 copy.14
  18.4 17.8 %all_to_all.12 = bf16[16,128,128]{2,1,0:T(8,128)(2,1)} all-to-all(bf16[16,128,128]{2,1,0:T(8,128)(2,1)S(1)} %copy.14), channel_id=1, replica_groups=mesh['hst'=16,'chip'=16] {'hst'}, dimensions={0} | all-to-all | bytes 1048576 | tf_op jit(solution)/shard_map/all_to_all | solution.py:52
  36.2 0.0 all-gather.2.cloned.1.call-update
  36.2 0.0 reduce-scatter.4.cloned.1.call-start
  36.3 8.1 convolution_bitcast_fusion
  44.4 17.8 %copy.18 = f32[2048,2048]{1,0:T(8,128)} copy(f32[2048,2048]{0,1:T(8,128)} %convolution_bitcast_fusion) | data formatting | bytes 33554432
  62.3 0.0 copy-start.5
  62.3 0.0 reduce-scatter.4.cloned.1.call-update
  62.3 0.9 copy-done.5
  63.2 0.2 copy-done.4
  63.5 0.2 copy.15
  63.6 0.0 copy-start.2
  63.7 0.2 squeeze_reshape.16
  63.9 30.3 %all-gather.2.cloned.1.call-done = bf16[1,32768,128]{2,1,0:T(8,128)(2,1)} async-done(((bf16[1,2048,128]{2,1,0:T(8,128)(2,1)}), bf16[1,32768,128]{2,1,0:T(8,128)(2,1)}) %all-gather.2.cloned.1.call-update) | async-done | bytes 8388624 | tf_op jit(solution)/shard_map/all_gather | solution.py:66
  94.2 0.0 copy-done.2
  94.2 44.9 %while.15 = (s32[]{:T(128)}, f32[256,128]{1,0:T(8,128)S(1)}, s32[1,4,16,16,128]{4,3,2,1,0:T(8,128)}, s32[]{:T(128)}, s32[1,16,16,128]{3,2,1,0:T(8,128)S(1)}, /*i...) while((s32[]{:T(128)}, f32[256,128]{1,0:T(8,128)S(1)}, ...), condition=%wide.wide.region_2.0_spmd.clone, body=%wide.wide.region_1.0_spmd.clone.sunk | while | flops 142680336 | bytes 911621 | solution.py:78
  94.2 0.1 constant_dynamic-slice_fusion.3
  94.3 2.6 convolution_add_fusion.4
  97.0 0.1 constant_dynamic-slice_fusion.3
  97.2 2.6 convolution_add_fusion.4
  99.8 0.1 constant_dynamic-slice_fusion.3
  100.0 2.6 convolution_add_fusion.4
  102.6 0.1 constant_dynamic-slice_fusion.3
  102.8 2.6 convolution_add_fusion.4
  105.4 0.1 constant_dynamic-slice_fusion.3
  105.6 2.6 convolution_add_fusion.4
  108.2 0.1 constant_dynamic-slice_fusion.3
  108.4 2.6 convolution_add_fusion.4
  111.1 0.1 constant_dynamic-slice_fusion.3
  111.2 2.6 convolution_add_fusion.4
  113.9 0.1 constant_dynamic-slice_fusion.3
  114.0 2.6 convolution_add_fusion.4
  116.7 0.1 constant_dynamic-slice_fusion.3
  116.8 2.6 convolution_add_fusion.4
  119.5 0.1 constant_dynamic-slice_fusion.3
  119.6 2.6 convolution_add_fusion.4
  122.3 0.1 constant_dynamic-slice_fusion.3
  122.4 2.6 convolution_add_fusion.4
  125.1 0.1 constant_dynamic-slice_fusion.3
  125.2 2.6 convolution_add_fusion.4
  127.9 0.1 constant_dynamic-slice_fusion.3
  128.0 2.6 convolution_add_fusion.4
  130.7 0.1 constant_dynamic-slice_fusion.3
  130.8 2.6 convolution_add_fusion.4
  133.5 0.1 constant_dynamic-slice_fusion.3
  133.6 2.6 convolution_add_fusion.4
  136.3 0.1 constant_dynamic-slice_fusion.3
  136.4 2.6 convolution_add_fusion.4
  139.1 0.0 copy-start.7
  139.1 1218.1 %reduce-scatter.4.cloned.1.call-done = f32[8,2048]{1,0:T(8,128)} async-done(((f32[2048,2048]{1,0:T(8,128)}), f32[8,2048]{1,0:T(8,128)}) %reduce-scatter.4.cloned.1.call-update) | async-done | bytes 65552
  1357.1 0.0 copy-done.7
  (36 shorter events, 0.4 us)
Async XLA Ops:
  8.0 1.0 copy-start
  8.0 5.8 copy-start.3
  8.0 86.2 %all-gather.2.cloned.1.call-start = ((), (), s32[]{:S(2)}) async-start(), calls=%async_computation.2 | async-start | bytes 8912896 | tf_op jit(solution)/shard_map/all_gather | solution.py:66
  9.0 5.8 copy-start.1
  14.9 3.1 copy-start.6
  36.2 1320.9 %reduce-scatter.4.cloned.1.call-start = ((), (), s32[]{:S(2)}) async-start(), calls=%async_computation.3 | async-start | bytes 16842752
  62.3 0.9 copy-start.5
  62.3 1.2 copy-start.4
  63.6 30.5 %copy-start.2 = (s32[1,4,16,16,128]{4,3,2,1,0:T(8,128)}, s32[1,4,16,16,128]{4,3,2,1,0:T(8,128)S(1)}, u32[]{:S(2)}) copy-start(s32[1,4,16,16,128]{4,3,2,1,0:T(8,128)S(1)} %copy.15) | copy-start | bytes 1572868
  139.1 1218.1 %copy-start.7 = (f32[256,128]{1,0:T(8,128)}, f32[256,128]{1,0:T(8,128)S(1)}, u32[]{:S(2)}) copy-start(f32[256,128]{1,0:T(8,128)S(1)} %get-tuple-element.111) | copy-start | bytes 393220
Sparse Core Ops, SparseCore 0:
  36.4 57.7 all-gather.1
Sparse Core Ops, SparseCore 1:
  62.4 1294.7 reduce-scatter.3
where the time goes:
time: 1370 us; the launch traced here: 1360 us
  waiting for transfers between devices  1250 us (91%)
  matrix products  57.9 us (4%)
  local copies, waits for them, and re-layouts  23.7 us (2%)
  blocking collectives  17.8 us (1%)
  between operations  15.6 us (1%)
    unnamed x3, waiting for transfers between devices  1220 us
    dot_general x16, matrix products, add_block(): return acc + jnp.dot(counts, rows_block, preferred_element_type=jnp.float32)  41.7 us
    all_gather x1, waiting for transfers between devices, body(): piece = lax.all_gather(received, 'chip', axis=1, tiled=True)  30.3 us
  transfers between devices with their start and end apart: 2, of which 2 were waited for; matrix products, arithmetic and copies ran while one was open for 5% of the time, Pallas kernels for 0%

commit v1 on v0

v1 whole, which is shorter than its diff:
```python
import functools

import jax
import jax.numpy as jnp
from jax import lax
from jax.experimental import pallas as pl
from jax.experimental.pallas import tpu as pltpu
from jax.sharding import PartitionSpec as P

NX, NY, NZ, NC = 4, 4, 8, 2
AXES = ("hst", "chip")
ROWS_DEV = 256
LOCAL_ROWS = NZ * ROWS_DEV


def device_index(x, y, z, c):
    return ((x * NY + y) * NZ + z) * NC + c


def shift_perm(dx=0, dy=0, dc=0):
    pairs = []
    for x in range(NX):
        for y in range(NY):
            for z in range(NZ):
                for c in range(NC):
                    pairs.append(
                        (
                            device_index(x, y, z, c),
                            device_index((x + dx) % NX, (y + dy) % NY, z, (c + dc) % NC),
                        )
                    )
    return pairs


def send(value, **shift):
    return lax.ppermute(value, AXES, shift_perm(**shift))


def table_kernel(chunk, rb, ids_ref, x_ref, o_ref):
    samples = x_ref.shape[0]
    one = jnp.ones((), jnp.bfloat16)
    zero = jnp.zeros((), jnp.bfloat16)
    target = lax.broadcasted_iota(jnp.int32, (rb, chunk), 0).astype(jnp.int16)

    def do_block(k, carry):
        base = k * rb
        acc = jnp.zeros((rb, x_ref.shape[1]), jnp.float32)
        for s in range(samples // chunk):
            ids = (ids_ref[:, s * chunk : (s + 1) * chunk] - base).astype(jnp.int16)
            counts = None
            for j in range(ids_ref.shape[0]):
                hit = jnp.where(jnp.broadcast_to(ids[j : j + 1], (rb, chunk)) == target, one, zero)
                counts = hit if counts is None else counts + hit
            acc = acc + jnp.dot(
                counts, x_ref[s * chunk : (s + 1) * chunk, :], preferred_element_type=jnp.float32
            )
        o_ref[pl.ds(pl.multiple_of(base, rb), rb), :] = acc
        return carry

    lax.fori_loop(0, o_ref.shape[0] // rb, do_block, 0)


def table_partial(ids, x):
    return pl.pallas_call(
        functools.partial(table_kernel, 256, 512),
        out_shape=jax.ShapeDtypeStruct((LOCAL_ROWS, x.shape[1]), jnp.float32),
        in_specs=[pl.BlockSpec(memory_space=pltpu.VMEM)] * 2,
        out_specs=pl.BlockSpec(memory_space=pltpu.VMEM),
        compiler_params=pltpu.CompilerParams(vmem_limit_bytes=32 << 20),
        name="table_partial",
    )(ids, x)


def f32(v):
    return v.astype(jnp.float32)


def body(top_input, grad_hidden, w_in, b_in, slice_map, lookup_ids, bag_len):
    hst = lax.axis_index("hst")
    chip = lax.axis_index("chip")
    x, y = hst // NY, hst % NY
    z, core = chip // NC, chip % NC
    b_dev, width = top_input.shape
    hidden = grad_hidden.shape[1]
    slices = slice_map.shape[0]
    slw = width // slices
    half = hidden // NC
    quart = half // 2

    top_other = send(top_input, dc=1)
    pre_act = jnp.dot(top_input, w_in, preferred_element_type=jnp.float32) + b_in
    gate_sig = jax.nn.sigmoid(pre_act)
    grad_pre = (f32(grad_hidden) * gate_sig * (1.0 + pre_act * (1.0 - gate_sig))).astype(jnp.bfloat16)
    grad_mine = lax.dynamic_slice_in_dim(grad_pre, core * half, half, 1)
    grad_other = send(lax.dynamic_slice_in_dim(grad_pre, (1 - core) * half, half, 1), dc=1)
    pooled = lax.dot_general(
        grad_pre, w_in, (((1,), (1,)), ((), ())), preferred_element_type=jnp.float32
    ).astype(jnp.bfloat16)

    top_chip = jnp.concatenate([top_input, top_other], axis=0)
    grad_chip = jnp.concatenate([grad_mine, grad_other], axis=0)
    part = lax.dot_general(
        top_chip, grad_chip, (((0,), (0,)), ((), ())), preferred_element_type=jnp.float32
    ).astype(jnp.bfloat16)
    part = part.reshape(NX, NY, width // (NX * NY), half)
    part_a, part_b = part[..., :quart], part[..., quart:]

    def take(v, axis, index):
        return lax.dynamic_index_in_dim(v, index, axis, keepdims=False)

    got_a = [send(take(part_a, 0, (x + d) % NX), dx=d) for d in (1, 3, 2)]
    got_b = [send(take(part_b, 1, (y + d) % NY), dy=d) for d in (1, 3, 2)]

    selector = (slice_map[:, None] == lax.iota(jnp.int32, slices)[None, :]).astype(jnp.bfloat16)
    ordered = jnp.einsum(
        "bkc,sk->sbc",
        pooled.reshape(b_dev, slices, slw),
        selector,
        preferred_element_type=jnp.float32,
    ).astype(jnp.bfloat16)
    received = lax.all_to_all(ordered, "hst", split_axis=0, concat_axis=1, tiled=True)[0]
    rec_other = send(received, dc=1)

    slots = lookup_ids.shape[1]
    ids = lookup_ids[0].reshape(slots, NX * NY, NZ, NC, b_dev)
    lens = bag_len[0].reshape(NX * NY, NZ, NC, b_dev)
    ids = lax.dynamic_index_in_dim(ids, z, 2, keepdims=False)
    lens = lax.dynamic_index_in_dim(lens, z, 1, keepdims=False)
    live = lax.iota(jnp.int32, slots)[:, None, None, None] < lens[None]
    here = (ids // ROWS_DEV) % NC == core
    local = (ids // (NC * ROWS_DEV)) * ROWS_DEV + ids % ROWS_DEV
    local = jnp.where(live & here, local, -1)
    mine = lax.dynamic_index_in_dim(local, core, 2, keepdims=False).reshape(slots, -1)
    theirs = lax.dynamic_index_in_dim(local, 1 - core, 2, keepdims=False).reshape(slots, -1)
    local = jnp.concatenate([mine, theirs], axis=1)
    table = table_partial(local, jnp.concatenate([received, rec_other], axis=0))
    groups = [[zz * NC + c for zz in range(NZ)] for c in range(NC)]
    table = lax.psum_scatter(
        table, "chip", scatter_dimension=0, axis_index_groups=groups, tiled=True
    )

    sum_a = (f32(take(part_a, 0, x)) + f32(got_a[0]) + f32(got_a[1]) + f32(got_a[2])).astype(jnp.bfloat16)
    sum_b = (f32(take(part_b, 1, y)) + f32(got_b[0]) + f32(got_b[1]) + f32(got_b[2])).astype(jnp.bfloat16)
    got_a = [send(take(sum_a, 0, (y + d) % NY), dy=d) for d in (1, 3, 2)]
    got_b = [send(take(sum_b, 0, (x + d) % NX), dx=d) for d in (1, 3, 2)]
    fin_a = f32(take(sum_a, 0, y)) + f32(got_a[0]) + f32(got_a[1]) + f32(got_a[2])
    fin_b = f32(take(sum_b, 0, x)) + f32(got_b[0]) + f32(got_b[1]) + f32(got_b[2])
    fin = jnp.concatenate([fin_a, fin_b], axis=1).astype(jnp.bfloat16)
    rows_out = fin.shape[0] // (NZ * NC)
    swapped = lax.all_to_all(
        fin.reshape(NZ * NC, rows_out, half), "chip", split_axis=0, concat_axis=0, tiled=True
    )
    total = f32(swapped).reshape(NZ, NC, rows_out, half).sum(0)
    w_in_grad = total.transpose(1, 0, 2).reshape(rows_out, hidden)
    return (w_in_grad, table[None])


def solution(mesh):
    in_specs = (
        P(("hst", "chip"), None),
        P(("hst", "chip"), None),
        P(),
        P(),
        P(),
        P("hst", None, None),
        P("hst", None),
    )
    out_specs = (P(("hst", "chip"), None), P("hst", "chip", None))
    return jax.shard_map(body, mesh=mesh, in_specs=in_specs, out_specs=out_specs, check_vma=False)
```

time: 1370 us -> 125 us (0.09)
  waiting for transfers between devices: 1250 us -> 37.1 us
  matrix products: 57.9 us -> 11 us
  starting transfers between devices: 0.08 us -> 19 us
  local copies, waits for them, and re-layouts: 23.7 us -> 6.21 us
    unnamed x3 -> x1, waiting for transfers between devices: 1220 us -> 0.02 us
    dot_general x17 -> x1, matrix products: 49.8 us -> 2.33 us  [body(): lax.dot_general(top_chip, grad_chip, (((0,), (0,)), ((), ())), preferred_...]
    all_gather x1 -> x0, waiting for transfers between devices: 30.3 us -> none  [body(): piece = lax.all_gather(received, 'chip', axis=1, tiled=True)]
    ppermute x0 -> x15, waiting for transfers between devices: none -> 28 us  [send(): return lax.ppermute(value, AXES, shift_perm(**shift))]
    unnamed x21 -> x20, local copies, waits for them, and re-layouts: 21.3 us -> 1.88 us
    ppermute x0 -> x15, starting transfers between devices: none -> 13.9 us  [send(): return lax.ppermute(value, AXES, shift_perm(**shift))]
  transfers between devices with their start and end apart: 2 -> 17, of which waited for: 2 -> 7; matrix products, arithmetic and copies ran while one was open for 5% -> 16% of each run, Pallas kernels for 0% -> 6%
where the time goes in v1:
time: 125 us; the launch traced here: 124 us
  waiting for transfers between devices  37.1 us (30%)
  blocking collectives  23.9 us (19%)
  starting transfers between devices  19 us (15%)
  between operations  14.5 us (12%)
  matrix products  11 us (9%)
  Pallas kernels  7.82 us (6%)
  local copies, waits for them, and re-layouts  6.21 us (5%)
  other arithmetic  4.3 us (3%)
    ppermute x15, waiting for transfers between devices, send(): return lax.ppermute(value, AXES, shift_perm(**shift))  28 us
    all_to_all x1, blocking collectives, body(): lax.all_to_all(fin.reshape(NZ * NC, rows_out, half), 'chip', split_axis=0...  23.9 us
    ppermute x15, starting transfers between devices, send(): return lax.ppermute(value, AXES, shift_perm(**shift))  13.9 us
    all_to_all x1, waiting for transfers between devices, body(): lax.all_to_all(ordered, 'hst', split_axis=0, concat_axis=1, tiled=True)[0]  9.09 us
    pallas_call x1, Pallas kernels, table_partial(): pl.pallas_call(functools.partial(table_kernel, 256, 512), out_shape=jax.S...  7.82 us
    dot_general x1, matrix products, body(): jnp.dot(top_input, w_in, preferred_element_type=jnp.float32) + b_in  5.37 us
    all_to_all x1, starting transfers between devices, body(): lax.all_to_all(ordered, 'hst', split_axis=0, concat_axis=1, tiled=True)[0]  5.02 us
    dot_general x1, matrix products, body(): lax.dot_general(grad_pre, w_in, (((1,), (1,)), ((), ())), preferred_eleme...  2.93 us
  transfers between devices with their start and end apart: 17, of which 7 were waited for; matrix products, arithmetic and copies ran while one was open for 16% of the time, Pallas kernels for 6%

profile of v1, /device:TPU:1, one launch (start us, length us, event | category | flops | bytes accessed | tf_op | source)
XLA Modules:
  0.0 123.8 jit_solution(14683558704536354871)
XLA Ops:
  7.2 0.0 copy-start
  7.2 3.3 %collective-permute-start = (bf16[128,2048]{1,0:T(8,128)(2,1)}, bf16[128,2048]{1,0:T(8,128)(2,1)}, u32[]{:S(2)}, u32[]{:S(2)}) collective-permute-start(bf16[128,2048]{1,0:T(8,128)(2,1)} %param.7), channel_id=1, source_target_pairs={{0,1},{1,0},{2,3},{3,2},{4,5},{5,4},{6,7},{7,6},{8,9},{9,8},{10,11... | collective-permute-start | bytes 1572872 | tf_op jit(solution)/shard_map/ppermute | solution.py:36
  10.5 5.4 %multiply_convert_fusion = (bf16[128,2048]{1,0:T(8,128)(2,1)S(1)}, f32[128,2048]{1,0:T(8,128)S(1)}) fusion(bf16[128,2048]{1,0:T(8,128)(2,1)} %param.8, f32[2048]{0:T(1024)} %param.10, bf16[128,2048]{1,0:T(8,128)(2,1)} %param.7, bf16[2048,2048]{1,0:T(8,128)(2,1)} %param.9), kind=kOutput, calls=%fused_computation.17 | convolution fusion | flops 1076625408 | bytes 11018240 | tf_op jit(solution)/shard_map/dot_general | solution.py:91
  15.9 0.1 collective-permute-start.1
  16.1 0.5 copy-done.6
  16.6 0.0 copy-done.7
  16.6 2.9 %fusion = bf16[16,8,16,128]{3,1,2,0:T(8,128)(2,1)S(1)} fusion(bf16[2048,2048]{1,0:T(8,128)(2,1)S(1)} %copy-done.6, f32[128,2048]{1,0:T(8,128)S(1)} %get-tuple-element.21, bf16[128,2048]{1,0:T(8,128)(2,1)S(1)} %copy-done.7), kind=kOutput, calls=%fused_computation.4 | convolution fusion | flops 1076625408 | bytes 10485760 | tf_op jit(solution)/shard_map/dot_general | solution.py:96
  19.6 0.0 copy-start.2
  19.6 0.1 copy.21
  19.7 0.0 copy-done.5
  19.7 0.3 convolution_convert_fusion.2
  20.1 0.0 copy-start.8
  20.1 1.0 copy.18
  21.0 5.0 %all-to-all-start.1 = ((bf16[16,128,128]{2,1,0:T(8,128)(2,1)}), bf16[16,128,128]{2,1,0:T(8,128)(2,1)S(1)}, u32[]{:S(2)}, u32[]{:S(2)}) async-start(bf16[16,128,128]{2,1,0:T(8,128)(2,1)} %copy.18), calls=%async_computation.1 | async-start | bytes 1048576 | tf_op jit(solution)/shard_map/all_to_all | solution.py:121
  26.1 0.0 reduce-scatter.2.cloned.1.call-start
  26.1 0.0 copy-done
  26.2 0.5 reshape_squeeze.7
  26.8 0.1 fusion.28
  27.1 9.1 %all-to-all-done.1 = bf16[16,128,128]{2,1,0:T(8,128)(2,1)S(1)} async-done(((bf16[16,128,128]{2,1,0:T(8,128)(2,1)}), bf16[16,128,128]{2,1,0:T(8,128)(2,1)S(1)}, u32[]{:S(2)}, u32[]{:S(2)}) %all-to-all-start.1) | async-done | bytes 524320 | tf_op jit(solution)/shard_map/all_to_all | solution.py:121
  36.2 2.3 %collective-permute-start.14 = (bf16[2048,128]{1,0:T(8,128)(2,1)S(1)}, bf16[2048,128]{1,0:T(8,128)(2,1)S(1)}, u32[]{:S(2)}, u32[]{:S(2)}) collective-permute-start(bf16[2048,128]{1,0:T(8,128)(2,1)S(1)} %bitcast.95), channel_id=1, source_target_pairs={{0,1},{1,0},{2,3},{3,2},{4,5},{5,4},{6,7},{7,6},{8,9},{9,8},{10,11... | collective-permute-start | bytes 1572872 | tf_op jit(solution)/shard_map/ppermute | solution.py:36
  38.5 0.0 collective-permute-done.1
  38.5 0.0 collective-permute-done
  38.5 2.3 %convolution_convert_fusion = bf16[2048,1024]{1,0:T(8,128)(2,1)S(1)} fusion(bf16[128,2048]{1,0:T(8,128)(2,1)} %collective-permute-done, bf16[128,2048]{1,0:T(8,128)(2,1)S(1)} %copy-done.8, bf16[128,1024]{1,0:T(8,128)(2,1)S(1)} %collective-permute-done.1, bf16[128,1024]{1,0:T(8,128)(2,1)S(1)} %get-tuple-element.16), kind=kOutput, calls=%fused_computation | convolution fusion | flops 1078984704 | bytes 5767168 | tf_op jit(solution)/shard_map/dot_general | solution.py:102
  40.9 0.3 fusion.40
  41.2 1.2 dynamic-slice_bitcast_fusion.5
  42.4 0.0 collective-permute-start.2
  42.4 0.5 copy-done.1
  42.9 1.5 %collective-permute-start.4 = (bf16[4,128,512]{2,1,0:T(8,128)(2,1)}, bf16[4,128,512]{2,1,0:T(8,128)(2,1)}, u32[]{:S(2)}, u32[]{:S(2)}) collective-permute-start(bf16[4,128,512]{2,1,0:T(8,128)(2,1)} %get-tuple-element.5), channel_id=1, source_target_pairs={{0,128},{1,129},{2,130},{3,131},{4,132},{5,133},{6,134},{7,135},{8... | collective-permute-start | bytes 1572872 | tf_op jit(solution)/shard_map/ppermute | solution.py:36
  44.4 1.1 collective-permute-start.3
  45.5 1.1 dynamic-slice_bitcast_fusion.2
  46.6 0.2 collective-permute-start.8
  46.8 0.0 collective-permute-done.14
  46.8 1.7 %collective-permute-start.10 = (bf16[4,128,512]{2,1,0:T(8,128)(2,1)}, bf16[4,128,512]{2,1,0:T(8,128)(2,1)}, u32[]{:S(2)}, u32[]{:S(2)}) collective-permute-start(bf16[4,128,512]{2,1,0:T(8,128)(2,1)} %get-tuple-element.8), channel_id=1, source_target_pairs={{0,32},{1,33},{2,34},{3,35},{4,36},{5,37},{6,38},{7,39},{8,40},{9,... | collective-permute-start | bytes 1572872 | tf_op jit(solution)/shard_map/ppermute | solution.py:36
  48.6 19.9 %collective-permute-done.2 = bf16[4,128,512]{2,1,0:T(8,128)(2,1)S(1)} collective-permute-done((bf16[4,128,512]{2,1,0:T(8,128)(2,1)S(1)}, bf16[4,128,512]{2,1,0:T(8,128)(2,1)S(1)}, u32[]{:S(2)}, u32[]{:S(2)}) %collective-permute-start.2) | collective-permute-done | bytes 524320 | tf_op jit(solution)/shard_map/ppermute | solution.py:36
  68.5 0.2 collective-permute-start.9
  68.7 0.7 copy-done.3
  69.3 0.1 pad_maximum_fusion.x_ref
  69.4 0.0 copy-start.4
  69.4 7.8 %table_partial.1 = f32[2048,128]{1,0:T(8,128)} custom-call(s32[4,4096]{1,0:T(4,128)S(1)} %pad_add_fusion.ids_ref, bf16[4096,128]{1,0:T(8,128)(2,1)S(1)} %pad_maximum_fusion.x_ref), custom_call_target="tpu_custom_call" | custom-call | tf_op jit(solution)/shard_map/table_partial/pallas_call | solution.py:64
  77.2 0.0 reduce-scatter.2.cloned.1.call-update
  77.3 0.0 collective-permute-done.4
  77.3 0.0 collective-permute-done.3
  77.3 0.0 copy-done.4
  77.3 1.6 %fusion.9 = bf16[4,128,512]{2,1,0:T(8,128)(2,1)S(1)} fusion(bf16[4,128,512]{2,1,0:T(8,128)(2,1)} %collective-permute-done.4, bf16[4,128,512]{2,1,0:T(8,128)(2,1)} %collective-permute-done.3, bf16[4,128,512]{2,1,0:T(8,128)(2,1)S(1)} %copy-done.4, bf16[4,4,128,512]{3,2,1,0:T(8,128)(2,1)} %copy-done.1, s32[]{:T(128)S(6)} %select_n.134), kind=kLoop, calls=%fused_computation.16 | loop fusion | flops 2097152 | bytes 2621444 | tf_op jit(solution)/shard_map/convert_element_type | solution.py:142
  79.0 0.7 collective-permute-start.5
  79.7 0.7 collective-permute-start.7
  80.4 0.0 collective-permute-done.8
  80.4 1.8 %collective-permute-start.6 = (bf16[128,512]{1,0:T(8,128)(2,1)S(1)}, bf16[128,512]{1,0:T(8,128)(2,1)S(1)}, u32[]{:S(2)}, u32[]{:S(2)}) collective-permute-start(bf16[128,512]{1,0:T(8,128)(2,1)S(1)} %get-tuple-element.12), channel_id=1, source_target_pairs={{0,48},{1,49},{2,50},{3,51},{4,52},{5,53},{6,54},{7,55},{8,56},{9,... | collective-permute-start | bytes 393224 | tf_op jit(solution)/shard_map/ppermute | solution.py:36
  82.3 0.0 collective-permute-done.10
  82.3 0.0 collective-permute-done.9
  82.3 1.6 %fusion.6 = bf16[4,128,512]{2,1,0:T(8,128)(2,1)S(1)} fusion(bf16[4,128,512]{2,1,0:T(8,128)(2,1)} %collective-permute-done.10, bf16[4,128,512]{2,1,0:T(8,128)(2,1)} %collective-permute-done.9, bf16[4,128,512]{2,1,0:T(8,128)(2,1)} %collective-permute-done.8, bf16[4,4,128,512]{3,2,1,0:T(8,128)(2,1)S(1)} %get-tuple-element.3, s32[]{:T(128)S(6)} %select_n.142), kind=kLoop, calls=%fused_computation.12 | loop fusion | flops 2097152 | bytes 2621444 | tf_op jit(solution)/shard_map/convert_element_type | solution.py:143
  84.0 0.1 collective-permute-start.11
  84.0 0.1 collective-permute-start.13
  84.1 3.4 %collective-permute-done.5 = bf16[128,512]{1,0:T(8,128)(2,1)S(1)} collective-permute-done((bf16[128,512]{1,0:T(8,128)(2,1)S(1)}, bf16[128,512]{1,0:T(8,128)(2,1)S(1)}, u32[]{:S(2)}, u32[]{:S(2)}) %collective-permute-start.5) | collective-permute-done | bytes 131104 | tf_op jit(solution)/shard_map/ppermute | solution.py:36
  87.6 0.0 collective-permute-start.12
  87.6 0.0 collective-permute-done.7
  87.6 0.1 collective-permute-done.6
  87.7 0.1 fusion.21
  87.8 2.3 %collective-permute-done.11 = bf16[128,512]{1,0:T(8,128)(2,1)S(1)} collective-permute-done((bf16[128,512]{1,0:T(8,128)(2,1)S(1)}, bf16[128,512]{1,0:T(8,128)(2,1)S(1)}, u32[]{:S(2)}, u32[]{:S(2)}) %collective-permute-start.11) | collective-permute-done | bytes 131104 | tf_op jit(solution)/shard_map/ppermute | solution.py:36
  90.1 1.0 collective-permute-done.13
  91.1 1.2 collective-permute-done.12
  92.3 0.1 fusion.22
  92.4 23.9 %all_to_all.14 = bf16[16,8,1024]{2,1,0:T(8,128)(2,1)S(1)} all-to-all(bf16[16,8,1024]{2,1,0:T(8,128)(2,1)S(1)} %pad_maximum_fusion.1), channel_id=1, replica_groups=mesh['hst'=16,'chip'=16] {'chip'}, dimensions={0} | all-to-all | bytes 524288 | tf_op jit(solution)/shard_map/all_to_all | solution.py:150
  116.3 0.7 convert_reduce_fusion
  (18 shorter events, 0.2 us)
Async XLA Ops:
  7.2 19.0 %copy-start = (s32[1,32768]{1,0:T(1,128)S(1)}, s32[1,32768]{1,0:T(1,128)}, u32[]{:S(2)}) copy-start(s32[1,32768]{1,0:T(1,128)} %param.13) | copy-start | bytes 393220
  7.2 31.3 %collective-permute-start = (bf16[128,2048]{1,0:T(8,128)(2,1)}, bf16[128,2048]{1,0:T(8,128)(2,1)}, u32[]{:S(2)}, u32[]{:S(2)}) collective-permute-start(bf16[128,2048]{1,0:T(8,128)(2,1)} %param.7), channel_id=1, source_target_pairs={{0,1},{1,0},{2,3},{3,2},{4,5},{5,4},{6,7},{7,6},{8,9},{9,8},{10,11... | collective-permute-start | bytes 1572872 | tf_op jit(solution)/shard_map/ppermute | solution.py:36
  10.5 6.1 %copy-start.6 = (bf16[2048,2048]{1,0:T(8,128)(2,1)S(1)}, bf16[2048,2048]{1,0:T(8,128)(2,1)}, u32[]{:S(2)}) copy-start(bf16[2048,2048]{1,0:T(8,128)(2,1)} %param.9) | copy-start | bytes 25165828
  10.5 6.1 %copy-start.7 = (bf16[128,2048]{1,0:T(8,128)(2,1)S(1)}, bf16[128,2048]{1,0:T(8,128)(2,1)}, u32[]{:S(2)}) copy-start(bf16[128,2048]{1,0:T(8,128)(2,1)} %param.8) | copy-start | bytes 1572868
  15.9 22.6 %collective-permute-start.1 = (bf16[128,1024]{1,0:T(8,128)(2,1)S(1)}, bf16[128,1024]{1,0:T(8,128)(2,1)S(1)}, u32[]{:S(2)}, u32[]{:S(2)}) collective-permute-start(bf16[128,1024]{1,0:T(8,128)(2,1)S(1)} %get-tuple-element.17), channel_id=1, source_target_pairs={{0,1},{1,0},{2,3},{3,2},{4,5},{5,4},{6,7},{7,6},{8,9},{9,8},{10,11... | collective-permute-start | bytes 786440 | tf_op jit(solution)/shard_map/ppermute | solution.py:36
  16.6 3.1 %copy-start.5 = (s32[16]{0:T(128)S(1)}, s32[16]{0:T(128)}, u32[]{:S(2)}) copy-start(s32[16]{0:T(128)} %param.11) | copy-start | bytes 196
  19.6 6.6 %copy-start.2 = (s32[1,4,32768]{2,1,0:T(4,128)S(1)}, s32[1,4,32768]{2,1,0:T(4,128)}, u32[]{:S(2)}) copy-start(s32[1,4,32768]{2,1,0:T(4,128)} %param.12) | copy-start | bytes 1572868
  20.1 18.4 %copy-start.8 = (bf16[128,2048]{1,0:T(8,128)(2,1)S(1)}, bf16[128,2048]{1,0:T(8,128)(2,1)}, u32[]{:S(2)}) copy-start(bf16[128,2048]{1,0:T(8,128)(2,1)} %param.7) | copy-start | bytes 1572868
  21.0 15.2 %all-to-all-start.1 = ((bf16[16,128,128]{2,1,0:T(8,128)(2,1)}), bf16[16,128,128]{2,1,0:T(8,128)(2,1)S(1)}, u32[]{:S(2)}, u32[]{:S(2)}) async-start(bf16[16,128,128]{2,1,0:T(8,128)(2,1)} %copy.18), calls=%async_computation.1 | async-start | bytes 1048576 | tf_op jit(solution)/shard_map/all_to_all | solution.py:121
  26.1 90.9 %reduce-scatter.2.cloned.1.call-start = ((), (), s32[]{:S(2)}) async-start(), calls=%async_computation.3 | async-start | bytes 1179648 | tf_op jit(solution)/shard_map/reduce_scatter | solution.py:138
  36.2 10.6 %collective-permute-start.14 = (bf16[2048,128]{1,0:T(8,128)(2,1)S(1)}, bf16[2048,128]{1,0:T(8,128)(2,1)S(1)}, u32[]{:S(2)}, u32[]{:S(2)}) collective-permute-start(bf16[2048,128]{1,0:T(8,128)(2,1)S(1)} %bitcast.95), channel_id=1, source_target_pairs={{0,1},{1,0},{2,3},{3,2},{4,5},{5,4},{6,7},{7,6},{8,9},{9,8},{10,11... | collective-permute-start | bytes 1572872 | tf_op jit(solution)/shard_map/ppermute | solution.py:36
  41.2 1.7 %copy-start.1 = (bf16[4,4,128,512]{3,2,1,0:T(8,128)(2,1)}, bf16[4,4,128,512]{3,2,1,0:T(8,128)(2,1)S(1)}, u32[]{:S(2)}) copy-start(bf16[4,4,128,512]{3,2,1,0:T(8,128)(2,1)S(1)} %get-tuple-element.2) | copy-start | bytes 6291460
  42.4 26.1 %collective-permute-start.2 = (bf16[4,128,512]{2,1,0:T(8,128)(2,1)S(1)}, bf16[4,128,512]{2,1,0:T(8,128)(2,1)S(1)}, u32[]{:S(2)}, u32[]{:S(2)}) collective-permute-start(bf16[4,128,512]{2,1,0:T(8,128)(2,1)S(1)} %get-tuple-element.4), channel_id=1, source_target_pairs={{0,64},{1,65},{2,66},{3,67},{4,68},{5,69},{6,70},{7,71},{8,72},{9,... | collective-permute-start | bytes 1572872 | tf_op jit(solution)/shard_map/ppermute | solution.py:36
  42.9 34.4 %collective-permute-start.4 = (bf16[4,128,512]{2,1,0:T(8,128)(2,1)}, bf16[4,128,512]{2,1,0:T(8,128)(2,1)}, u32[]{:S(2)}, u32[]{:S(2)}) collective-permute-start(bf16[4,128,512]{2,1,0:T(8,128)(2,1)} %get-tuple-element.5), channel_id=1, source_target_pairs={{0,128},{1,129},{2,130},{3,131},{4,132},{5,133},{6,134},{7,135},{8... | collective-permute-start | bytes 1572872 | tf_op jit(solution)/shard_map/ppermute | solution.py:36
  44.4 32.9 %collective-permute-start.3 = (bf16[4,128,512]{2,1,0:T(8,128)(2,1)}, bf16[4,128,512]{2,1,0:T(8,128)(2,1)}, u32[]{:S(2)}, u32[]{:S(2)}) collective-permute-start(bf16[4,128,512]{2,1,0:T(8,128)(2,1)} %get-tuple-element.6), channel_id=1, source_target_pairs={{0,192},{1,193},{2,194},{3,195},{4,196},{5,197},{6,198},{7,199},{8... | collective-permute-start | bytes 1572872 | tf_op jit(solution)/shard_map/ppermute | solution.py:36
  46.6 33.8 %collective-permute-start.8 = (bf16[4,128,512]{2,1,0:T(8,128)(2,1)}, bf16[4,128,512]{2,1,0:T(8,128)(2,1)}, u32[]{:S(2)}, u32[]{:S(2)}) collective-permute-start(bf16[4,128,512]{2,1,0:T(8,128)(2,1)} %get-tuple-element.7), channel_id=1, source_target_pairs={{0,16},{1,17},{2,18},{3,19},{4,20},{5,21},{6,22},{7,23},{8,24},{9,... | collective-permute-start | bytes 1572872 | tf_op jit(solution)/shard_map/ppermute | solution.py:36
  46.8 35.4 %collective-permute-start.10 = (bf16[4,128,512]{2,1,0:T(8,128)(2,1)}, bf16[4,128,512]{2,1,0:T(8,128)(2,1)}, u32[]{:S(2)}, u32[]{:S(2)}) collective-permute-start(bf16[4,128,512]{2,1,0:T(8,128)(2,1)} %get-tuple-element.8), channel_id=1, source_target_pairs={{0,32},{1,33},{2,34},{3,35},{4,36},{5,37},{6,38},{7,39},{8,40},{9,... | collective-permute-start | bytes 1572872 | tf_op jit(solution)/shard_map/ppermute | solution.py:36
  68.5 0.8 copy-start.3
  68.5 13.8 %collective-permute-start.9 = (bf16[4,128,512]{2,1,0:T(8,128)(2,1)S(1)}, bf16[4,128,512]{2,1,0:T(8,128)(2,1)}, u32[]{:S(2)}, u32[]{:S(2)}) collective-permute-start(bf16[4,128,512]{2,1,0:T(8,128)(2,1)S(1)} %get-tuple-element.9), channel_id=1, source_target_pairs={{0,48},{1,49},{2,50},{3,51},{4,52},{5,53},{6,54},{7,55},{8,56},{9,... | collective-permute-start | bytes 1572872 | tf_op jit(solution)/shard_map/ppermute | solution.py:36
  69.4 7.9 %copy-start.4 = (bf16[4,128,512]{2,1,0:T(8,128)(2,1)S(1)}, bf16[4,128,512]{2,1,0:T(8,128)(2,1)}, u32[]{:S(2)}) copy-start(bf16[4,128,512]{2,1,0:T(8,128)(2,1)} %copy-done.3) | copy-start | bytes 1572868
  79.0 8.6 %collective-permute-start.5 = (bf16[128,512]{1,0:T(8,128)(2,1)S(1)}, bf16[128,512]{1,0:T(8,128)(2,1)S(1)}, u32[]{:S(2)}, u32[]{:S(2)}) collective-permute-start(bf16[128,512]{1,0:T(8,128)(2,1)S(1)} %get-tuple-element.10), channel_id=1, source_target_pairs={{0,16},{1,17},{2,18},{3,19},{4,20},{5,21},{6,22},{7,23},{8,24},{9,... | collective-permute-start | bytes 393224 | tf_op jit(solution)/shard_map/ppermute | solution.py:36
  79.7 7.9 %collective-permute-start.7 = (bf16[128,512]{1,0:T(8,128)(2,1)S(1)}, bf16[128,512]{1,0:T(8,128)(2,1)S(1)}, u32[]{:S(2)}, u32[]{:S(2)}) collective-permute-start(bf16[128,512]{1,0:T(8,128)(2,1)S(1)} %get-tuple-element.11), channel_id=1, source_target_pairs={{0,32},{1,33},{2,34},{3,35},{4,36},{5,37},{6,38},{7,39},{8,40},{9,... | collective-permute-start | bytes 393224 | tf_op jit(solution)/shard_map/ppermute | solution.py:36
  80.4 7.3 %collective-permute-start.6 = (bf16[128,512]{1,0:T(8,128)(2,1)S(1)}, bf16[128,512]{1,0:T(8,128)(2,1)S(1)}, u32[]{:S(2)}, u32[]{:S(2)}) collective-permute-start(bf16[128,512]{1,0:T(8,128)(2,1)S(1)} %get-tuple-element.12), channel_id=1, source_target_pairs={{0,48},{1,49},{2,50},{3,51},{4,52},{5,53},{6,54},{7,55},{8,56},{9,... | collective-permute-start | bytes 393224 | tf_op jit(solution)/shard_map/ppermute | solution.py:36
  84.0 6.1 %collective-permute-start.11 = (bf16[128,512]{1,0:T(8,128)(2,1)S(1)}, bf16[128,512]{1,0:T(8,128)(2,1)S(1)}, u32[]{:S(2)}, u32[]{:S(2)}) collective-permute-start(bf16[128,512]{1,0:T(8,128)(2,1)S(1)} %get-tuple-element.13), channel_id=1, source_target_pairs={{0,64},{1,65},{2,66},{3,67},{4,68},{5,69},{6,70},{7,71},{8,72},{9,... | collective-permute-start | bytes 393224 | tf_op jit(solution)/shard_map/ppermute | solution.py:36
  84.0 7.0 %collective-permute-start.13 = (bf16[128,512]{1,0:T(8,128)(2,1)S(1)}, bf16[128,512]{1,0:T(8,128)(2,1)S(1)}, u32[]{:S(2)}, u32[]{:S(2)}) collective-permute-start(bf16[128,512]{1,0:T(8,128)(2,1)S(1)} %get-tuple-element.14), channel_id=1, source_target_pairs={{0,128},{1,129},{2,130},{3,131},{4,132},{5,133},{6,134},{7,135},{8... | collective-permute-start | bytes 393224 | tf_op jit(solution)/shard_map/ppermute | solution.py:36
  87.6 4.7 %collective-permute-start.12 = (bf16[128,512]{1,0:T(8,128)(2,1)S(1)}, bf16[128,512]{1,0:T(8,128)(2,1)S(1)}, u32[]{:S(2)}, u32[]{:S(2)}) collective-permute-start(bf16[128,512]{1,0:T(8,128)(2,1)S(1)} %get-tuple-element.15), channel_id=1, source_target_pairs={{0,192},{1,193},{2,194},{3,195},{4,196},{5,197},{6,198},{7,199},{8... | collective-permute-start | bytes 393224 | tf_op jit(solution)/shard_map/ppermute | solution.py:36
Sparse Core Ops, SparseCore 0:
  77.4 37.3 reduce-scatter.1

commit v2 on v1

v2 whole, which is shorter than its diff:
```python
import functools

import jax
import jax.numpy as jnp
from jax import lax
from jax.experimental import pallas as pl
from jax.experimental.pallas import tpu as pltpu
from jax.sharding import PartitionSpec as P

NX, NY, NZ, NC = 4, 4, 8, 2
AXES = ("hst", "chip")
ROWS_DEV = 256
LOCAL_ROWS = NZ * ROWS_DEV
VMEM = pl.BlockSpec(memory_space=pltpu.VMEM)


def device_index(x, y, z, c):
    return ((x * NY + y) * NZ + z) * NC + c


def permutation(target):
    pairs = []
    for x in range(NX):
        for y in range(NY):
            for z in range(NZ):
                for c in range(NC):
                    pairs.append((device_index(x, y, z, c), device_index(*target(x, y, z, c))))
    return pairs


def core_swap(value):
    return lax.ppermute(value, AXES, permutation(lambda x, y, z, c: (x, y, z, 1 - c)))


def pair_swap(value):
    return lax.ppermute(value, AXES, permutation(lambda x, y, z, c: (x, y, z ^ 1, c)))


def z_shift(value, d):
    return lax.ppermute(value, AXES, permutation(lambda x, y, z, c: (x, y, (z + d) % NZ, c)))


def f32(v):
    return v.astype(jnp.float32)


def params(mib):
    return pltpu.CompilerParams(vmem_limit_bytes=mib << 20)


def weight_kernel(x0, x1, x2, x3, g0, g1, g2, g3, o_ref):
    grads = jnp.concatenate([g[...] for g in (g0, g1, g2, g3)], axis=0)
    step = 512
    for first in range(0, x0.shape[1], step):
        left = jnp.concatenate([v[:, first : first + step] for v in (x0, x1, x2, x3)], axis=0)
        o_ref[first : first + step, :] = lax.dot_general(
            left, grads, (((0,), (0,)), ((), ())), preferred_element_type=jnp.float32
        ).astype(jnp.bfloat16)


def weight_part(tops, grads):
    return pl.pallas_call(
        weight_kernel,
        out_shape=jax.ShapeDtypeStruct((tops[0].shape[1], grads[0].shape[1]), jnp.bfloat16),
        in_specs=[VMEM] * 8,
        out_specs=VMEM,
        compiler_params=params(32),
        name="weight_part",
    )(*tops, *grads)


def table_kernel(chunk, rb, ids_ref, x_ref, y_ref, o_ref):
    samples = x_ref.shape[0]
    one = jnp.ones((), jnp.bfloat16)
    zero = jnp.zeros((), jnp.bfloat16)
    target = lax.broadcasted_iota(jnp.int32, (rb, chunk), 0).astype(jnp.int16)

    def do_block(k, carry):
        base = k * rb
        acc = jnp.zeros((rb, x_ref.shape[1]), jnp.float32)
        for s in range(2 * samples // chunk):
            ids = (ids_ref[:, s * chunk : (s + 1) * chunk] - base).astype(jnp.int16)
            counts = None
            for j in range(ids_ref.shape[0]):
                hit = jnp.where(jnp.broadcast_to(ids[j : j + 1], (rb, chunk)) == target, one, zero)
                counts = hit if counts is None else counts + hit
            first = s * chunk
            rows = x_ref[first : first + chunk, :] if first < samples else y_ref[first - samples : first - samples + chunk, :]
            acc = acc + jnp.dot(counts, rows, preferred_element_type=jnp.float32)
        o_ref[pl.ds(pl.multiple_of(base, rb), rb), :] = acc.astype(jnp.bfloat16)
        return carry

    lax.fori_loop(0, o_ref.shape[0] // rb, do_block, 0)


def table_partial(ids, x, y):
    return pl.pallas_call(
        functools.partial(table_kernel, 256, 512),
        out_shape=jax.ShapeDtypeStruct((LOCAL_ROWS, x.shape[1]), jnp.bfloat16),
        in_specs=[VMEM] * 3,
        out_specs=VMEM,
        compiler_params=params(32),
        name="table_partial",
    )(ids, x, y)


def body(top_input, grad_hidden, w_in, b_in, slice_map, lookup_ids, bag_len):
    chip = lax.axis_index("chip")
    z, core = lax.div(chip, NC), lax.rem(chip, NC)
    bit = lax.rem(z, 2)
    b_dev, width = top_input.shape
    hidden = grad_hidden.shape[1]
    slices = slice_map.shape[0]
    slw = width // slices
    half = hidden // 2
    quart = half // NC

    top_core = core_swap(top_input)
    top_pair = pair_swap(top_input)
    top_both = core_swap(top_pair)

    pre_act = jnp.dot(top_input, w_in, preferred_element_type=jnp.float32) + b_in
    gate_sig = jax.nn.sigmoid(pre_act)
    grad_pre = (f32(grad_hidden) * gate_sig * (1.0 + pre_act * (1.0 - gate_sig))).astype(jnp.bfloat16)

    keep = lax.dynamic_slice_in_dim(grad_pre, bit * half, half, 1)
    pair = pair_swap(lax.dynamic_slice_in_dim(grad_pre, (1 - bit) * half, half, 1))

    def mine(v):
        return lax.dynamic_slice_in_dim(v, core * quart, quart, 1)

    def other(v):
        return lax.dynamic_slice_in_dim(v, (1 - core) * quart, quart, 1)

    grads = (mine(keep), core_swap(other(keep)), mine(pair), core_swap(other(pair)))
    part = weight_part((top_input, top_core, top_pair, top_both), grads)

    pooled = lax.dot_general(
        grad_pre, w_in, (((1,), (1,)), ((), ())), preferred_element_type=jnp.float32
    ).astype(jnp.bfloat16)
    selector = (slice_map[:, None] == lax.iota(jnp.int32, slices)[None, :]).astype(jnp.bfloat16)
    ordered = jnp.einsum(
        "bkc,sk->sbc",
        pooled.reshape(b_dev, slices, slw),
        selector,
        preferred_element_type=jnp.float32,
    ).astype(jnp.bfloat16)
    received = lax.all_to_all(ordered, "hst", split_axis=0, concat_axis=1, tiled=True)[0]
    rec_other = core_swap(received)

    blocks = lax.all_to_all(
        part.reshape(NX * NY, width // (NX * NY), quart), "hst", split_axis=0, concat_axis=0, tiled=True
    )

    slots = lookup_ids.shape[1]
    ids = lookup_ids[0].reshape(slots, NX * NY, NZ, NC, b_dev)
    lens = bag_len[0].reshape(NX * NY, NZ, NC, b_dev)
    ids = lax.dynamic_index_in_dim(ids, z, 2, keepdims=False)
    lens = lax.dynamic_index_in_dim(lens, z, 1, keepdims=False)
    live = lax.iota(jnp.int32, slots)[:, None, None, None] < lens[None]
    here = (ids // ROWS_DEV) % NC == core
    local = (ids // (NC * ROWS_DEV)) * ROWS_DEV + ids % ROWS_DEV
    local = jnp.where(live & here, local, -1)
    near = lax.dynamic_index_in_dim(local, core, 2, keepdims=False).reshape(slots, -1)
    far = lax.dynamic_index_in_dim(local, 1 - core, 2, keepdims=False).reshape(slots, -1)
    local = jnp.concatenate([near, far], axis=1)
    table = table_partial(local, received, rec_other)
    table = table.reshape(NZ, ROWS_DEV, -1)

    def rows_of(d):
        return lax.dynamic_index_in_dim(table, lax.rem(z + d, NZ), 0, keepdims=False)

    table_grad = f32(rows_of(0))
    for d in (4, 3, 5, 2, 6, 1, 7):
        table_grad = table_grad + f32(z_shift(rows_of(d), d))

    summed = f32(blocks).sum(0).astype(jnp.bfloat16)
    rows_out = summed.shape[0] // (NZ * NC)
    swapped = lax.all_to_all(
        summed.reshape(NZ * NC, rows_out, quart), "chip", split_axis=0, concat_axis=0, tiled=True
    )
    total = f32(swapped).reshape(NZ // 2, 2 * NC, rows_out, quart).sum(0)
    w_in_grad = total.transpose(1, 0, 2).reshape(rows_out, hidden)
    return (w_in_grad, table_grad[None])


def solution(mesh):
    in_specs = (
        P(("hst", "chip"), None),
        P(("hst", "chip"), None),
        P(),
        P(),
        P(),
        P("hst", None, None),
        P("hst", None),
    )
    out_specs = (P(("hst", "chip"), None), P("hst", "chip", None))
    return jax.shard_map(body, mesh=mesh, in_specs=in_specs, out_specs=out_specs, check_vma=False)
```

time: 125 us -> 91.9 us (0.74)
  starting transfers between devices: 19 us -> 50 us
  blocking collectives: 23.9 us -> 0 us
  waiting for transfers between devices: 37.1 us -> 15.5 us
  between operations: 14.5 us -> 1.02 us
  local copies, waits for them, and re-layouts: 6.21 us -> 2.93 us
  matrix products: 11 us -> 8.64 us
  Pallas kernels: 7.82 us -> 9.42 us
    ppermute x15 -> x14, waiting for transfers between devices: 28 us -> 2.56 us  [the longest x5 2.53 us: core_swap(): lax.ppermute(value, AXES, permutation(lambda x, y, z, c: (x, y, z, 1 - c)))]
    all_to_all x1 -> x0, blocking collectives: 23.9 us -> none  [body(): lax.all_to_all(fin.reshape(NZ * NC, rows_out, half), 'chip', split_axis=0...]
    ppermute x15 -> x14, starting transfers between devices: 13.9 us -> 30.9 us  [the longest x7 17.7 us: z_shift(): lax.ppermute(value, AXES, permutation(lambda x, y, z, c: (x, y, (z + d) %...]
    all_to_all x0 -> x2, starting transfers between devices: none -> 14.1 us  [the longest x1 9.69 us: body(): lax.all_to_all(summed.reshape(NZ * NC, rows_out, quart), 'chip', split_ax...]
    all_to_all x0 -> x2, waiting for transfers between devices: none -> 8.39 us  [the longest x1 8.39 us: body(): lax.all_to_all(summed.reshape(NZ * NC, rows_out, quart), 'chip', split_ax...]
    all_to_all x1, waiting for transfers between devices: 9.09 us -> 4.51 us  [body(): lax.all_to_all(ordered, 'hst', split_axis=0, concat_axis=1, tiled=True)[0]]
    convert_element_type x2 -> x0, other arithmetic: 3.26 us -> none  [the longest x1 1.63 us: body(): (f32(take(part_a, 0, x)) + f32(got_a[0]) + f32(got_a[1]) + f32(got_a[2]))...]
    pallas_call x0 -> x1, Pallas kernels: none -> 2.6 us  [weight_part(): pl.pallas_call(weight_kernel, out_shape=jax.ShapeDtypeStruct((tops[0].sha...]
  transfers between devices with their start and end apart: 17 -> 17, of which waited for: 7 -> 4; matrix products, arithmetic and copies ran while one was open for 16% -> 16% of each run, Pallas kernels for 6% -> 10%
where the time goes in v2:
time: 91.9 us; the launch traced here: 91.5 us
  starting transfers between devices  50 us (54%)
  waiting for transfers between devices  15.5 us (17%)
  Pallas kernels  9.42 us (10%)
  matrix products  8.64 us (9%)
  other arithmetic  4.08 us (4%)
  local copies, waits for them, and re-layouts  2.93 us (3%)
  between operations  1.02 us (1%)
    ppermute x7, starting transfers between devices, z_shift(): lax.ppermute(value, AXES, permutation(lambda x, y, z, c: (x, y, (z + d) %...  17.7 us
    all_to_all x1, starting transfers between devices, body(): lax.all_to_all(summed.reshape(NZ * NC, rows_out, quart), 'chip', split_ax...  9.69 us
    ppermute x5, starting transfers between devices, core_swap(): lax.ppermute(value, AXES, permutation(lambda x, y, z, c: (x, y, z, 1 - c)))  8.95 us
    all_to_all x1, waiting for transfers between devices, body(): lax.all_to_all(summed.reshape(NZ * NC, rows_out, quart), 'chip', split_ax...  8.39 us
    pallas_call x1, Pallas kernels, table_partial(): pl.pallas_call(functools.partial(table_kernel, 256, 512), out_shape=jax.S...  6.82 us
    dot_general x1, matrix products, body(): jnp.dot(top_input, w_in, preferred_element_type=jnp.float32) + b_in  5.37 us
    all_to_all x1, starting transfers between devices, body(): lax.all_to_all(ordered, 'hst', split_axis=0, concat_axis=1, tiled=True)[0]  4.94 us
    all_to_all x1, waiting for transfers between devices, body(): lax.all_to_all(ordered, 'hst', split_axis=0, concat_axis=1, tiled=True)[0]  4.51 us
  transfers between devices with their start and end apart: 17, of which 4 were waited for; matrix products, arithmetic and copies ran while one was open for 16% of the time, Pallas kernels for 10%

profile of v2, /device:TPU:1, one launch (start us, length us, event | category | flops | bytes accessed | tf_op | source)
XLA Modules:
  0.0 91.5 jit_solution(15069893672583800667)
XLA Ops:
  0.6 0.0 copy-start
  0.6 2.6 %collective-permute-start.1 = (bf16[128,2048]{1,0:T(8,128)(2,1)}, bf16[128,2048]{1,0:T(8,128)(2,1)S(1)}, u32[]{:S(2)}, u32[]{:S(2)}) collective-permute-start(bf16[128,2048]{1,0:T(8,128)(2,1)} %x0.1), channel_id=1, source_target_pairs={{0,2},{1,3},{2,0},{3,1},{4,6},{5,7},{6,4},{7,5},{8,10},{9,11},{10,... | collective-permute-start | bytes 1572872 | tf_op jit(solution)/shard_map/ppermute | solution.py:36
  3.2 1.0 %collective-permute-start = (bf16[128,2048]{1,0:T(8,128)(2,1)}, bf16[128,2048]{1,0:T(8,128)(2,1)S(1)}, u32[]{:S(2)}, u32[]{:S(2)}) collective-permute-start(bf16[128,2048]{1,0:T(8,128)(2,1)} %x0.1), channel_id=1, source_target_pairs={{0,1},{1,0},{2,3},{3,2},{4,5},{5,4},{6,7},{7,6},{8,9},{9,8},{10,11... | collective-permute-start | bytes 1572872 | tf_op jit(solution)/shard_map/ppermute | solution.py:32
  4.2 0.0 copy-start.4
  4.2 0.0 copy-start.5
  4.2 5.4 %multiply_convert_fusion = (bf16[128,2048]{1,0:T(8,128)(2,1)S(1)}, f32[128,2048]{1,0:T(8,128)S(1)}) fusion(bf16[128,2048]{1,0:T(8,128)(2,1)} %param.8, f32[2048]{0:T(1024)} %param.10, bf16[128,2048]{1,0:T(8,128)(2,1)} %x0.1, bf16[2048,2048]{1,0:T(8,128)(2,1)} %param.9), kind=kOutput, calls=%fused_computation.4 | convolution fusion | flops 1076625408 | bytes 11018240 | tf_op jit(solution)/shard_map/dot_general | solution.py:122
  9.5 0.0 copy-start.3
  9.6 1.7 %collective-permute-start.4 = (bf16[128,1024]{1,0:T(8,128)(2,1)S(1)}, bf16[128,1024]{1,0:T(8,128)(2,1)}, u32[]{:S(2)}, u32[]{:S(2)}) collective-permute-start(bf16[128,1024]{1,0:T(8,128)(2,1)S(1)} %constant_dynamic-slice_fusion.4), channel_id=1, source_target_pairs={{0,2},{1,3},{2,0},{3,1},{4,6},{5,7},{6,4},{7,5},{8,10},{9,11},{10,... | collective-permute-start | bytes 786440 | tf_op jit(solution)/shard_map/ppermute | solution.py:36
  11.2 0.0 copy-done.4
  11.2 0.0 copy-done.5
  11.2 0.0 copy-start.1
  11.2 2.9 %fusion = bf16[16,8,16,128]{3,1,2,0:T(8,128)(2,1)S(1)} fusion(bf16[2048,2048]{1,0:T(8,128)(2,1)S(1)} %copy-done.4, f32[128,2048]{1,0:T(8,128)S(1)} %get-tuple-element.16, bf16[128,2048]{1,0:T(8,128)(2,1)S(1)} %copy-done.5), kind=kOutput, calls=%fused_computation.3 | convolution fusion | flops 1076625408 | bytes 10485760 | tf_op jit(solution)/shard_map/dot_general | solution.py:138
  14.2 0.1 copy.24
  14.3 0.0 collective-permute-done.1.x2
  14.3 4.7 %collective-permute-start.2 = (bf16[128,2048]{1,0:T(8,128)(2,1)S(1)}, bf16[128,2048]{1,0:T(8,128)(2,1)S(1)}, u32[]{:S(2)}, u32[]{:S(2)}) collective-permute-start(bf16[128,2048]{1,0:T(8,128)(2,1)S(1)} %collective-permute-done.1.x2), channel_id=1, source_target_pairs={{0,1},{1,0},{2,3},{3,2},{4,5},{5,4},{6,7},{7,6},{8,9},{9,8},{10,11... | collective-permute-start | bytes 1572872 | tf_op jit(solution)/shard_map/ppermute | solution.py:32
  19.0 0.0 copy-done.3
  19.0 0.3 convolution_convert_fusion.1
  19.4 0.9 %copy.21 = bf16[16,128,128]{2,1,0:T(8,128)(2,1)} copy(bf16[16,128,128]{2,0,1:T(8,128)(2,1)S(1)} %convolution_convert_fusion.1) | data formatting | bytes 1048576 | tf_op jit(solution)/shard_map/convert_element_type | solution.py:147
  20.3 4.9 %all-to-all-start.2 = ((bf16[16,128,128]{2,1,0:T(8,128)(2,1)}), bf16[16,128,128]{2,1,0:T(8,128)(2,1)S(1)}, u32[]{:S(2)}, u32[]{:S(2)}) async-start(bf16[16,128,128]{2,1,0:T(8,128)(2,1)} %copy.21), calls=%async_computation.2 | async-start | bytes 1048576 | tf_op jit(solution)/shard_map/all_to_all | solution.py:148
  25.3 0.2 constant_dynamic-slice_fusion.5
  25.5 0.0 copy-start.2
  25.5 0.4 collective-permute-start.3
  25.9 0.0 collective-permute-done.4
  25.9 1.0 %constant_dynamic-slice_fusion.2 = (bf16[128,512]{1,0:T(8,128)(2,1)S(1)}, bf16[128,512]{1,0:T(8,128)(2,1)S(1)}) fusion(bf16[128,1024]{1,0:T(8,128)(2,1)} %collective-permute-done.4, s32[]{:T(128)S(6)} %select_n.85, s32[]{:T(128)S(6)} %select_n.81), kind=kLoop, calls=%fused_computation.59 | loop fusion | bytes 524296 | tf_op jit(solution)/shard_map/dynamic_slice | solution.py:133
  26.9 0.3 collective-permute-start.5
  27.2 0.0 collective-permute-done.3.g1
  27.2 1.1 %collective-permute-done.5.g3 = bf16[128,512]{1,0:T(8,128)(2,1)S(1)} collective-permute-done((bf16[128,512]{1,0:T(8,128)(2,1)S(1)}, bf16[128,512]{1,0:T(8,128)(2,1)S(1)}, u32[]{:S(2)}, u32[]{:S(2)}) %collective-permute-start.5) | collective-permute-done | bytes 131104 | tf_op jit(solution)/shard_map/ppermute | solution.py:32
  28.3 0.0 collective-permute-done.x1
  28.3 0.0 collective-permute-done.2.x3
  28.3 0.0 copy-done.1
  28.3 2.6 %weight_part.1 = bf16[2048,512]{1,0:T(8,128)(2,1)} custom-call(bf16[128,2048]{1,0:T(8,128)(2,1)S(1)} %copy-done.1, bf16[128,2048]{1,0:T(8,128)(2,1)S(1)} %collective-permute-done.x1, bf16[128,2048]{1,0:T(8,128)(2,1)S(1)} %collective-permute-done.1.x2, bf16[128,2048]{1,0:T(8,128)(2,1)S(1)} %collective-permute-done.2.x3, ...), custom_call_target="tpu_custom_call" | custom-call | tf_op jit(solution)/shard_map/weight_part/pallas_call | solution.py:62
  30.9 4.5 %all-to-all-done.2 = bf16[16,128,128]{2,1,0:T(8,128)(2,1)S(1)} async-done(((bf16[16,128,128]{2,1,0:T(8,128)(2,1)}), bf16[16,128,128]{2,1,0:T(8,128)(2,1)S(1)}, u32[]{:S(2)}, u32[]{:S(2)}) %all-to-all-start.2) | async-done | bytes 524320 | tf_op jit(solution)/shard_map/all_to_all | solution.py:148
  35.4 4.4 %all-to-all-start = ((bf16[16,128,512]{2,1,0:T(8,128)(2,1)}), bf16[16,128,512]{2,1,0:T(8,128)(2,1)}, u32[]{:S(2)}, u32[]{:S(2)}) async-start(bf16[16,128,512]{2,1,0:T(8,128)(2,1)} %bitcast), calls=%async_computation | async-start | bytes 4194304 | tf_op jit(solution)/shard_map/all_to_all | solution.py:151
  39.9 0.0 copy-done.2
  39.9 0.5 reshape_squeeze.7
  40.4 0.0 copy-done
  40.5 0.1 fusion.15
  40.7 2.6 %collective-permute-start.6 = (bf16[2048,128]{1,0:T(8,128)(2,1)S(1)}, bf16[2048,128]{1,0:T(8,128)(2,1)S(1)}, u32[]{:S(2)}, u32[]{:S(2)}) collective-permute-start(bf16[2048,128]{1,0:T(8,128)(2,1)S(1)} %bitcast.73), channel_id=1, source_target_pairs={{0,1},{1,0},{2,3},{3,2},{4,5},{5,4},{6,7},{7,6},{8,9},{9,8},{10,11... | collective-permute-start | bytes 1572872 | tf_op jit(solution)/shard_map/ppermute | solution.py:32
  43.4 1.4 %collective-permute-done.6.y_ref = bf16[2048,128]{1,0:T(8,128)(2,1)S(1)} collective-permute-done((bf16[2048,128]{1,0:T(8,128)(2,1)S(1)}, bf16[2048,128]{1,0:T(8,128)(2,1)S(1)}, u32[]{:S(2)}, u32[]{:S(2)}) %collective-permute-start.6) | collective-permute-done | bytes 524320 | tf_op jit(solution)/shard_map/ppermute | solution.py:32
  44.8 6.8 %table_partial.1 = bf16[2048,128]{1,0:T(8,128)(2,1)S(1)} custom-call(s32[4,4096]{1,0:T(4,128)S(1)} %pad_add_fusion.ids_ref, bf16[2048,128]{1,0:T(8,128)(2,1)S(1)} %bitcast.74, bf16[2048,128]{1,0:T(8,128)(2,1)S(1)} %collective-permute-done.6.y_ref), custom_call_target="tpu_custom_call" | custom-call | tf_op jit(solution)/shard_map/table_partial/pallas_call | solution.py:97
  51.7 3.1 %collective-permute-start.10 = (bf16[256,128]{1,0:T(8,128)(2,1)S(1)}, bf16[256,128]{1,0:T(8,128)(2,1)S(1)}, u32[]{:S(2)}, u32[]{:S(2)}) collective-permute-start(bf16[256,128]{1,0:T(8,128)(2,1)S(1)} %get-tuple-element.6), channel_id=1, source_target_pairs={{0,4},{1,5},{2,6},{3,7},{4,8},{5,9},{6,10},{7,11},{8,12},{9,13},{1... | collective-permute-start | bytes 196616 | tf_op jit(solution)/shard_map/ppermute | solution.py:40
  54.8 3.1 %collective-permute-start.11 = (bf16[256,128]{1,0:T(8,128)(2,1)S(1)}, bf16[256,128]{1,0:T(8,128)(2,1)S(1)}, u32[]{:S(2)}, u32[]{:S(2)}) collective-permute-start(bf16[256,128]{1,0:T(8,128)(2,1)S(1)} %get-tuple-element.5), channel_id=1, source_target_pairs={{0,12},{1,13},{2,14},{3,15},{4,0},{5,1},{6,2},{7,3},{8,4},{9,5},{1... | collective-permute-start | bytes 196616 | tf_op jit(solution)/shard_map/ppermute | solution.py:40
  57.9 0.7 collective-permute-start.12
  58.6 1.9 %collective-permute-start.13 = (bf16[256,128]{1,0:T(8,128)(2,1)S(1)}, bf16[256,128]{1,0:T(8,128)(2,1)S(1)}, u32[]{:S(2)}, u32[]{:S(2)}) collective-permute-start(bf16[256,128]{1,0:T(8,128)(2,1)S(1)} %get-tuple-element.3), channel_id=1, source_target_pairs={{0,14},{1,15},{2,0},{3,1},{4,2},{5,3},{6,4},{7,5},{8,6},{9,7},{10,... | collective-permute-start | bytes 196616 | tf_op jit(solution)/shard_map/ppermute | solution.py:40
  60.6 4.4 %collective-permute-start.7 = (bf16[256,128]{1,0:T(8,128)(2,1)S(1)}, bf16[256,128]{1,0:T(8,128)(2,1)S(1)}, u32[]{:S(2)}, u32[]{:S(2)}) collective-permute-start(bf16[256,128]{1,0:T(8,128)(2,1)S(1)} %get-tuple-element.2), channel_id=1, source_target_pairs={{0,8},{1,9},{2,10},{3,11},{4,12},{5,13},{6,14},{7,15},{8,0},{9,1},... | collective-permute-start | bytes 196616 | tf_op jit(solution)/shard_map/ppermute | solution.py:40
  65.0 0.0 collective-permute-done.10
  65.0 0.0 collective-permute-start.8
  65.0 0.0 collective-permute-done.11
  65.0 4.5 %collective-permute-start.9 = (bf16[256,128]{1,0:T(8,128)(2,1)S(1)}, bf16[256,128]{1,0:T(8,128)(2,1)S(1)}, u32[]{:S(2)}, u32[]{:S(2)}) collective-permute-start(bf16[256,128]{1,0:T(8,128)(2,1)S(1)} %get-tuple-element.7), channel_id=1, source_target_pairs={{0,10},{1,11},{2,12},{3,13},{4,14},{5,15},{6,0},{7,1},{8,2},{9,3},... | collective-permute-start | bytes 196616 | tf_op jit(solution)/shard_map/ppermute | solution.py:40
  69.4 0.0 all-to-all-done
  69.4 2.6 %reduce_sum.21 = bf16[128,512]{1,0:T(8,128)(2,1)} reduce(bf16[16,128,512]{2,1,0:T(8,128)(2,1)} %all-to-all-done, bf16[]{:T(256)} %constant.138.clone.1), dimensions={0}, to_apply=%region_0.1 | reduce | flops 983040 | bytes 2228226 | tf_op jit(solution)/shard_map/reduce_sum | solution.py:177
  72.0 9.7 %all-to-all-start.1 = ((bf16[16,8,512]{2,1,0:T(8,128)(2,1)}), bf16[16,8,512]{2,1,0:T(8,128)(2,1)S(1)}, u32[]{:S(2)}, u32[]{:S(2)}) async-start(bf16[16,8,512]{2,1,0:T(8,128)(2,1)} %bitcast.1), calls=%async_computation.1 | async-start | bytes 262144 | tf_op jit(solution)/shard_map/all_to_all | solution.py:179
  81.7 0.0 collective-permute-done.12
  81.7 0.0 collective-permute-done.13
  81.7 0.0 collective-permute-done.7
  81.7 0.0 collective-permute-done.8
  81.7 0.0 collective-permute-done.9
  81.7 0.7 fusion.9
  82.5 8.4 %all-to-all-done.1 = bf16[16,8,512]{2,1,0:T(8,128)(2,1)S(1)} async-done(((bf16[16,8,512]{2,1,0:T(8,128)(2,1)}), bf16[16,8,512]{2,1,0:T(8,128)(2,1)S(1)}, u32[]{:S(2)}, u32[]{:S(2)}) %all-to-all-start.1) | async-done | bytes 131104 | tf_op jit(solution)/shard_map/all_to_all | solution.py:179
  90.9 0.6 convert_reduce_fusion
  (8 shorter events, 0.2 us)
Async XLA Ops:
  0.6 39.8 %copy-start = (s32[1,32768]{1,0:T(1,128)S(1)}, s32[1,32768]{1,0:T(1,128)}, u32[]{:S(2)}) copy-start(s32[1,32768]{1,0:T(1,128)} %param.13) | copy-start | bytes 393220
  0.6 13.7 %collective-permute-start.1 = (bf16[128,2048]{1,0:T(8,128)(2,1)}, bf16[128,2048]{1,0:T(8,128)(2,1)S(1)}, u32[]{:S(2)}, u32[]{:S(2)}) collective-permute-start(bf16[128,2048]{1,0:T(8,128)(2,1)} %x0.1), channel_id=1, source_target_pairs={{0,2},{1,3},{2,0},{3,1},{4,6},{5,7},{6,4},{7,5},{8,10},{9,11},{10,... | collective-permute-start | bytes 1572872 | tf_op jit(solution)/shard_map/ppermute | solution.py:36
  3.2 25.1 %collective-permute-start = (bf16[128,2048]{1,0:T(8,128)(2,1)}, bf16[128,2048]{1,0:T(8,128)(2,1)S(1)}, u32[]{:S(2)}, u32[]{:S(2)}) collective-permute-start(bf16[128,2048]{1,0:T(8,128)(2,1)} %x0.1), channel_id=1, source_target_pairs={{0,1},{1,0},{2,3},{3,2},{4,5},{5,4},{6,7},{7,6},{8,9},{9,8},{10,11... | collective-permute-start | bytes 1572872 | tf_op jit(solution)/shard_map/ppermute | solution.py:32
  4.2 7.1 %copy-start.4 = (bf16[2048,2048]{1,0:T(8,128)(2,1)S(1)}, bf16[2048,2048]{1,0:T(8,128)(2,1)}, u32[]{:S(2)}) copy-start(bf16[2048,2048]{1,0:T(8,128)(2,1)} %param.9) | copy-start | bytes 25165828
  4.2 7.1 %copy-start.5 = (bf16[128,2048]{1,0:T(8,128)(2,1)S(1)}, bf16[128,2048]{1,0:T(8,128)(2,1)}, u32[]{:S(2)}) copy-start(bf16[128,2048]{1,0:T(8,128)(2,1)} %param.8) | copy-start | bytes 1572868
  9.5 9.5 %copy-start.3 = (s32[16]{0:T(128)S(1)}, s32[16]{0:T(128)}, u32[]{:S(2)}) copy-start(s32[16]{0:T(128)} %param.11) | copy-start | bytes 196
  9.6 16.3 %collective-permute-start.4 = (bf16[128,1024]{1,0:T(8,128)(2,1)S(1)}, bf16[128,1024]{1,0:T(8,128)(2,1)}, u32[]{:S(2)}, u32[]{:S(2)}) collective-permute-start(bf16[128,1024]{1,0:T(8,128)(2,1)S(1)} %constant_dynamic-slice_fusion.4), channel_id=1, source_target_pairs={{0,2},{1,3},{2,0},{3,1},{4,6},{5,7},{6,4},{7,5},{8,10},{9,11},{10,... | collective-permute-start | bytes 786440 | tf_op jit(solution)/shard_map/ppermute | solution.py:36
  11.2 17.1 %copy-start.1 = (bf16[128,2048]{1,0:T(8,128)(2,1)S(1)}, bf16[128,2048]{1,0:T(8,128)(2,1)}, u32[]{:S(2)}) copy-start(bf16[128,2048]{1,0:T(8,128)(2,1)} %x0.1) | copy-start | bytes 1572868
  14.3 14.0 %collective-permute-start.2 = (bf16[128,2048]{1,0:T(8,128)(2,1)S(1)}, bf16[128,2048]{1,0:T(8,128)(2,1)S(1)}, u32[]{:S(2)}, u32[]{:S(2)}) collective-permute-start(bf16[128,2048]{1,0:T(8,128)(2,1)S(1)} %collective-permute-done.1.x2), channel_id=1, source_target_pairs={{0,1},{1,0},{2,3},{3,2},{4,5},{5,4},{6,7},{7,6},{8,9},{9,8},{10,11... | collective-permute-start | bytes 1572872 | tf_op jit(solution)/shard_map/ppermute | solution.py:32
  20.3 15.1 %all-to-all-start.2 = ((bf16[16,128,128]{2,1,0:T(8,128)(2,1)}), bf16[16,128,128]{2,1,0:T(8,128)(2,1)S(1)}, u32[]{:S(2)}, u32[]{:S(2)}) async-start(bf16[16,128,128]{2,1,0:T(8,128)(2,1)} %copy.21), calls=%async_computation.2 | async-start | bytes 1048576 | tf_op jit(solution)/shard_map/all_to_all | solution.py:148
  25.5 14.4 %copy-start.2 = (s32[1,4,32768]{2,1,0:T(4,128)S(1)}, s32[1,4,32768]{2,1,0:T(4,128)}, u32[]{:S(2)}) copy-start(s32[1,4,32768]{2,1,0:T(4,128)} %param.12) | copy-start | bytes 1572868
  25.5 1.7 %collective-permute-start.3 = (bf16[128,512]{1,0:T(8,128)(2,1)S(1)}, bf16[128,512]{1,0:T(8,128)(2,1)S(1)}, u32[]{:S(2)}, u32[]{:S(2)}) collective-permute-start(bf16[128,512]{1,0:T(8,128)(2,1)S(1)} %get-tuple-element.9), channel_id=1, source_target_pairs={{0,1},{1,0},{2,3},{3,2},{4,5},{5,4},{6,7},{7,6},{8,9},{9,8},{10,11... | collective-permute-start | bytes 393224 | tf_op jit(solution)/shard_map/ppermute | solution.py:32
  26.9 1.4 %collective-permute-start.5 = (bf16[128,512]{1,0:T(8,128)(2,1)S(1)}, bf16[128,512]{1,0:T(8,128)(2,1)S(1)}, u32[]{:S(2)}, u32[]{:S(2)}) collective-permute-start(bf16[128,512]{1,0:T(8,128)(2,1)S(1)} %get-tuple-element.11), channel_id=1, source_target_pairs={{0,1},{1,0},{2,3},{3,2},{4,5},{5,4},{6,7},{7,6},{8,9},{9,8},{10,11... | collective-permute-start | bytes 393224 | tf_op jit(solution)/shard_map/ppermute | solution.py:32
  35.4 34.0 %all-to-all-start = ((bf16[16,128,512]{2,1,0:T(8,128)(2,1)}), bf16[16,128,512]{2,1,0:T(8,128)(2,1)}, u32[]{:S(2)}, u32[]{:S(2)}) async-start(bf16[16,128,512]{2,1,0:T(8,128)(2,1)} %bitcast), calls=%async_computation | async-start | bytes 4194304 | tf_op jit(solution)/shard_map/all_to_all | solution.py:151
  40.7 4.1 %collective-permute-start.6 = (bf16[2048,128]{1,0:T(8,128)(2,1)S(1)}, bf16[2048,128]{1,0:T(8,128)(2,1)S(1)}, u32[]{:S(2)}, u32[]{:S(2)}) collective-permute-start(bf16[2048,128]{1,0:T(8,128)(2,1)S(1)} %bitcast.73), channel_id=1, source_target_pairs={{0,1},{1,0},{2,3},{3,2},{4,5},{5,4},{6,7},{7,6},{8,9},{9,8},{10,11... | collective-permute-start | bytes 1572872 | tf_op jit(solution)/shard_map/ppermute | solution.py:32
  51.7 13.3 %collective-permute-start.10 = (bf16[256,128]{1,0:T(8,128)(2,1)S(1)}, bf16[256,128]{1,0:T(8,128)(2,1)S(1)}, u32[]{:S(2)}, u32[]{:S(2)}) collective-permute-start(bf16[256,128]{1,0:T(8,128)(2,1)S(1)} %get-tuple-element.6), channel_id=1, source_target_pairs={{0,4},{1,5},{2,6},{3,7},{4,8},{5,9},{6,10},{7,11},{8,12},{9,13},{1... | collective-permute-start | bytes 196616 | tf_op jit(solution)/shard_map/ppermute | solution.py:40
  54.8 10.2 %collective-permute-start.11 = (bf16[256,128]{1,0:T(8,128)(2,1)S(1)}, bf16[256,128]{1,0:T(8,128)(2,1)S(1)}, u32[]{:S(2)}, u32[]{:S(2)}) collective-permute-start(bf16[256,128]{1,0:T(8,128)(2,1)S(1)} %get-tuple-element.5), channel_id=1, source_target_pairs={{0,12},{1,13},{2,14},{3,15},{4,0},{5,1},{6,2},{7,3},{8,4},{9,5},{1... | collective-permute-start | bytes 196616 | tf_op jit(solution)/shard_map/ppermute | solution.py:40
  57.9 23.8 %collective-permute-start.12 = (bf16[256,128]{1,0:T(8,128)(2,1)S(1)}, bf16[256,128]{1,0:T(8,128)(2,1)S(1)}, u32[]{:S(2)}, u32[]{:S(2)}) collective-permute-start(bf16[256,128]{1,0:T(8,128)(2,1)S(1)} %get-tuple-element.4), channel_id=1, source_target_pairs={{0,2},{1,3},{2,4},{3,5},{4,6},{5,7},{6,8},{7,9},{8,10},{9,11},{10,... | collective-permute-start | bytes 196616 | tf_op jit(solution)/shard_map/ppermute | solution.py:40
  58.6 23.1 %collective-permute-start.13 = (bf16[256,128]{1,0:T(8,128)(2,1)S(1)}, bf16[256,128]{1,0:T(8,128)(2,1)S(1)}, u32[]{:S(2)}, u32[]{:S(2)}) collective-permute-start(bf16[256,128]{1,0:T(8,128)(2,1)S(1)} %get-tuple-element.3), channel_id=1, source_target_pairs={{0,14},{1,15},{2,0},{3,1},{4,2},{5,3},{6,4},{7,5},{8,6},{9,7},{10,... | collective-permute-start | bytes 196616 | tf_op jit(solution)/shard_map/ppermute | solution.py:40
  60.6 21.1 %collective-permute-start.7 = (bf16[256,128]{1,0:T(8,128)(2,1)S(1)}, bf16[256,128]{1,0:T(8,128)(2,1)S(1)}, u32[]{:S(2)}, u32[]{:S(2)}) collective-permute-start(bf16[256,128]{1,0:T(8,128)(2,1)S(1)} %get-tuple-element.2), channel_id=1, source_target_pairs={{0,8},{1,9},{2,10},{3,11},{4,12},{5,13},{6,14},{7,15},{8,0},{9,1},... | collective-permute-start | bytes 196616 | tf_op jit(solution)/shard_map/ppermute | solution.py:40
  65.0 16.8 %collective-permute-start.8 = (bf16[256,128]{1,0:T(8,128)(2,1)S(1)}, bf16[256,128]{1,0:T(8,128)(2,1)S(1)}, u32[]{:S(2)}, u32[]{:S(2)}) collective-permute-start(bf16[256,128]{1,0:T(8,128)(2,1)S(1)} %get-tuple-element.8), channel_id=1, source_target_pairs={{0,6},{1,7},{2,8},{3,9},{4,10},{5,11},{6,12},{7,13},{8,14},{9,15},... | collective-permute-start | bytes 196616 | tf_op jit(solution)/shard_map/ppermute | solution.py:40
  65.0 16.8 %collective-permute-start.9 = (bf16[256,128]{1,0:T(8,128)(2,1)S(1)}, bf16[256,128]{1,0:T(8,128)(2,1)S(1)}, u32[]{:S(2)}, u32[]{:S(2)}) collective-permute-start(bf16[256,128]{1,0:T(8,128)(2,1)S(1)} %get-tuple-element.7), channel_id=1, source_target_pairs={{0,10},{1,11},{2,12},{3,13},{4,14},{5,15},{6,0},{7,1},{8,2},{9,3},... | collective-permute-start | bytes 196616 | tf_op jit(solution)/shard_map/ppermute | solution.py:40
  72.0 18.9 %all-to-all-start.1 = ((bf16[16,8,512]{2,1,0:T(8,128)(2,1)}), bf16[16,8,512]{2,1,0:T(8,128)(2,1)S(1)}, u32[]{:S(2)}, u32[]{:S(2)}) async-start(bf16[16,8,512]{2,1,0:T(8,128)(2,1)} %bitcast.1), calls=%async_computation.1 | async-start | bytes 262144 | tf_op jit(solution)/shard_map/all_to_all | solution.py:179

commit v3 on v2

--- a/solution.py
+++ b/solution.py
@@ -12,6 +12,7 @@
 ROWS_DEV = 256
 LOCAL_ROWS = NZ * ROWS_DEV
 VMEM = pl.BlockSpec(memory_space=pltpu.VMEM)
+HBM = pl.BlockSpec(memory_space=pltpu.MemorySpace.HBM)
 
 
 def device_index(x, y, z, c):
@@ -44,8 +45,84 @@
     return v.astype(jnp.float32)
 
 
+def in_hbm(v):
+    return pltpu.with_memory_space_constraint(v, pltpu.MemorySpace.HBM)
+
+
 def params(mib):
     return pltpu.CompilerParams(vmem_limit_bytes=mib << 20)
+
+
+def front_kernel(map_hbm, top_hbm, gh_hbm, w_hbm, b_hbm, gp_ref, out_ref, map_ref, top_ref, gh_ref, w_ref, b_ref, acc_ref, sems):
+    hidden = gh_ref.shape[1]
+    blocks = sems.shape[0] - 4
+    block = hidden // blocks
+    small = [
+        pltpu.make_async_copy(src, dst, sems.at[k])
+        for k, (src, dst) in enumerate(
+            ((top_hbm, top_ref), (b_hbm, b_ref), (gh_hbm, gh_ref), (map_hbm, map_ref))
+        )
+    ]
+    large = [
+        pltpu.make_async_copy(
+            w_hbm.at[:, pl.ds(j * block, block)],
+            w_ref.at[:, pl.ds(j * block, block)],
+            sems.at[4 + j],
+        )
+        for j in range(blocks)
+    ]
+    for copy in small[:1] + large[:1] + small[1:] + large[1:]:
+        copy.start()
+    for j in range(blocks):
+        cols = slice(j * block, (j + 1) * block)
+        if j == 0:
+            small[0].wait()
+        large[j].wait()
+        w = w_ref[:, cols]
+        pre = jnp.dot(top_ref[...], w, preferred_element_type=jnp.float32)
+        if j == 0:
+            for copy in small[1:]:
+                copy.wait()
+        pre = pre + b_ref[:, cols]
+        sig = 1.0 / (1.0 + jnp.exp(-pre))
+        grad = (f32(gh_ref[:, cols]) * sig * (1.0 + pre * (1.0 - sig))).astype(jnp.bfloat16)
+        gp_ref[:, cols] = grad
+        part = lax.dot_general(grad, w, (((1,), (1,)), ((), ())), preferred_element_type=jnp.float32)
+        if j == 0:
+            acc_ref[...] = part
+        else:
+            acc_ref[...] += part
+    slw = out_ref.shape[2]
+    for s in range(out_ref.shape[0]):
+        first = pl.multiple_of(map_ref[s] * slw, slw)
+        out_ref[s] = acc_ref[:, pl.ds(first, slw)].astype(jnp.bfloat16)
+
+
+def front(slice_map, top_input, grad_hidden, w_in, b_in, blocks=4):
+    b_dev, width = top_input.shape
+    hidden = grad_hidden.shape[1]
+    slices = slice_map.shape[0]
+    slw = width // slices
+    return pl.pallas_call(
+        front_kernel,
+        in_specs=[HBM] * 5,
+        out_specs=[VMEM] * 2,
+        out_shape=[
+            jax.ShapeDtypeStruct((b_dev, hidden), jnp.bfloat16),
+            jax.ShapeDtypeStruct((slices, b_dev, slw), jnp.bfloat16),
+        ],
+        scratch_shapes=[
+            pltpu.SMEM((slices,), jnp.int32),
+            pltpu.VMEM((b_dev, width), jnp.bfloat16),
+            pltpu.VMEM((b_dev, hidden), jnp.bfloat16),
+            pltpu.VMEM((width, hidden), jnp.bfloat16),
+            pltpu.VMEM((1, hidden), jnp.float32),
+            pltpu.VMEM((b_dev, width), jnp.float32),
+            pltpu.SemaphoreType.DMA((4 + blocks,)),
+        ],
+        compiler_params=params(40),
+        name="front",
+    )(*[in_hbm(v) for v in (slice_map, top_input, grad_hidden, w_in, b_in[None])])
 
 
 def weight_kernel(x0, x1, x2, x3, g0, g1, g2, g3, o_ref):
@@ -110,22 +187,23 @@
     bit = lax.rem(z, 2)
     b_dev, width = top_input.shape
     hidden = grad_hidden.shape[1]
-    slices = slice_map.shape[0]
-    slw = width // slices
     half = hidden // 2
     quart = half // NC
 
     top_core = core_swap(top_input)
     top_pair = pair_swap(top_input)
-    top_both = core_swap(top_pair)
-
-    pre_act = jnp.dot(top_input, w_in, preferred_element_type=jnp.float32) + b_in
-    gate_sig = jax.nn.sigmoid(pre_act)
-    grad_pre = (f32(grad_hidden) * gate_sig * (1.0 + pre_act * (1.0 - gate_sig))).astype(jnp.bfloat16)
+
+    grad_pre, ordered = front(slice_map, top_input, grad_hidden, w_in, b_in)
 
     keep = lax.dynamic_slice_in_dim(grad_pre, bit * half, half, 1)
     pair = pair_swap(lax.dynamic_slice_in_dim(grad_pre, (1 - bit) * half, half, 1))
 
+    top_pair, pair = lax.optimization_barrier((top_pair, pair))
+    piece = b_dev // 4
+    top_both = jnp.concatenate(
+        [core_swap(top_pair[k * piece : (k + 1) * piece]) for k in range(4)], axis=0
+    )
+
     def mine(v):
         return lax.dynamic_slice_in_dim(v, core * quart, quart, 1)
 
@@ -135,16 +213,6 @@
     grads = (mine(keep), core_swap(other(keep)), mine(pair), core_swap(other(pair)))
     part = weight_part((top_input, top_core, top_pair, top_both), grads)
 
-    pooled = lax.dot_general(
-        grad_pre, w_in, (((1,), (1,)), ((), ())), preferred_element_type=jnp.float32
-    ).astype(jnp.bfloat16)
-    selector = (slice_map[:, None] == lax.iota(jnp.int32, slices)[None, :]).astype(jnp.bfloat16)
-    ordered = jnp.einsum(
-        "bkc,sk->sbc",
-        pooled.reshape(b_dev, slices, slw),
-        selector,
-        preferred_element_type=jnp.float32,
-    ).astype(jnp.bfloat16)
     received = lax.all_to_all(ordered, "hst", split_axis=0, concat_axis=1, tiled=True)[0]
     rec_other = core_swap(received)
 
@@ -174,7 +242,10 @@
     for d in (4, 3, 5, 2, 6, 1, 7):
         table_grad = table_grad + f32(z_shift(rows_of(d), d))
 
-    summed = f32(blocks).sum(0).astype(jnp.bfloat16)
+    summed = f32(blocks[0])
+    for h in range(1, NX * NY):
+        summed = summed + f32(blocks[h])
+    summed = summed.astype(jnp.bfloat16)
     rows_out = summed.shape[0] // (NZ * NC)
     swapped = lax.all_to_all(
         summed.reshape(NZ * NC, rows_out, quart), "chip", split_axis=0, concat_axis=0, tiled=True

time: 91.9 us -> 86.1 us (0.937)
  matrix products: 8.64 us -> 0 us
  Pallas kernels: 9.42 us -> 17 us
  starting transfers between devices: 50 us -> 47.8 us
  local copies, waits for them, and re-layouts: 2.93 us -> 0.93 us
    dot_general x3 -> x0, matrix products: 8.64 us -> none  [the longest x1 5.37 us: body(): jnp.dot(top_input, w_in, preferred_element_type=jnp.float32) + b_in]
    pallas_call x0 -> x1, Pallas kernels: none -> 7.55 us  [front(): pl.pallas_call(front_kernel, in_specs=[HBM] * 5, out_specs=[VMEM] * 2, ou...]
    all_to_all x1, waiting for transfers between devices: 4.51 us -> 1.51 us  [body(): lax.all_to_all(ordered, 'hst', split_axis=0, concat_axis=1, tiled=True)[0]]
    reduce_sum x1 -> x0, other arithmetic: 2.57 us -> none  [body(): summed = f32(blocks).sum(0).astype(jnp.bfloat16)]
    convert_element_type x0 -> x1, other arithmetic: none -> 2.52 us  [body(): summed = summed.astype(jnp.bfloat16)]
    ppermute x2, starting transfers between devices: 4.2 us -> 2.68 us  [pair_swap(): lax.ppermute(value, AXES, permutation(lambda x, y, z, c: (x, y, z ^ 1, c)))]
    ppermute x7, starting transfers between devices: 17.7 us -> 16.2 us  [z_shift(): lax.ppermute(value, AXES, permutation(lambda x, y, z, c: (x, y, (z + d) %...]
    ppermute x7, waiting for transfers between devices: 0.02 us -> 1.5 us  [z_shift(): lax.ppermute(value, AXES, permutation(lambda x, y, z, c: (x, y, (z + d) %...]
  transfers between devices with their start and end apart: 17 -> 20, of which waited for: 4 -> 9; matrix products, arithmetic and copies ran while one was open for 16% -> 5% of each run, Pallas kernels for 10% -> 20%
where the time goes in v3:
time: 86.1 us; the launch traced here: 85.7 us
  starting transfers between devices  47.8 us (56%)
  Pallas kernels  17 us (20%)
  waiting for transfers between devices  15 us (17%)
  other arithmetic  4.07 us (5%)
  between operations  0.99 us (1%)
  local copies, waits for them, and re-layouts  0.93 us (1%)
    ppermute x7, starting transfers between devices, z_shift(): lax.ppermute(value, AXES, permutation(lambda x, y, z, c: (x, y, (z + d) %...  16.2 us
    all_to_all x1, starting transfers between devices, body(): lax.all_to_all(summed.reshape(NZ * NC, rows_out, quart), 'chip', split_ax...  10.4 us
    all_to_all x1, waiting for transfers between devices, body(): lax.all_to_all(summed.reshape(NZ * NC, rows_out, quart), 'chip', split_ax...  8.39 us
    ppermute x8, starting transfers between devices, core_swap(): lax.ppermute(value, AXES, permutation(lambda x, y, z, c: (x, y, z, 1 - c)))  8.02 us
    pallas_call x1, Pallas kernels, front(): pl.pallas_call(front_kernel, in_specs=[HBM] * 5, out_specs=[VMEM] * 2, ou...  7.55 us
    pallas_call x1, Pallas kernels, table_partial(): pl.pallas_call(functools.partial(table_kernel, 256, 512), out_shape=jax.S...  6.83 us
    all_to_all x1, starting transfers between devices, body(): lax.all_to_all(part.reshape(NX * NY, width // (NX * NY), quart), 'hst', s...  5.42 us
    all_to_all x1, starting transfers between devices, body(): lax.all_to_all(ordered, 'hst', split_axis=0, concat_axis=1, tiled=True)[0]  5.01 us
  transfers between devices with their start and end apart: 20, of which 9 were waited for; matrix products, arithmetic and copies ran while one was open for 5% of the time, Pallas kernels for 20%

profile of v3, /device:TPU:1, one launch (start us, length us, event | category | flops | bytes accessed | tf_op | source)
XLA Modules:
  0.0 85.7 jit_solution(6607209868809036589)
XLA Ops:
  0.6 0.0 copy-start
  0.6 2.6 %collective-permute-start.1 = (bf16[128,2048]{1,0:T(8,128)(2,1)}, bf16[128,2048]{1,0:T(8,128)(2,1)S(1)}, u32[]{:S(2)}, u32[]{:S(2)}) collective-permute-start(bf16[128,2048]{1,0:T(8,128)(2,1)} %x0.1), channel_id=1, source_target_pairs={{0,2},{1,3},{2,0},{3,1},{4,6},{5,7},{6,4},{7,5},{8,10},{9,11},{10,... | collective-permute-start | bytes 1572872 | tf_op jit(solution)/shard_map/ppermute | solution.py:37
  3.2 0.0 copy-start.1
  3.2 7.5 %front.1 = (bf16[128,2048]{1,0:T(8,128)(2,1)S(1)}, bf16[16,128,128]{2,1,0:T(8,128)(2,1)}) custom-call(s32[16]{0:T(128)} %map_hbm.1, bf16[128,2048]{1,0:T(8,128)(2,1)} %x0.1, bf16[128,2048]{1,0:T(8,128)(2,1)} %gh_hbm.1, bf16[2048,2048]{1,0:T(8,128)(2,1)} %w_hbm.1, f32[1,2048]{1,0:T(1,128)} %bitcast.77), custom_call_target="tpu_custom_call" | custom-call | tf_op jit(solution)/shard_map/front/pallas_call | solution.py:106
  10.8 0.1 collective-permute-start.2
  10.9 0.0 copy-done.1
  10.9 2.8 %collective-permute-start = (bf16[128,2048]{1,0:T(8,128)(2,1)S(1)}, bf16[128,2048]{1,0:T(8,128)(2,1)S(1)}, u32[]{:S(2)}, u32[]{:S(2)}) collective-permute-start(bf16[128,2048]{1,0:T(8,128)(2,1)S(1)} %copy-done.1), channel_id=1, source_target_pairs={{0,1},{1,0},{2,3},{3,2},{4,5},{5,4},{6,7},{7,6},{8,9},{9,8},{10,11... | collective-permute-start | bytes 1572872 | tf_op jit(solution)/shard_map/ppermute | solution.py:33
  13.7 5.0 %all-to-all-start.2 = ((bf16[16,128,128]{2,1,0:T(8,128)(2,1)}), bf16[16,128,128]{2,1,0:T(8,128)(2,1)S(1)}, u32[]{:S(2)}, u32[]{:S(2)}) async-start(bf16[16,128,128]{2,1,0:T(8,128)(2,1)} %get-tuple-element.9), calls=%async_computation.2 | async-start | bytes 1048576 | tf_op jit(solution)/shard_map/all_to_all | solution.py:216
  18.7 0.9 %collective-permute-done.2 = bf16[128,1024]{1,0:T(8,128)(2,1)S(1)} collective-permute-done((bf16[128,1024]{1,0:T(8,128)(2,1)S(1)}, bf16[128,1024]{1,0:T(8,128)(2,1)S(1)}, u32[]{:S(2)}, u32[]{:S(2)}) %collective-permute-start.2) | collective-permute-done | bytes 262176 | tf_op jit(solution)/shard_map/ppermute | solution.py:37
  19.6 0.0 collective-permute-done.1.x2
  19.7 2.4 %collective-permute-start.3 = (bf16[32,2048]{1,0:T(8,128)(2,1)S(1)}, bf16[32,2048]{1,0:T(8,128)(2,1)S(1)}, u32[]{:S(2)}, u32[]{:S(2)}) collective-permute-start(bf16[32,2048]{1,0:T(8,128)(2,1)S(1)} %get-tuple-element.19), channel_id=1, source_target_pairs={{0,1},{1,0},{2,3},{3,2},{4,5},{5,4},{6,7},{7,6},{8,9},{9,8},{10,11... | collective-permute-start | bytes 393224 | tf_op jit(solution)/shard_map/ppermute | solution.py:33
  22.0 0.1 collective-permute-start.4
  22.1 0.4 collective-permute-start.5
  22.5 0.1 collective-permute-start.6
  22.6 0.2 constant_dynamic-slice_fusion.4
  22.8 0.2 collective-permute-done.3
  23.0 0.4 collective-permute-start.7
  23.4 0.0 collective-permute-done.4
  23.4 0.2 collective-permute-start.8
  23.6 0.0 collective-permute-done.5
  23.6 0.3 collective-permute-done.6
  23.9 0.4 collective-permute-done.7.g1
  24.4 0.0 collective-permute-done.x1
  24.4 0.4 collective-permute-done.8.g3
  24.7 2.6 %weight_part.1 = bf16[2048,512]{1,0:T(8,128)(2,1)} custom-call(bf16[128,2048]{1,0:T(8,128)(2,1)S(1)} %copy-done.1, bf16[128,2048]{1,0:T(8,128)(2,1)S(1)} %collective-permute-done.x1, bf16[128,2048]{1,0:T(8,128)(2,1)S(1)} %collective-permute-done.1.x2, bf16[128,2048]{1,0:T(8,128)(2,1)S(1)} %pad_maximum_fusion.x3, bf16[128,512]{1,0:T(8,128)(2,1)S(1)} %get-tuple-element.18.g0, ...), custom_call_target="tpu_custom_call" | custom-call | tf_op jit(solution)/shard_map/weight_part/pallas_call | solution.py:139
  27.3 1.5 %all-to-all-done.2 = bf16[16,128,128]{2,1,0:T(8,128)(2,1)S(1)} async-done(((bf16[16,128,128]{2,1,0:T(8,128)(2,1)}), bf16[16,128,128]{2,1,0:T(8,128)(2,1)S(1)}, u32[]{:S(2)}, u32[]{:S(2)}) %all-to-all-start.2) | async-done | bytes 524320 | tf_op jit(solution)/shard_map/all_to_all | solution.py:216
  28.8 0.0 copy-start.2
  28.8 5.4 %all-to-all-start = ((bf16[16,128,512]{2,1,0:T(8,128)(2,1)}), bf16[16,128,512]{2,1,0:T(8,128)(2,1)}, u32[]{:S(2)}, u32[]{:S(2)}) async-start(bf16[16,128,512]{2,1,0:T(8,128)(2,1)} %bitcast.1), calls=%async_computation | async-start | bytes 4194304 | tf_op jit(solution)/shard_map/all_to_all | solution.py:219
  34.3 0.0 copy-done.2
  34.3 0.5 reshape_squeeze.7
  34.8 0.0 copy-done
  34.9 0.1 fusion.13
  35.1 1.7 %collective-permute-start.9 = (bf16[2048,128]{1,0:T(8,128)(2,1)S(1)}, bf16[2048,128]{1,0:T(8,128)(2,1)S(1)}, u32[]{:S(2)}, u32[]{:S(2)}) collective-permute-start(bf16[2048,128]{1,0:T(8,128)(2,1)S(1)} %bitcast.70), channel_id=1, source_target_pairs={{0,1},{1,0},{2,3},{3,2},{4,5},{5,4},{6,7},{7,6},{8,9},{9,8},{10,11... | collective-permute-start | bytes 1572872 | tf_op jit(solution)/shard_map/ppermute | solution.py:33
  37.0 1.4 %collective-permute-done.9.y_ref = bf16[2048,128]{1,0:T(8,128)(2,1)S(1)} collective-permute-done((bf16[2048,128]{1,0:T(8,128)(2,1)S(1)}, bf16[2048,128]{1,0:T(8,128)(2,1)S(1)}, u32[]{:S(2)}, u32[]{:S(2)}) %collective-permute-start.9) | collective-permute-done | bytes 524320 | tf_op jit(solution)/shard_map/ppermute | solution.py:33
  38.4 6.8 %table_partial.1 = bf16[2048,128]{1,0:T(8,128)(2,1)S(1)} custom-call(s32[4,4096]{1,0:T(4,128)S(1)} %pad_add_fusion.ids_ref, bf16[2048,128]{1,0:T(8,128)(2,1)S(1)} %bitcast.71, bf16[2048,128]{1,0:T(8,128)(2,1)S(1)} %collective-permute-done.9.y_ref), custom_call_target="tpu_custom_call" | custom-call | tf_op jit(solution)/shard_map/table_partial/pallas_call | solution.py:174
  45.2 7.0 %collective-permute-start.10 = (bf16[256,128]{1,0:T(8,128)(2,1)S(1)}, bf16[256,128]{1,0:T(8,128)(2,1)S(1)}, u32[]{:S(2)}, u32[]{:S(2)}) collective-permute-start(bf16[256,128]{1,0:T(8,128)(2,1)S(1)} %get-tuple-element.10), channel_id=1, source_target_pairs={{0,8},{1,9},{2,10},{3,11},{4,12},{5,13},{6,14},{7,15},{8,0},{9,1},... | collective-permute-start | bytes 196616 | tf_op jit(solution)/shard_map/ppermute | solution.py:41
  52.2 1.7 %collective-permute-start.11 = (bf16[256,128]{1,0:T(8,128)(2,1)S(1)}, bf16[256,128]{1,0:T(8,128)(2,1)S(1)}, u32[]{:S(2)}, u32[]{:S(2)}) collective-permute-start(bf16[256,128]{1,0:T(8,128)(2,1)S(1)} %get-tuple-element.16), channel_id=1, source_target_pairs={{0,6},{1,7},{2,8},{3,9},{4,10},{5,11},{6,12},{7,13},{8,14},{9,15},... | collective-permute-start | bytes 196616 | tf_op jit(solution)/shard_map/ppermute | solution.py:41
  53.9 2.8 %collective-permute-start.12 = (bf16[256,128]{1,0:T(8,128)(2,1)S(1)}, bf16[256,128]{1,0:T(8,128)(2,1)S(1)}, u32[]{:S(2)}, u32[]{:S(2)}) collective-permute-start(bf16[256,128]{1,0:T(8,128)(2,1)S(1)} %get-tuple-element.15), channel_id=1, source_target_pairs={{0,10},{1,11},{2,12},{3,13},{4,14},{5,15},{6,0},{7,1},{8,2},{9,3},... | collective-permute-start | bytes 196616 | tf_op jit(solution)/shard_map/ppermute | solution.py:41
  56.7 1.2 %collective-permute-start.13 = (bf16[256,128]{1,0:T(8,128)(2,1)S(1)}, bf16[256,128]{1,0:T(8,128)(2,1)S(1)}, u32[]{:S(2)}, u32[]{:S(2)}) collective-permute-start(bf16[256,128]{1,0:T(8,128)(2,1)S(1)} %get-tuple-element.14), channel_id=1, source_target_pairs={{0,4},{1,5},{2,6},{3,7},{4,8},{5,9},{6,10},{7,11},{8,12},{9,13},{1... | collective-permute-start | bytes 196616 | tf_op jit(solution)/shard_map/ppermute | solution.py:41
  57.9 2.4 %collective-permute-start.14 = (bf16[256,128]{1,0:T(8,128)(2,1)S(1)}, bf16[256,128]{1,0:T(8,128)(2,1)S(1)}, u32[]{:S(2)}, u32[]{:S(2)}) collective-permute-start(bf16[256,128]{1,0:T(8,128)(2,1)S(1)} %get-tuple-element.13), channel_id=1, source_target_pairs={{0,12},{1,13},{2,14},{3,15},{4,0},{5,1},{6,2},{7,3},{8,4},{9,5},{1... | collective-permute-start | bytes 196616 | tf_op jit(solution)/shard_map/ppermute | solution.py:41
  60.3 0.0 collective-permute-done.10
  60.3 0.7 collective-permute-start.15
  61.0 1.5 %collective-permute-done.11 = bf16[256,128]{1,0:T(8,128)(2,1)S(1)} collective-permute-done((bf16[256,128]{1,0:T(8,128)(2,1)S(1)}, bf16[256,128]{1,0:T(8,128)(2,1)S(1)}, u32[]{:S(2)}, u32[]{:S(2)}) %collective-permute-start.11) | collective-permute-done | bytes 65568 | tf_op jit(solution)/shard_map/ppermute | solution.py:41
  62.5 0.5 collective-permute-start.16
  63.0 0.0 all-to-all-done
  63.0 2.5 %fusion = bf16[16,8,512]{2,1,0:T(8,128)(2,1)} fusion(bf16[16,128,512]{2,1,0:T(8,128)(2,1)} %all-to-all-done), kind=kLoop, calls=%fused_computation.3 | loop fusion | flops 2097152 | bytes 2228224 | tf_op jit(solution)/shard_map/convert_element_type | solution.py:248
  65.5 10.4 %all-to-all-start.1 = ((bf16[16,8,512]{2,1,0:T(8,128)(2,1)}), bf16[16,8,512]{2,1,0:T(8,128)(2,1)S(1)}, u32[]{:S(2)}, u32[]{:S(2)}) async-start(bf16[16,8,512]{2,1,0:T(8,128)(2,1)} %fusion), calls=%async_computation.1 | async-start | bytes 262144 | tf_op jit(solution)/shard_map/all_to_all | solution.py:250
  75.9 0.0 collective-permute-done.12
  75.9 0.0 collective-permute-done.13
  75.9 0.0 collective-permute-done.14
  75.9 0.0 collective-permute-done.15
  75.9 0.0 collective-permute-done.16
  75.9 0.7 fusion.7
  76.7 8.4 %all-to-all-done.1 = bf16[16,8,512]{2,1,0:T(8,128)(2,1)S(1)} async-done(((bf16[16,8,512]{2,1,0:T(8,128)(2,1)}), bf16[16,8,512]{2,1,0:T(8,128)(2,1)S(1)}, u32[]{:S(2)}, u32[]{:S(2)}) %all-to-all-start.1) | async-done | bytes 131104 | tf_op jit(solution)/shard_map/all_to_all | solution.py:250
  85.1 0.6 convert_reduce_fusion
  (11 shorter events, 0.3 us)
Async XLA Ops:
  0.6 34.2 %copy-start = (s32[1,32768]{1,0:T(1,128)S(1)}, s32[1,32768]{1,0:T(1,128)}, u32[]{:S(2)}) copy-start(s32[1,32768]{1,0:T(1,128)} %param.13) | copy-start | bytes 393220
  0.6 19.0 %collective-permute-start.1 = (bf16[128,2048]{1,0:T(8,128)(2,1)}, bf16[128,2048]{1,0:T(8,128)(2,1)S(1)}, u32[]{:S(2)}, u32[]{:S(2)}) collective-permute-start(bf16[128,2048]{1,0:T(8,128)(2,1)} %x0.1), channel_id=1, source_target_pairs={{0,2},{1,3},{2,0},{3,1},{4,6},{5,7},{6,4},{7,5},{8,10},{9,11},{10,... | collective-permute-start | bytes 1572872 | tf_op jit(solution)/shard_map/ppermute | solution.py:37
  3.2 7.7 %copy-start.1 = (bf16[128,2048]{1,0:T(8,128)(2,1)S(1)}, bf16[128,2048]{1,0:T(8,128)(2,1)}, u32[]{:S(2)}) copy-start(bf16[128,2048]{1,0:T(8,128)(2,1)} %x0.1) | copy-start | bytes 1572868
  10.8 8.8 %collective-permute-start.2 = (bf16[128,1024]{1,0:T(8,128)(2,1)S(1)}, bf16[128,1024]{1,0:T(8,128)(2,1)S(1)}, u32[]{:S(2)}, u32[]{:S(2)}) collective-permute-start(bf16[128,1024]{1,0:T(8,128)(2,1)S(1)} %constant_dynamic-slice_fusion.6), channel_id=1, source_target_pairs={{0,2},{1,3},{2,0},{3,1},{4,6},{5,7},{6,4},{7,5},{8,10},{9,11},{10,... | collective-permute-start | bytes 786440 | tf_op jit(solution)/shard_map/ppermute | solution.py:37
  10.9 13.5 %collective-permute-start = (bf16[128,2048]{1,0:T(8,128)(2,1)S(1)}, bf16[128,2048]{1,0:T(8,128)(2,1)S(1)}, u32[]{:S(2)}, u32[]{:S(2)}) collective-permute-start(bf16[128,2048]{1,0:T(8,128)(2,1)S(1)} %copy-done.1), channel_id=1, source_target_pairs={{0,1},{1,0},{2,3},{3,2},{4,5},{5,4},{6,7},{7,6},{8,9},{9,8},{10,11... | collective-permute-start | bytes 1572872 | tf_op jit(solution)/shard_map/ppermute | solution.py:33
  13.7 15.2 %all-to-all-start.2 = ((bf16[16,128,128]{2,1,0:T(8,128)(2,1)}), bf16[16,128,128]{2,1,0:T(8,128)(2,1)S(1)}, u32[]{:S(2)}, u32[]{:S(2)}) async-start(bf16[16,128,128]{2,1,0:T(8,128)(2,1)} %get-tuple-element.9), calls=%async_computation.2 | async-start | bytes 1048576 | tf_op jit(solution)/shard_map/all_to_all | solution.py:216
  19.7 3.4 %collective-permute-start.3 = (bf16[32,2048]{1,0:T(8,128)(2,1)S(1)}, bf16[32,2048]{1,0:T(8,128)(2,1)S(1)}, u32[]{:S(2)}, u32[]{:S(2)}) collective-permute-start(bf16[32,2048]{1,0:T(8,128)(2,1)S(1)} %get-tuple-element.19), channel_id=1, source_target_pairs={{0,1},{1,0},{2,3},{3,2},{4,5},{5,4},{6,7},{7,6},{8,9},{9,8},{10,11... | collective-permute-start | bytes 393224 | tf_op jit(solution)/shard_map/ppermute | solution.py:33
  22.0 1.4 %collective-permute-start.4 = (bf16[32,2048]{1,0:T(8,128)(2,1)S(1)}, bf16[32,2048]{1,0:T(8,128)(2,1)S(1)}, u32[]{:S(2)}, u32[]{:S(2)}) collective-permute-start(bf16[32,2048]{1,0:T(8,128)(2,1)S(1)} %get-tuple-element.22), channel_id=1, source_target_pairs={{0,1},{1,0},{2,3},{3,2},{4,5},{5,4},{6,7},{7,6},{8,9},{9,8},{10,11... | collective-permute-start | bytes 393224 | tf_op jit(solution)/shard_map/ppermute | solution.py:33
  22.1 1.4 %collective-permute-start.5 = (bf16[32,2048]{1,0:T(8,128)(2,1)S(1)}, bf16[32,2048]{1,0:T(8,128)(2,1)S(1)}, u32[]{:S(2)}, u32[]{:S(2)}) collective-permute-start(bf16[32,2048]{1,0:T(8,128)(2,1)S(1)} %get-tuple-element.21), channel_id=1, source_target_pairs={{0,1},{1,0},{2,3},{3,2},{4,5},{5,4},{6,7},{7,6},{8,9},{9,8},{10,11... | collective-permute-start | bytes 393224 | tf_op jit(solution)/shard_map/ppermute | solution.py:33
  22.5 1.3 %collective-permute-start.6 = (bf16[32,2048]{1,0:T(8,128)(2,1)S(1)}, bf16[32,2048]{1,0:T(8,128)(2,1)S(1)}, u32[]{:S(2)}, u32[]{:S(2)}) collective-permute-start(bf16[32,2048]{1,0:T(8,128)(2,1)S(1)} %get-tuple-element.20), channel_id=1, source_target_pairs={{0,1},{1,0},{2,3},{3,2},{4,5},{5,4},{6,7},{7,6},{8,9},{9,8},{10,11... | collective-permute-start | bytes 393224 | tf_op jit(solution)/shard_map/ppermute | solution.py:33
  23.0 1.3 %collective-permute-start.7 = (bf16[128,512]{1,0:T(8,128)(2,1)S(1)}, bf16[128,512]{1,0:T(8,128)(2,1)S(1)}, u32[]{:S(2)}, u32[]{:S(2)}) collective-permute-start(bf16[128,512]{1,0:T(8,128)(2,1)S(1)} %get-tuple-element.17), channel_id=1, source_target_pairs={{0,1},{1,0},{2,3},{3,2},{4,5},{5,4},{6,7},{7,6},{8,9},{9,8},{10,11... | collective-permute-start | bytes 393224 | tf_op jit(solution)/shard_map/ppermute | solution.py:33
  23.4 1.3 %collective-permute-start.8 = (bf16[128,512]{1,0:T(8,128)(2,1)S(1)}, bf16[128,512]{1,0:T(8,128)(2,1)S(1)}, u32[]{:S(2)}, u32[]{:S(2)}) collective-permute-start(bf16[128,512]{1,0:T(8,128)(2,1)S(1)} %get-tuple-element.23), channel_id=1, source_target_pairs={{0,1},{1,0},{2,3},{3,2},{4,5},{5,4},{6,7},{7,6},{8,9},{9,8},{10,11... | collective-permute-start | bytes 393224 | tf_op jit(solution)/shard_map/ppermute | solution.py:33
  28.8 5.5 %copy-start.2 = (s32[1,4,32768]{2,1,0:T(4,128)S(1)}, s32[1,4,32768]{2,1,0:T(4,128)}, u32[]{:S(2)}) copy-start(s32[1,4,32768]{2,1,0:T(4,128)} %param.12) | copy-start | bytes 1572868
  28.8 34.1 %all-to-all-start = ((bf16[16,128,512]{2,1,0:T(8,128)(2,1)}), bf16[16,128,512]{2,1,0:T(8,128)(2,1)}, u32[]{:S(2)}, u32[]{:S(2)}) async-start(bf16[16,128,512]{2,1,0:T(8,128)(2,1)} %bitcast.1), calls=%async_computation | async-start | bytes 4194304 | tf_op jit(solution)/shard_map/all_to_all | solution.py:219
  35.1 3.3 %collective-permute-start.9 = (bf16[2048,128]{1,0:T(8,128)(2,1)S(1)}, bf16[2048,128]{1,0:T(8,128)(2,1)S(1)}, u32[]{:S(2)}, u32[]{:S(2)}) collective-permute-start(bf16[2048,128]{1,0:T(8,128)(2,1)S(1)} %bitcast.70), channel_id=1, source_target_pairs={{0,1},{1,0},{2,3},{3,2},{4,5},{5,4},{6,7},{7,6},{8,9},{9,8},{10,11... | collective-permute-start | bytes 1572872 | tf_op jit(solution)/shard_map/ppermute | solution.py:33
  45.2 15.0 %collective-permute-start.10 = (bf16[256,128]{1,0:T(8,128)(2,1)S(1)}, bf16[256,128]{1,0:T(8,128)(2,1)S(1)}, u32[]{:S(2)}, u32[]{:S(2)}) collective-permute-start(bf16[256,128]{1,0:T(8,128)(2,1)S(1)} %get-tuple-element.10), channel_id=1, source_target_pairs={{0,8},{1,9},{2,10},{3,11},{4,12},{5,13},{6,14},{7,15},{8,0},{9,1},... | collective-permute-start | bytes 196616 | tf_op jit(solution)/shard_map/ppermute | solution.py:41
  52.2 10.3 %collective-permute-start.11 = (bf16[256,128]{1,0:T(8,128)(2,1)S(1)}, bf16[256,128]{1,0:T(8,128)(2,1)S(1)}, u32[]{:S(2)}, u32[]{:S(2)}) collective-permute-start(bf16[256,128]{1,0:T(8,128)(2,1)S(1)} %get-tuple-element.16), channel_id=1, source_target_pairs={{0,6},{1,7},{2,8},{3,9},{4,10},{5,11},{6,12},{7,13},{8,14},{9,15},... | collective-permute-start | bytes 196616 | tf_op jit(solution)/shard_map/ppermute | solution.py:41
  53.9 22.0 %collective-permute-start.12 = (bf16[256,128]{1,0:T(8,128)(2,1)S(1)}, bf16[256,128]{1,0:T(8,128)(2,1)S(1)}, u32[]{:S(2)}, u32[]{:S(2)}) collective-permute-start(bf16[256,128]{1,0:T(8,128)(2,1)S(1)} %get-tuple-element.15), channel_id=1, source_target_pairs={{0,10},{1,11},{2,12},{3,13},{4,14},{5,15},{6,0},{7,1},{8,2},{9,3},... | collective-permute-start | bytes 196616 | tf_op jit(solution)/shard_map/ppermute | solution.py:41
  56.7 19.2 %collective-permute-start.13 = (bf16[256,128]{1,0:T(8,128)(2,1)S(1)}, bf16[256,128]{1,0:T(8,128)(2,1)S(1)}, u32[]{:S(2)}, u32[]{:S(2)}) collective-permute-start(bf16[256,128]{1,0:T(8,128)(2,1)S(1)} %get-tuple-element.14), channel_id=1, source_target_pairs={{0,4},{1,5},{2,6},{3,7},{4,8},{5,9},{6,10},{7,11},{8,12},{9,13},{1... | collective-permute-start | bytes 196616 | tf_op jit(solution)/shard_map/ppermute | solution.py:41
  57.9 18.0 %collective-permute-start.14 = (bf16[256,128]{1,0:T(8,128)(2,1)S(1)}, bf16[256,128]{1,0:T(8,128)(2,1)S(1)}, u32[]{:S(2)}, u32[]{:S(2)}) collective-permute-start(bf16[256,128]{1,0:T(8,128)(2,1)S(1)} %get-tuple-element.13), channel_id=1, source_target_pairs={{0,12},{1,13},{2,14},{3,15},{4,0},{5,1},{6,2},{7,3},{8,4},{9,5},{1... | collective-permute-start | bytes 196616 | tf_op jit(solution)/shard_map/ppermute | solution.py:41
  60.3 15.6 %collective-permute-start.15 = (bf16[256,128]{1,0:T(8,128)(2,1)S(1)}, bf16[256,128]{1,0:T(8,128)(2,1)S(1)}, u32[]{:S(2)}, u32[]{:S(2)}) collective-permute-start(bf16[256,128]{1,0:T(8,128)(2,1)S(1)} %get-tuple-element.12), channel_id=1, source_target_pairs={{0,2},{1,3},{2,4},{3,5},{4,6},{5,7},{6,8},{7,9},{8,10},{9,11},{10,... | collective-permute-start | bytes 196616 | tf_op jit(solution)/shard_map/ppermute | solution.py:41
  62.5 13.4 %collective-permute-start.16 = (bf16[256,128]{1,0:T(8,128)(2,1)S(1)}, bf16[256,128]{1,0:T(8,128)(2,1)S(1)}, u32[]{:S(2)}, u32[]{:S(2)}) collective-permute-start(bf16[256,128]{1,0:T(8,128)(2,1)S(1)} %get-tuple-element.11), channel_id=1, source_target_pairs={{0,14},{1,15},{2,0},{3,1},{4,2},{5,3},{6,4},{7,5},{8,6},{9,7},{10,... | collective-permute-start | bytes 196616 | tf_op jit(solution)/shard_map/ppermute | solution.py:41
  65.5 19.6 %all-to-all-start.1 = ((bf16[16,8,512]{2,1,0:T(8,128)(2,1)}), bf16[16,8,512]{2,1,0:T(8,128)(2,1)S(1)}, u32[]{:S(2)}, u32[]{:S(2)}) async-start(bf16[16,8,512]{2,1,0:T(8,128)(2,1)} %fusion), calls=%async_computation.1 | async-start | bytes 262144 | tf_op jit(solution)/shard_map/all_to_all | solution.py:250

commit v4 on v3

--- a/solution.py
+++ b/solution.py
@@ -120,7 +120,7 @@
             pltpu.VMEM((b_dev, width), jnp.float32),
             pltpu.SemaphoreType.DMA((4 + blocks,)),
         ],
-        compiler_params=params(40),
+        compiler_params=params(20),
         name="front",
     )(*[in_hbm(v) for v in (slice_map, top_input, grad_hidden, w_in, b_in[None])])
 
@@ -141,12 +141,38 @@
         out_shape=jax.ShapeDtypeStruct((tops[0].shape[1], grads[0].shape[1]), jnp.bfloat16),
         in_specs=[VMEM] * 8,
         out_specs=VMEM,
-        compiler_params=params(32),
+        compiler_params=params(16),
         name="weight_part",
     )(*tops, *grads)
 
 
-def table_kernel(chunk, rb, ids_ref, x_ref, y_ref, o_ref):
+def sum_kernel(x_ref, o_ref):
+    total = f32(x_ref[0])
+    for k in range(1, x_ref.shape[0]):
+        total = total + f32(x_ref[k])
+    o_ref[...] = total.astype(o_ref.dtype)
+
+
+def sum_blocks(blocks):
+    return pl.pallas_call(
+        sum_kernel,
+        out_shape=jax.ShapeDtypeStruct(blocks.shape[1:], blocks.dtype),
+        in_specs=[VMEM],
+        out_specs=VMEM,
+        compiler_params=params(8),
+        name="sum_blocks",
+    )(blocks)
+
+
+def table_kernel(chunk, rb, ids_ref, x_hbm, y_hbm, o_ref, x_ref, y_ref, sems):
+    copies = [
+        pltpu.make_async_copy(x_hbm, x_ref, sems.at[0]),
+        pltpu.make_async_copy(y_hbm, y_ref, sems.at[1]),
+    ]
+    for copy in copies:
+        copy.start()
+    for copy in copies:
+        copy.wait()
     samples = x_ref.shape[0]
     one = jnp.ones((), jnp.bfloat16)
     zero = jnp.zeros((), jnp.bfloat16)
@@ -174,11 +200,16 @@
     return pl.pallas_call(
         functools.partial(table_kernel, 256, 512),
         out_shape=jax.ShapeDtypeStruct((LOCAL_ROWS, x.shape[1]), jnp.bfloat16),
-        in_specs=[VMEM] * 3,
+        in_specs=[VMEM, HBM, HBM],
         out_specs=VMEM,
-        compiler_params=params(32),
+        scratch_shapes=[
+            pltpu.VMEM(x.shape, jnp.bfloat16),
+            pltpu.VMEM(y.shape, jnp.bfloat16),
+            pltpu.SemaphoreType.DMA((2,)),
+        ],
+        compiler_params=params(16),
         name="table_partial",
-    )(ids, x, y)
+    )(ids, in_hbm(x), in_hbm(y))
 
 
 def body(top_input, grad_hidden, w_in, b_in, slice_map, lookup_ids, bag_len):
@@ -242,10 +273,7 @@
     for d in (4, 3, 5, 2, 6, 1, 7):
         table_grad = table_grad + f32(z_shift(rows_of(d), d))
 
-    summed = f32(blocks[0])
-    for h in range(1, NX * NY):
-        summed = summed + f32(blocks[h])
-    summed = summed.astype(jnp.bfloat16)
+    summed = sum_blocks(blocks)
     rows_out = summed.shape[0] // (NZ * NC)
     swapped = lax.all_to_all(
         summed.reshape(NZ * NC, rows_out, quart), "chip", split_axis=0, concat_axis=0, tiled=True

time: 86.1 us -> 85 us (0.987)
  other arithmetic: 4.07 us -> 1.55 us
  Pallas kernels: 17 us -> 19.2 us
  starting transfers between devices: 47.8 us -> 46 us
  local copies, waits for them, and re-layouts: 0.93 us -> 1.98 us
    convert_element_type x1 -> x0, other arithmetic: 2.52 us -> none  [body(): summed = summed.astype(jnp.bfloat16)]
    pallas_call x1, Pallas kernels: 6.83 us -> 8.04 us  [table_partial(): pl.pallas_call(functools.partial(table_kernel, 256, 512), out_shape=jax.S...]
    another operation x1, local copies, waits for them, and re-layouts: 0.53 us -> 1.57 us  [body(): ids = lookup_ids[0].reshape(slots, NX * NY, NZ, NC, b_dev)]
    all_to_all x1, starting transfers between devices: 10.4 us -> 9.41 us  [body(): lax.all_to_all(summed.reshape(NZ * NC, rows_out, quart), 'chip', split_ax...]
    pallas_call x0 -> x1, Pallas kernels: none -> 0.92 us  [sum_blocks(): pl.pallas_call(sum_kernel, out_shape=jax.ShapeDtypeStruct(blocks.shape[1:...]
  transfers between devices with their start and end apart: 20 -> 20, of which waited for: 9 -> 9; matrix products, arithmetic and copies ran while one was open for 5% -> 3% of each run, Pallas kernels for 20% -> 23%
where the time goes in v4:
time: 85 us; the launch traced here: 84.6 us
  starting transfers between devices  46 us (54%)
  Pallas kernels  19.2 us (23%)
  waiting for transfers between devices  14.9 us (18%)
  local copies, waits for them, and re-layouts  1.98 us (2%)
  other arithmetic  1.55 us (2%)
  between operations  0.99 us (1%)
    ppermute x7, starting transfers between devices, z_shift(): lax.ppermute(value, AXES, permutation(lambda x, y, z, c: (x, y, (z + d) %...  16.3 us
    all_to_all x1, starting transfers between devices, body(): lax.all_to_all(summed.reshape(NZ * NC, rows_out, quart), 'chip', split_ax...  9.41 us
    all_to_all x1, waiting for transfers between devices, body(): lax.all_to_all(summed.reshape(NZ * NC, rows_out, quart), 'chip', split_ax...  8.39 us
    pallas_call x1, Pallas kernels, table_partial(): pl.pallas_call(functools.partial(table_kernel, 256, 512), out_shape=jax.S...  8.04 us
    pallas_call x1, Pallas kernels, front(): pl.pallas_call(front_kernel, in_specs=[HBM] * 5, out_specs=[VMEM] * 2, ou...  7.54 us
    ppermute x8, starting transfers between devices, core_swap(): lax.ppermute(value, AXES, permutation(lambda x, y, z, c: (x, y, z, 1 - c)))  7.27 us
    all_to_all x1, starting transfers between devices, body(): lax.all_to_all(part.reshape(NX * NY, width // (NX * NY), quart), 'hst', s...  5.31 us
    all_to_all x1, starting transfers between devices, body(): lax.all_to_all(ordered, 'hst', split_axis=0, concat_axis=1, tiled=True)[0]  5.01 us
  transfers between devices with their start and end apart: 20, of which 9 were waited for; matrix products, arithmetic and copies ran while one was open for 3% of the time, Pallas kernels for 23%

profile of v4, /device:TPU:1, one launch (start us, length us, event | category | flops | bytes accessed | tf_op | source)
XLA Modules:
  0.0 84.6 jit_solution(6124156625043333384)
XLA Ops:
  0.6 0.0 copy-start
  0.6 2.6 %collective-permute-start.1 = (bf16[128,2048]{1,0:T(8,128)(2,1)}, bf16[128,2048]{1,0:T(8,128)(2,1)S(1)}, u32[]{:S(2)}, u32[]{:S(2)}) collective-permute-start(bf16[128,2048]{1,0:T(8,128)(2,1)} %x0.1), channel_id=1, source_target_pairs={{0,2},{1,3},{2,0},{3,1},{4,6},{5,7},{6,4},{7,5},{8,10},{9,11},{10,... | collective-permute-start | bytes 1572872 | tf_op jit(solution)/shard_map/ppermute | solution.py:37
  3.2 0.0 copy-start.1
  3.2 7.5 %front.1 = (bf16[128,2048]{1,0:T(8,128)(2,1)S(1)}, bf16[16,128,128]{2,1,0:T(8,128)(2,1)}) custom-call(s32[16]{0:T(128)} %map_hbm.1, bf16[128,2048]{1,0:T(8,128)(2,1)} %x0.1, bf16[128,2048]{1,0:T(8,128)(2,1)} %gh_hbm.1, bf16[2048,2048]{1,0:T(8,128)(2,1)} %w_hbm.1, f32[1,2048]{1,0:T(1,128)} %bitcast.71), custom_call_target="tpu_custom_call" | custom-call | tf_op jit(solution)/shard_map/front/pallas_call | solution.py:106
  10.8 0.1 collective-permute-start.2
  10.9 0.0 copy-done.1
  10.9 2.8 %collective-permute-start = (bf16[128,2048]{1,0:T(8,128)(2,1)S(1)}, bf16[128,2048]{1,0:T(8,128)(2,1)S(1)}, u32[]{:S(2)}, u32[]{:S(2)}) collective-permute-start(bf16[128,2048]{1,0:T(8,128)(2,1)S(1)} %copy-done.1), channel_id=1, source_target_pairs={{0,1},{1,0},{2,3},{3,2},{4,5},{5,4},{6,7},{7,6},{8,9},{9,8},{10,11... | collective-permute-start | bytes 1572872 | tf_op jit(solution)/shard_map/ppermute | solution.py:33
  13.7 5.0 %all-to-all-start.2 = ((bf16[16,128,128]{2,1,0:T(8,128)(2,1)}), bf16[16,128,128]{2,1,0:T(8,128)(2,1)S(1)}, u32[]{:S(2)}, u32[]{:S(2)}) async-start(bf16[16,128,128]{2,1,0:T(8,128)(2,1)} %get-tuple-element.9), calls=%async_computation.2 | async-start | bytes 1048576 | tf_op jit(solution)/shard_map/all_to_all | solution.py:247
  18.7 0.9 %collective-permute-done.2 = bf16[128,1024]{1,0:T(8,128)(2,1)S(1)} collective-permute-done((bf16[128,1024]{1,0:T(8,128)(2,1)S(1)}, bf16[128,1024]{1,0:T(8,128)(2,1)S(1)}, u32[]{:S(2)}, u32[]{:S(2)}) %collective-permute-start.2) | collective-permute-done | bytes 262176 | tf_op jit(solution)/shard_map/ppermute | solution.py:37
  19.6 0.0 collective-permute-done.1.x2
  19.7 2.4 %collective-permute-start.3 = (bf16[32,2048]{1,0:T(8,128)(2,1)S(1)}, bf16[32,2048]{1,0:T(8,128)(2,1)S(1)}, u32[]{:S(2)}, u32[]{:S(2)}) collective-permute-start(bf16[32,2048]{1,0:T(8,128)(2,1)S(1)} %get-tuple-element.19), channel_id=1, source_target_pairs={{0,1},{1,0},{2,3},{3,2},{4,5},{5,4},{6,7},{7,6},{8,9},{9,8},{10,11... | collective-permute-start | bytes 393224 | tf_op jit(solution)/shard_map/ppermute | solution.py:33
  22.0 0.1 collective-permute-start.4
  22.1 0.4 collective-permute-start.5
  22.6 0.1 collective-permute-start.6
  22.7 0.2 constant_dynamic-slice_fusion.4
  22.9 0.2 collective-permute-done.3
  23.0 0.4 collective-permute-start.7
  23.4 0.0 collective-permute-done.4
  23.4 0.2 collective-permute-start.8
  23.6 0.0 collective-permute-done.5
  23.6 0.3 collective-permute-done.6
  24.0 0.4 collective-permute-done.7.g1
  24.4 0.0 collective-permute-done.x1
  24.4 0.4 collective-permute-done.8.g3
  24.7 2.6 %weight_part.1 = bf16[2048,512]{1,0:T(8,128)(2,1)} custom-call(bf16[128,2048]{1,0:T(8,128)(2,1)S(1)} %copy-done.1, bf16[128,2048]{1,0:T(8,128)(2,1)S(1)} %collective-permute-done.x1, bf16[128,2048]{1,0:T(8,128)(2,1)S(1)} %collective-permute-done.1.x2, bf16[128,2048]{1,0:T(8,128)(2,1)S(1)} %pad_maximum_fusion.x3, bf16[128,512]{1,0:T(8,128)(2,1)S(1)} %get-tuple-element.18.g0, ...), custom_call_target="tpu_custom_call" | custom-call | tf_op jit(solution)/shard_map/weight_part/pallas_call | solution.py:139
  27.4 1.4 %all-to-all-done.2 = bf16[16,128,128]{2,1,0:T(8,128)(2,1)S(1)} async-done(((bf16[16,128,128]{2,1,0:T(8,128)(2,1)}), bf16[16,128,128]{2,1,0:T(8,128)(2,1)S(1)}, u32[]{:S(2)}, u32[]{:S(2)}) %all-to-all-start.2) | async-done | bytes 524320 | tf_op jit(solution)/shard_map/all_to_all | solution.py:247
  28.8 0.0 copy-start.2
  28.8 5.3 %all-to-all-start = ((bf16[16,128,512]{2,1,0:T(8,128)(2,1)}), bf16[16,128,512]{2,1,0:T(8,128)(2,1)S(1)}, u32[]{:S(2)}, u32[]{:S(2)}) async-start(bf16[16,128,512]{2,1,0:T(8,128)(2,1)} %bitcast.1), calls=%async_computation | async-start | bytes 4194304 | tf_op jit(solution)/shard_map/all_to_all | solution.py:250
  34.2 1.6 %reshape_squeeze.7 = s32[4,16,8,2,128]{4,3,2,1,0:T(2,128)S(1)} reshape(s32[1,4,32768]{2,1,0:T(4,128)} %param.12) | data formatting | bytes 1048576 | tf_op jit(solution)/shard_map/reshape;squeeze | solution.py:255
  35.8 0.0 copy-done
  35.8 0.1 fusion.12
  36.0 0.0 copy-done.2
  36.0 1.0 %collective-permute-start.9 = (bf16[2048,128]{1,0:T(8,128)(2,1)S(1)}, bf16[2048,128]{1,0:T(8,128)(2,1)}, u32[]{:S(2)}, u32[]{:S(2)}) collective-permute-start(bf16[2048,128]{1,0:T(8,128)(2,1)S(1)} %bitcast.66), channel_id=1, source_target_pairs={{0,1},{1,0},{2,3},{3,2},{4,5},{5,4},{6,7},{7,6},{8,9},{9,8},{10,11... | collective-permute-start | bytes 1572872 | tf_op jit(solution)/shard_map/ppermute | solution.py:33
  37.1 1.5 %collective-permute-done.9.y_hbm = bf16[2048,128]{1,0:T(8,128)(2,1)} collective-permute-done((bf16[2048,128]{1,0:T(8,128)(2,1)S(1)}, bf16[2048,128]{1,0:T(8,128)(2,1)}, u32[]{:S(2)}, u32[]{:S(2)}) %collective-permute-start.9) | collective-permute-done | bytes 524320 | tf_op jit(solution)/shard_map/ppermute | solution.py:33
  38.7 8.0 %table_partial.1 = bf16[2048,128]{1,0:T(8,128)(2,1)S(1)} custom-call(s32[4,4096]{1,0:T(4,128)S(1)} %pad_add_fusion.ids_ref, bf16[2048,128]{1,0:T(8,128)(2,1)} %bitcast.67, bf16[2048,128]{1,0:T(8,128)(2,1)} %collective-permute-done.9.y_hbm), custom_call_target="tpu_custom_call" | custom-call | tf_op jit(solution)/shard_map/table_partial/pallas_call | solution.py:200
  46.8 7.0 %collective-permute-start.10 = (bf16[256,128]{1,0:T(8,128)(2,1)S(1)}, bf16[256,128]{1,0:T(8,128)(2,1)S(1)}, u32[]{:S(2)}, u32[]{:S(2)}) collective-permute-start(bf16[256,128]{1,0:T(8,128)(2,1)S(1)} %get-tuple-element.10), channel_id=1, source_target_pairs={{0,8},{1,9},{2,10},{3,11},{4,12},{5,13},{6,14},{7,15},{8,0},{9,1},... | collective-permute-start | bytes 196616 | tf_op jit(solution)/shard_map/ppermute | solution.py:41
  53.8 1.7 %collective-permute-start.11 = (bf16[256,128]{1,0:T(8,128)(2,1)S(1)}, bf16[256,128]{1,0:T(8,128)(2,1)S(1)}, u32[]{:S(2)}, u32[]{:S(2)}) collective-permute-start(bf16[256,128]{1,0:T(8,128)(2,1)S(1)} %get-tuple-element.16), channel_id=1, source_target_pairs={{0,6},{1,7},{2,8},{3,9},{4,10},{5,11},{6,12},{7,13},{8,14},{9,15},... | collective-permute-start | bytes 196616 | tf_op jit(solution)/shard_map/ppermute | solution.py:41
  55.4 2.8 %collective-permute-start.12 = (bf16[256,128]{1,0:T(8,128)(2,1)S(1)}, bf16[256,128]{1,0:T(8,128)(2,1)S(1)}, u32[]{:S(2)}, u32[]{:S(2)}) collective-permute-start(bf16[256,128]{1,0:T(8,128)(2,1)S(1)} %get-tuple-element.15), channel_id=1, source_target_pairs={{0,10},{1,11},{2,12},{3,13},{4,14},{5,15},{6,0},{7,1},{8,2},{9,3},... | collective-permute-start | bytes 196616 | tf_op jit(solution)/shard_map/ppermute | solution.py:41
  58.2 1.2 %collective-permute-start.13 = (bf16[256,128]{1,0:T(8,128)(2,1)S(1)}, bf16[256,128]{1,0:T(8,128)(2,1)S(1)}, u32[]{:S(2)}, u32[]{:S(2)}) collective-permute-start(bf16[256,128]{1,0:T(8,128)(2,1)S(1)} %get-tuple-element.14), channel_id=1, source_target_pairs={{0,4},{1,5},{2,6},{3,7},{4,8},{5,9},{6,10},{7,11},{8,12},{9,13},{1... | collective-permute-start | bytes 196616 | tf_op jit(solution)/shard_map/ppermute | solution.py:41
  59.4 2.4 %collective-permute-start.14 = (bf16[256,128]{1,0:T(8,128)(2,1)S(1)}, bf16[256,128]{1,0:T(8,128)(2,1)S(1)}, u32[]{:S(2)}, u32[]{:S(2)}) collective-permute-start(bf16[256,128]{1,0:T(8,128)(2,1)S(1)} %get-tuple-element.13), channel_id=1, source_target_pairs={{0,12},{1,13},{2,14},{3,15},{4,0},{5,1},{6,2},{7,3},{8,4},{9,5},{1... | collective-permute-start | bytes 196616 | tf_op jit(solution)/shard_map/ppermute | solution.py:41
  61.8 0.0 collective-permute-done.10
  61.8 0.7 collective-permute-start.15
  62.5 1.4 %collective-permute-done.11 = bf16[256,128]{1,0:T(8,128)(2,1)S(1)} collective-permute-done((bf16[256,128]{1,0:T(8,128)(2,1)S(1)}, bf16[256,128]{1,0:T(8,128)(2,1)S(1)}, u32[]{:S(2)}, u32[]{:S(2)}) %collective-permute-start.11) | collective-permute-done | bytes 65568 | tf_op jit(solution)/shard_map/ppermute | solution.py:41
  63.9 0.6 collective-permute-start.16
  64.5 0.0 all-to-all-done.x_ref
  64.5 0.9 %sum_blocks.1 = bf16[128,512]{1,0:T(8,128)(2,1)} custom-call(bf16[16,128,512]{2,1,0:T(8,128)(2,1)S(1)} %all-to-all-done.x_ref), custom_call_target="tpu_custom_call" | custom-call | tf_op jit(solution)/shard_map/sum_blocks/pallas_call | solution.py:157
  65.4 9.4 %all-to-all-start.1 = ((bf16[16,8,512]{2,1,0:T(8,128)(2,1)}), bf16[16,8,512]{2,1,0:T(8,128)(2,1)S(1)}, u32[]{:S(2)}, u32[]{:S(2)}) async-start(bf16[16,8,512]{2,1,0:T(8,128)(2,1)} %bitcast.2), calls=%async_computation.1 | async-start | bytes 262144 | tf_op jit(solution)/shard_map/all_to_all | solution.py:278
  74.8 0.0 collective-permute-done.12
  74.8 0.0 collective-permute-done.13
  74.8 0.0 collective-permute-done.14
  74.9 0.0 collective-permute-done.15
  74.9 0.0 collective-permute-done.16
  74.9 0.7 fusion.6
  75.6 8.4 %all-to-all-done.1 = bf16[16,8,512]{2,1,0:T(8,128)(2,1)S(1)} async-done(((bf16[16,8,512]{2,1,0:T(8,128)(2,1)}), bf16[16,8,512]{2,1,0:T(8,128)(2,1)S(1)}, u32[]{:S(2)}, u32[]{:S(2)}) %all-to-all-start.1) | async-done | bytes 131104 | tf_op jit(solution)/shard_map/all_to_all | solution.py:278
  84.0 0.6 convert_reduce_fusion
  (11 shorter events, 0.3 us)
Async XLA Ops:
  0.6 35.1 %copy-start = (s32[1,32768]{1,0:T(1,128)S(1)}, s32[1,32768]{1,0:T(1,128)}, u32[]{:S(2)}) copy-start(s32[1,32768]{1,0:T(1,128)} %param.13) | copy-start | bytes 393220
  0.6 19.0 %collective-permute-start.1 = (bf16[128,2048]{1,0:T(8,128)(2,1)}, bf16[128,2048]{1,0:T(8,128)(2,1)S(1)}, u32[]{:S(2)}, u32[]{:S(2)}) collective-permute-start(bf16[128,2048]{1,0:T(8,128)(2,1)} %x0.1), channel_id=1, source_target_pairs={{0,2},{1,3},{2,0},{3,1},{4,6},{5,7},{6,4},{7,5},{8,10},{9,11},{10,... | collective-permute-start | bytes 1572872 | tf_op jit(solution)/shard_map/ppermute | solution.py:37
  3.2 7.7 %copy-start.1 = (bf16[128,2048]{1,0:T(8,128)(2,1)S(1)}, bf16[128,2048]{1,0:T(8,128)(2,1)}, u32[]{:S(2)}) copy-start(bf16[128,2048]{1,0:T(8,128)(2,1)} %x0.1) | copy-start | bytes 1572868
  10.8 8.8 %collective-permute-start.2 = (bf16[128,1024]{1,0:T(8,128)(2,1)S(1)}, bf16[128,1024]{1,0:T(8,128)(2,1)S(1)}, u32[]{:S(2)}, u32[]{:S(2)}) collective-permute-start(bf16[128,1024]{1,0:T(8,128)(2,1)S(1)} %constant_dynamic-slice_fusion.6), channel_id=1, source_target_pairs={{0,2},{1,3},{2,0},{3,1},{4,6},{5,7},{6,4},{7,5},{8,10},{9,11},{10,... | collective-permute-start | bytes 786440 | tf_op jit(solution)/shard_map/ppermute | solution.py:37
  10.9 13.5 %collective-permute-start = (bf16[128,2048]{1,0:T(8,128)(2,1)S(1)}, bf16[128,2048]{1,0:T(8,128)(2,1)S(1)}, u32[]{:S(2)}, u32[]{:S(2)}) collective-permute-start(bf16[128,2048]{1,0:T(8,128)(2,1)S(1)} %copy-done.1), channel_id=1, source_target_pairs={{0,1},{1,0},{2,3},{3,2},{4,5},{5,4},{6,7},{7,6},{8,9},{9,8},{10,11... | collective-permute-start | bytes 1572872 | tf_op jit(solution)/shard_map/ppermute | solution.py:33
  13.7 15.2 %all-to-all-start.2 = ((bf16[16,128,128]{2,1,0:T(8,128)(2,1)}), bf16[16,128,128]{2,1,0:T(8,128)(2,1)S(1)}, u32[]{:S(2)}, u32[]{:S(2)}) async-start(bf16[16,128,128]{2,1,0:T(8,128)(2,1)} %get-tuple-element.9), calls=%async_computation.2 | async-start | bytes 1048576 | tf_op jit(solution)/shard_map/all_to_all | solution.py:247
  19.7 3.4 %collective-permute-start.3 = (bf16[32,2048]{1,0:T(8,128)(2,1)S(1)}, bf16[32,2048]{1,0:T(8,128)(2,1)S(1)}, u32[]{:S(2)}, u32[]{:S(2)}) collective-permute-start(bf16[32,2048]{1,0:T(8,128)(2,1)S(1)} %get-tuple-element.19), channel_id=1, source_target_pairs={{0,1},{1,0},{2,3},{3,2},{4,5},{5,4},{6,7},{7,6},{8,9},{9,8},{10,11... | collective-permute-start | bytes 393224 | tf_op jit(solution)/shard_map/ppermute | solution.py:33
  22.0 1.4 %collective-permute-start.4 = (bf16[32,2048]{1,0:T(8,128)(2,1)S(1)}, bf16[32,2048]{1,0:T(8,128)(2,1)S(1)}, u32[]{:S(2)}, u32[]{:S(2)}) collective-permute-start(bf16[32,2048]{1,0:T(8,128)(2,1)S(1)} %get-tuple-element.22), channel_id=1, source_target_pairs={{0,1},{1,0},{2,3},{3,2},{4,5},{5,4},{6,7},{7,6},{8,9},{9,8},{10,11... | collective-permute-start | bytes 393224 | tf_op jit(solution)/shard_map/ppermute | solution.py:33
  22.1 1.4 %collective-permute-start.5 = (bf16[32,2048]{1,0:T(8,128)(2,1)S(1)}, bf16[32,2048]{1,0:T(8,128)(2,1)S(1)}, u32[]{:S(2)}, u32[]{:S(2)}) collective-permute-start(bf16[32,2048]{1,0:T(8,128)(2,1)S(1)} %get-tuple-element.21), channel_id=1, source_target_pairs={{0,1},{1,0},{2,3},{3,2},{4,5},{5,4},{6,7},{7,6},{8,9},{9,8},{10,11... | collective-permute-start | bytes 393224 | tf_op jit(solution)/shard_map/ppermute | solution.py:33
  22.6 1.3 %collective-permute-start.6 = (bf16[32,2048]{1,0:T(8,128)(2,1)S(1)}, bf16[32,2048]{1,0:T(8,128)(2,1)S(1)}, u32[]{:S(2)}, u32[]{:S(2)}) collective-permute-start(bf16[32,2048]{1,0:T(8,128)(2,1)S(1)} %get-tuple-element.20), channel_id=1, source_target_pairs={{0,1},{1,0},{2,3},{3,2},{4,5},{5,4},{6,7},{7,6},{8,9},{9,8},{10,11... | collective-permute-start | bytes 393224 | tf_op jit(solution)/shard_map/ppermute | solution.py:33
  23.0 1.3 %collective-permute-start.7 = (bf16[128,512]{1,0:T(8,128)(2,1)S(1)}, bf16[128,512]{1,0:T(8,128)(2,1)S(1)}, u32[]{:S(2)}, u32[]{:S(2)}) collective-permute-start(bf16[128,512]{1,0:T(8,128)(2,1)S(1)} %get-tuple-element.17), channel_id=1, source_target_pairs={{0,1},{1,0},{2,3},{3,2},{4,5},{5,4},{6,7},{7,6},{8,9},{9,8},{10,11... | collective-permute-start | bytes 393224 | tf_op jit(solution)/shard_map/ppermute | solution.py:33
  23.4 1.3 %collective-permute-start.8 = (bf16[128,512]{1,0:T(8,128)(2,1)S(1)}, bf16[128,512]{1,0:T(8,128)(2,1)S(1)}, u32[]{:S(2)}, u32[]{:S(2)}) collective-permute-start(bf16[128,512]{1,0:T(8,128)(2,1)S(1)} %get-tuple-element.23), channel_id=1, source_target_pairs={{0,1},{1,0},{2,3},{3,2},{4,5},{5,4},{6,7},{7,6},{8,9},{9,8},{10,11... | collective-permute-start | bytes 393224 | tf_op jit(solution)/shard_map/ppermute | solution.py:33
  28.8 7.2 %copy-start.2 = (bf16[16,128,128]{2,1,0:T(8,128)(2,1)}, bf16[16,128,128]{2,1,0:T(8,128)(2,1)S(1)}, u32[]{:S(2)}) copy-start(bf16[16,128,128]{2,1,0:T(8,128)(2,1)S(1)} %all-to-all-done.2) | copy-start | bytes 1572868
  28.8 35.7 %all-to-all-start = ((bf16[16,128,512]{2,1,0:T(8,128)(2,1)}), bf16[16,128,512]{2,1,0:T(8,128)(2,1)S(1)}, u32[]{:S(2)}, u32[]{:S(2)}) async-start(bf16[16,128,512]{2,1,0:T(8,128)(2,1)} %bitcast.1), calls=%async_computation | async-start | bytes 4194304 | tf_op jit(solution)/shard_map/all_to_all | solution.py:250
  36.0 2.6 %collective-permute-start.9 = (bf16[2048,128]{1,0:T(8,128)(2,1)S(1)}, bf16[2048,128]{1,0:T(8,128)(2,1)}, u32[]{:S(2)}, u32[]{:S(2)}) collective-permute-start(bf16[2048,128]{1,0:T(8,128)(2,1)S(1)} %bitcast.66), channel_id=1, source_target_pairs={{0,1},{1,0},{2,3},{3,2},{4,5},{5,4},{6,7},{7,6},{8,9},{9,8},{10,11... | collective-permute-start | bytes 1572872 | tf_op jit(solution)/shard_map/ppermute | solution.py:33
  46.8 15.0 %collective-permute-start.10 = (bf16[256,128]{1,0:T(8,128)(2,1)S(1)}, bf16[256,128]{1,0:T(8,128)(2,1)S(1)}, u32[]{:S(2)}, u32[]{:S(2)}) collective-permute-start(bf16[256,128]{1,0:T(8,128)(2,1)S(1)} %get-tuple-element.10), channel_id=1, source_target_pairs={{0,8},{1,9},{2,10},{3,11},{4,12},{5,13},{6,14},{7,15},{8,0},{9,1},... | collective-permute-start | bytes 196616 | tf_op jit(solution)/shard_map/ppermute | solution.py:41
  53.8 10.2 %collective-permute-start.11 = (bf16[256,128]{1,0:T(8,128)(2,1)S(1)}, bf16[256,128]{1,0:T(8,128)(2,1)S(1)}, u32[]{:S(2)}, u32[]{:S(2)}) collective-permute-start(bf16[256,128]{1,0:T(8,128)(2,1)S(1)} %get-tuple-element.16), channel_id=1, source_target_pairs={{0,6},{1,7},{2,8},{3,9},{4,10},{5,11},{6,12},{7,13},{8,14},{9,15},... | collective-permute-start | bytes 196616 | tf_op jit(solution)/shard_map/ppermute | solution.py:41
  55.4 19.4 %collective-permute-start.12 = (bf16[256,128]{1,0:T(8,128)(2,1)S(1)}, bf16[256,128]{1,0:T(8,128)(2,1)S(1)}, u32[]{:S(2)}, u32[]{:S(2)}) collective-permute-start(bf16[256,128]{1,0:T(8,128)(2,1)S(1)} %get-tuple-element.15), channel_id=1, source_target_pairs={{0,10},{1,11},{2,12},{3,13},{4,14},{5,15},{6,0},{7,1},{8,2},{9,3},... | collective-permute-start | bytes 196616 | tf_op jit(solution)/shard_map/ppermute | solution.py:41
  58.2 16.6 %collective-permute-start.13 = (bf16[256,128]{1,0:T(8,128)(2,1)S(1)}, bf16[256,128]{1,0:T(8,128)(2,1)S(1)}, u32[]{:S(2)}, u32[]{:S(2)}) collective-permute-start(bf16[256,128]{1,0:T(8,128)(2,1)S(1)} %get-tuple-element.14), channel_id=1, source_target_pairs={{0,4},{1,5},{2,6},{3,7},{4,8},{5,9},{6,10},{7,11},{8,12},{9,13},{1... | collective-permute-start | bytes 196616 | tf_op jit(solution)/shard_map/ppermute | solution.py:41
  59.4 15.4 %collective-permute-start.14 = (bf16[256,128]{1,0:T(8,128)(2,1)S(1)}, bf16[256,128]{1,0:T(8,128)(2,1)S(1)}, u32[]{:S(2)}, u32[]{:S(2)}) collective-permute-start(bf16[256,128]{1,0:T(8,128)(2,1)S(1)} %get-tuple-element.13), channel_id=1, source_target_pairs={{0,12},{1,13},{2,14},{3,15},{4,0},{5,1},{6,2},{7,3},{8,4},{9,5},{1... | collective-permute-start | bytes 196616 | tf_op jit(solution)/shard_map/ppermute | solution.py:41
  61.8 13.0 %collective-permute-start.15 = (bf16[256,128]{1,0:T(8,128)(2,1)S(1)}, bf16[256,128]{1,0:T(8,128)(2,1)S(1)}, u32[]{:S(2)}, u32[]{:S(2)}) collective-permute-start(bf16[256,128]{1,0:T(8,128)(2,1)S(1)} %get-tuple-element.12), channel_id=1, source_target_pairs={{0,2},{1,3},{2,4},{3,5},{4,6},{5,7},{6,8},{7,9},{8,10},{9,11},{10,... | collective-permute-start | bytes 196616 | tf_op jit(solution)/shard_map/ppermute | solution.py:41
  63.9 10.9 %collective-permute-start.16 = (bf16[256,128]{1,0:T(8,128)(2,1)S(1)}, bf16[256,128]{1,0:T(8,128)(2,1)S(1)}, u32[]{:S(2)}, u32[]{:S(2)}) collective-permute-start(bf16[256,128]{1,0:T(8,128)(2,1)S(1)} %get-tuple-element.11), channel_id=1, source_target_pairs={{0,14},{1,15},{2,0},{3,1},{4,2},{5,3},{6,4},{7,5},{8,6},{9,7},{10,... | collective-permute-start | bytes 196616 | tf_op jit(solution)/shard_map/ppermute | solution.py:41
  65.4 18.6 %all-to-all-start.1 = ((bf16[16,8,512]{2,1,0:T(8,128)(2,1)}), bf16[16,8,512]{2,1,0:T(8,128)(2,1)S(1)}, u32[]{:S(2)}, u32[]{:S(2)}) async-start(bf16[16,8,512]{2,1,0:T(8,128)(2,1)} %bitcast.2), calls=%async_computation.1 | async-start | bytes 262144 | tf_op jit(solution)/shard_map/all_to_all | solution.py:278

commit v5 on v4

--- a/solution.py
+++ b/solution.py
@@ -53,7 +53,7 @@
     return pltpu.CompilerParams(vmem_limit_bytes=mib << 20)
 
 
-def front_kernel(map_hbm, top_hbm, gh_hbm, w_hbm, b_hbm, gp_ref, out_ref, map_ref, top_ref, gh_ref, w_ref, b_ref, acc_ref, sems):
+def front_kernel(map_hbm, top_hbm, gh_hbm, w_hbm, b_hbm, keep_ref, give_ref, out_ref, map_ref, top_ref, gh_ref, w_ref, b_ref, gp_ref, acc_ref, sems):
     hidden = gh_ref.shape[1]
     blocks = sems.shape[0] - 4
     block = hidden // blocks
@@ -92,6 +92,10 @@
             acc_ref[...] = part
         else:
             acc_ref[...] += part
+    bit = lax.rem(lax.div(lax.axis_index("chip"), NC), 2)
+    half = hidden // 2
+    keep_ref[...] = gp_ref[:, pl.ds(pl.multiple_of(bit * half, half), half)]
+    give_ref[...] = gp_ref[:, pl.ds(pl.multiple_of((1 - bit) * half, half), half)]
     slw = out_ref.shape[2]
     for s in range(out_ref.shape[0]):
         first = pl.multiple_of(map_ref[s] * slw, slw)
@@ -106,9 +110,10 @@
     return pl.pallas_call(
         front_kernel,
         in_specs=[HBM] * 5,
-        out_specs=[VMEM] * 2,
+        out_specs=[VMEM] * 3,
         out_shape=[
-            jax.ShapeDtypeStruct((b_dev, hidden), jnp.bfloat16),
+            jax.ShapeDtypeStruct((b_dev, hidden // 2), jnp.bfloat16),
+            jax.ShapeDtypeStruct((b_dev, hidden // 2), jnp.bfloat16),
             jax.ShapeDtypeStruct((slices, b_dev, slw), jnp.bfloat16),
         ],
         scratch_shapes=[
@@ -117,6 +122,7 @@
             pltpu.VMEM((b_dev, hidden), jnp.bfloat16),
             pltpu.VMEM((width, hidden), jnp.bfloat16),
             pltpu.VMEM((1, hidden), jnp.float32),
+            pltpu.VMEM((b_dev, hidden), jnp.bfloat16),
             pltpu.VMEM((b_dev, width), jnp.float32),
             pltpu.SemaphoreType.DMA((4 + blocks,)),
         ],
@@ -126,7 +132,10 @@
 
 
 def weight_kernel(x0, x1, x2, x3, g0, g1, g2, g3, o_ref):
-    grads = jnp.concatenate([g[...] for g in (g0, g1, g2, g3)], axis=0)
+    quart = o_ref.shape[1]
+    core = lax.rem(lax.axis_index("chip"), NC)
+    cols = pl.ds(pl.multiple_of(core * quart, quart), quart)
+    grads = jnp.concatenate([g[:, cols] for g in (g0, g1, g2, g3)], axis=0)
     step = 512
     for first in range(0, x0.shape[1], step):
         left = jnp.concatenate([v[:, first : first + step] for v in (x0, x1, x2, x3)], axis=0)
@@ -138,7 +147,7 @@
 def weight_part(tops, grads):
     return pl.pallas_call(
         weight_kernel,
-        out_shape=jax.ShapeDtypeStruct((tops[0].shape[1], grads[0].shape[1]), jnp.bfloat16),
+        out_shape=jax.ShapeDtypeStruct((tops[0].shape[1], grads[0].shape[1] // NC), jnp.bfloat16),
         in_specs=[VMEM] * 8,
         out_specs=VMEM,
         compiler_params=params(16),
@@ -164,15 +173,8 @@
     )(blocks)
 
 
-def table_kernel(chunk, rb, ids_ref, x_hbm, y_hbm, o_ref, x_ref, y_ref, sems):
-    copies = [
-        pltpu.make_async_copy(x_hbm, x_ref, sems.at[0]),
-        pltpu.make_async_copy(y_hbm, y_ref, sems.at[1]),
-    ]
-    for copy in copies:
-        copy.start()
-    for copy in copies:
-        copy.wait()
+def table_kernel(chunk, rb, first, ids_ref, x_ref, *refs):
+    o_ref = refs[-1]
     samples = x_ref.shape[0]
     one = jnp.ones((), jnp.bfloat16)
     zero = jnp.zeros((), jnp.bfloat16)
@@ -180,42 +182,70 @@
 
     def do_block(k, carry):
         base = k * rb
-        acc = jnp.zeros((rb, x_ref.shape[1]), jnp.float32)
-        for s in range(2 * samples // chunk):
-            ids = (ids_ref[:, s * chunk : (s + 1) * chunk] - base).astype(jnp.int16)
+        rows = pl.ds(pl.multiple_of(base, rb), rb)
+        if len(refs) > 1:
+            acc = refs[0][rows, :]
+        else:
+            acc = jnp.zeros((rb, x_ref.shape[1]), jnp.float32)
+        for s in range(samples // chunk):
+            here = slice(first + s * chunk, first + (s + 1) * chunk)
+            ids = (ids_ref[:, here] - base).astype(jnp.int16)
             counts = None
             for j in range(ids_ref.shape[0]):
                 hit = jnp.where(jnp.broadcast_to(ids[j : j + 1], (rb, chunk)) == target, one, zero)
                 counts = hit if counts is None else counts + hit
-            first = s * chunk
-            rows = x_ref[first : first + chunk, :] if first < samples else y_ref[first - samples : first - samples + chunk, :]
-            acc = acc + jnp.dot(counts, rows, preferred_element_type=jnp.float32)
-        o_ref[pl.ds(pl.multiple_of(base, rb), rb), :] = acc.astype(jnp.bfloat16)
+            acc = acc + jnp.dot(
+                counts, x_ref[s * chunk : (s + 1) * chunk, :], preferred_element_type=jnp.float32
+            )
+        o_ref[rows, :] = acc.astype(o_ref.dtype)
         return carry
 
     lax.fori_loop(0, o_ref.shape[0] // rb, do_block, 0)
 
 
-def table_partial(ids, x, y):
-    return pl.pallas_call(
-        functools.partial(table_kernel, 256, 512),
-        out_shape=jax.ShapeDtypeStruct((LOCAL_ROWS, x.shape[1]), jnp.bfloat16),
-        in_specs=[VMEM, HBM, HBM],
+def table_partial(ids, x, sums=None):
+    first = 0 if sums is None else x.shape[0]
+    more = [] if sums is None else [sums]
+    dtype = jnp.float32 if sums is None else jnp.bfloat16
+    return pl.pallas_call(
+        functools.partial(table_kernel, 256, 512, first),
+        out_shape=jax.ShapeDtypeStruct((LOCAL_ROWS, x.shape[1]), dtype),
+        in_specs=[VMEM] * (2 + len(more)),
         out_specs=VMEM,
-        scratch_shapes=[
-            pltpu.VMEM(x.shape, jnp.bfloat16),
-            pltpu.VMEM(y.shape, jnp.bfloat16),
-            pltpu.SemaphoreType.DMA((2,)),
+        compiler_params=params(16),
+        name="table_own" if sums is None else "table_other",
+    )(ids, x, *more)
+
+
+def last_kernel(w_ref, *refs):
+    shares, w_out, t_out = refs[:-2], refs[-2], refs[-1]
+    quart = w_ref.shape[2]
+    parts = w_out.shape[1] // quart
+    for q in range(parts):
+        w_out[:, q * quart : (q + 1) * quart] = sum(
+            f32(w_ref[k]) for k in range(q, w_ref.shape[0], parts)
+        )
+    t_out[...] = sum(f32(s[...]) for s in shares)
+
+
+def last_sums(swapped, shares):
+    _, rows, quart = swapped.shape
+    return pl.pallas_call(
+        last_kernel,
+        out_shape=[
+            jax.ShapeDtypeStruct((rows, 2 * NC * quart), jnp.float32),
+            jax.ShapeDtypeStruct(shares[0].shape, jnp.float32),
         ],
-        compiler_params=params(16),
-        name="table_partial",
-    )(ids, in_hbm(x), in_hbm(y))
+        in_specs=[VMEM] * (1 + len(shares)),
+        out_specs=[VMEM] * 2,
+        compiler_params=params(8),
+        name="last_sums",
+    )(swapped, *shares)
 
 
 def body(top_input, grad_hidden, w_in, b_in, slice_map, lookup_ids, bag_len):
     chip = lax.axis_index("chip")
     z, core = lax.div(chip, NC), lax.rem(chip, NC)
-    bit = lax.rem(z, 2)
     b_dev, width = top_input.shape
     hidden = grad_hidden.shape[1]
     half = hidden // 2
@@ -224,10 +254,8 @@
     top_core = core_swap(top_input)
     top_pair = pair_swap(top_input)
 
-    grad_pre, ordered = front(slice_map, top_input, grad_hidden, w_in, b_in)
-
-    keep = lax.dynamic_slice_in_dim(grad_pre, bit * half, half, 1)
-    pair = pair_swap(lax.dynamic_slice_in_dim(grad_pre, (1 - bit) * half, half, 1))
+    keep, give, ordered = front(slice_map, top_input, grad_hidden, w_in, b_in)
+    pair = pair_swap(give)
 
     top_pair, pair = lax.optimization_barrier((top_pair, pair))
     piece = b_dev // 4
@@ -235,21 +263,7 @@
         [core_swap(top_pair[k * piece : (k + 1) * piece]) for k in range(4)], axis=0
     )
 
-    def mine(v):
-        return lax.dynamic_slice_in_dim(v, core * quart, quart, 1)
-
-    def other(v):
-        return lax.dynamic_slice_in_dim(v, (1 - core) * quart, quart, 1)
-
-    grads = (mine(keep), core_swap(other(keep)), mine(pair), core_swap(other(pair)))
-    part = weight_part((top_input, top_core, top_pair, top_both), grads)
-
-    received = lax.all_to_all(ordered, "hst", split_axis=0, concat_axis=1, tiled=True)[0]
-    rec_other = core_swap(received)
-
-    blocks = lax.all_to_all(
-        part.reshape(NX * NY, width // (NX * NY), quart), "hst", split_axis=0, concat_axis=0, tiled=True
-    )
+    grads = (keep, core_swap(keep), pair, core_swap(pair))
 
     slots = lookup_ids.shape[1]
     ids = lookup_ids[0].reshape(slots, NX * NY, NZ, NC, b_dev)
@@ -263,23 +277,31 @@
     near = lax.dynamic_index_in_dim(local, core, 2, keepdims=False).reshape(slots, -1)
     far = lax.dynamic_index_in_dim(local, 1 - core, 2, keepdims=False).reshape(slots, -1)
     local = jnp.concatenate([near, far], axis=1)
-    table = table_partial(local, received, rec_other)
+    grads, local = lax.optimization_barrier((grads, local))
+    part = weight_part((top_input, top_core, top_pair, top_both), grads)
+
+    received = lax.all_to_all(ordered, "hst", split_axis=0, concat_axis=1, tiled=True)[0]
+    rec_other = core_swap(received)
+
+    blocks = lax.all_to_all(
+        part.reshape(NX * NY, width // (NX * NY), quart), "hst", split_axis=0, concat_axis=0, tiled=True
+    )
+
+    table = table_partial(local, rec_other, table_partial(local, received))
     table = table.reshape(NZ, ROWS_DEV, -1)
 
     def rows_of(d):
         return lax.dynamic_index_in_dim(table, lax.rem(z + d, NZ), 0, keepdims=False)
 
-    table_grad = f32(rows_of(0))
-    for d in (4, 3, 5, 2, 6, 1, 7):
-        table_grad = table_grad + f32(z_shift(rows_of(d), d))
-
+    shares = [rows_of(0)] + [z_shift(rows_of(d), d) for d in (4, 3, 5, 2, 6, 1, 7)]
+
+    blocks, shares = lax.optimization_barrier((blocks, shares))
     summed = sum_blocks(blocks)
     rows_out = summed.shape[0] // (NZ * NC)
     swapped = lax.all_to_all(
         summed.reshape(NZ * NC, rows_out, quart), "chip", split_axis=0, concat_axis=0, tiled=True
     )
-    total = f32(swapped).reshape(NZ // 2, 2 * NC, rows_out, quart).sum(0)
-    w_in_grad = total.transpose(1, 0, 2).reshape(rows_out, hidden)
+    w_in_grad, table_grad = last_sums(swapped, shares)
     return (w_in_grad, table_grad[None])
 
 

time: 85 us -> 85.3 us (level)
  blocking collectives: 0 us -> 18.3 us
  starting transfers between devices: 46 us -> 35.8 us
  waiting for transfers between devices: 14.9 us -> 7.63 us
  local copies, waits for them, and re-layouts: 1.98 us -> 3.45 us
  other arithmetic: 1.55 us -> 0.17 us
    all_to_all x0 -> x1, blocking collectives: none -> 18.3 us  [body(): lax.all_to_all(summed.reshape(NZ * NC, rows_out, quart), 'chip', split_ax...]
    all_to_all x1 -> x0, starting transfers between devices: 9.41 us -> none  [body(): lax.all_to_all(summed.reshape(NZ * NC, rows_out, quart), 'chip', split_ax...]
    all_to_all x1 -> x0, waiting for transfers between devices: 8.39 us -> none  [body(): lax.all_to_all(summed.reshape(NZ * NC, rows_out, quart), 'chip', split_ax...]
    ppermute x7, waiting for transfers between devices: 1.4 us -> 5.6 us  [z_shift(): lax.ppermute(value, AXES, permutation(lambda x, y, z, c: (x, y, (z + d) %...]
    ppermute x8, starting transfers between devices: 7.27 us -> 3.93 us  [core_swap(): lax.ppermute(value, AXES, permutation(lambda x, y, z, c: (x, y, z, 1 - c)))]
    ppermute x2, starting transfers between devices: 2.68 us -> 4.23 us  [pair_swap(): lax.ppermute(value, AXES, permutation(lambda x, y, z, c: (x, y, z ^ 1, c)))]
    ppermute x8, waiting for transfers between devices: 2.82 us -> 1.53 us  [core_swap(): lax.ppermute(value, AXES, permutation(lambda x, y, z, c: (x, y, z, 1 - c)))]
    all_to_all x1, starting transfers between devices: 5.31 us -> 6.44 us  [body(): lax.all_to_all(part.reshape(NX * NY, width // (NX * NY), quart), 'hst', s...]
  transfers between devices with their start and end apart: 20 -> 19, of which waited for: 9 -> 7; matrix products, arithmetic and copies ran while one was open for 3% -> 4% of each run, Pallas kernels for 23% -> 21%
where the time goes in v5:
time: 85.3 us; the launch traced here: 84.9 us
  starting transfers between devices  35.8 us (42%)
  Pallas kernels  18.7 us (22%)
  blocking collectives  18.3 us (21%)
  waiting for transfers between devices  7.63 us (9%)
  local copies, waits for them, and re-layouts  3.45 us (4%)
    all_to_all x1, blocking collectives, body(): lax.all_to_all(summed.reshape(NZ * NC, rows_out, quart), 'chip', split_ax...  18.3 us
    ppermute x7, starting transfers between devices, z_shift(): lax.ppermute(value, AXES, permutation(lambda x, y, z, c: (x, y, (z + d) %...  16.2 us
    pallas_call x1, Pallas kernels, front(): pl.pallas_call(front_kernel, in_specs=[HBM] * 5, out_specs=[VMEM] * 3, ou...  7.55 us
    pallas_call x2, Pallas kernels, table_partial(): pl.pallas_call(functools.partial(table_kernel, 256, 512, first), out_shap...  7.51 us
    all_to_all x1, starting transfers between devices, body(): lax.all_to_all(part.reshape(NX * NY, width // (NX * NY), quart), 'hst', s...  6.44 us
    ppermute x7, waiting for transfers between devices, z_shift(): lax.ppermute(value, AXES, permutation(lambda x, y, z, c: (x, y, (z + d) %...  5.6 us
    all_to_all x1, starting transfers between devices, body(): lax.all_to_all(ordered, 'hst', split_axis=0, concat_axis=1, tiled=True)[0]  5.03 us
    ppermute x2, starting transfers between devices, pair_swap(): lax.ppermute(value, AXES, permutation(lambda x, y, z, c: (x, y, z ^ 1, c)))  4.23 us
  transfers between devices with their start and end apart: 19, of which 7 were waited for; matrix products, arithmetic and copies ran while one was open for 4% of the time, Pallas kernels for 21%

profile of v5, /device:TPU:1, one launch (start us, length us, event | category | flops | bytes accessed | tf_op | source)
XLA Modules:
  0.0 84.9 jit_solution(3418476430553864975)
XLA Ops:
  0.6 0.0 copy-start
  0.6 2.6 %collective-permute-start.1 = (bf16[128,2048]{1,0:T(8,128)(2,1)}, bf16[128,2048]{1,0:T(8,128)(2,1)S(1)}, u32[]{:S(2)}, u32[]{:S(2)}) collective-permute-start(bf16[128,2048]{1,0:T(8,128)(2,1)} %x0.1), channel_id=1, source_target_pairs={{0,2},{1,3},{2,0},{3,1},{4,6},{5,7},{6,4},{7,5},{8,10},{9,11},{10,... | collective-permute-start | bytes 1572872 | tf_op jit(solution)/shard_map/ppermute | solution.py:37
  3.2 1.0 %collective-permute-start = (bf16[128,2048]{1,0:T(8,128)(2,1)}, bf16[128,2048]{1,0:T(8,128)(2,1)S(1)}, u32[]{:S(2)}, u32[]{:S(2)}) collective-permute-start(bf16[128,2048]{1,0:T(8,128)(2,1)} %x0.1), channel_id=1, source_target_pairs={{0,1},{1,0},{2,3},{3,2},{4,5},{5,4},{6,7},{7,6},{8,9},{9,8},{10,11... | collective-permute-start | bytes 1572872 | tf_op jit(solution)/shard_map/ppermute | solution.py:33
  4.2 7.5 %front.1 = (bf16[128,1024]{1,0:T(8,128)(2,1)S(1)}, bf16[128,1024]{1,0:T(8,128)(2,1)S(1)}, bf16[16,128,128]{2,1,0:T(8,128)(2,1)}) custom-call(s32[16]{0:T(128)} %map_hbm.1, bf16[128,2048]{1,0:T(8,128)(2,1)} %x0.1, bf16[128,2048]{1,0:T(8,128)(2,1)} %gh_hbm.1, bf16[2048,2048]{1,0:T(8,128)(2,1)} %w_hbm.1, f32[1,2048]{1,0:T(1,128)} %bitcast.62), custom_call_target="tpu_custom_call" | custom-call | tf_op jit(solution)/shard_map/front/pallas_call | solution.py:110
  11.7 1.7 %collective-permute-start.2 = (bf16[128,1024]{1,0:T(8,128)(2,1)S(1)}, bf16[128,1024]{1,0:T(8,128)(2,1)S(1)}, u32[]{:S(2)}, u32[]{:S(2)}) collective-permute-start(bf16[128,1024]{1,0:T(8,128)(2,1)S(1)} %get-tuple-element.23), channel_id=1, source_target_pairs={{0,2},{1,3},{2,0},{3,1},{4,6},{5,7},{6,4},{7,5},{8,10},{9,11},{10,... | collective-permute-start | bytes 786440 | tf_op jit(solution)/shard_map/ppermute | solution.py:37
  13.4 0.3 collective-permute-start.7
  13.7 5.0 %all-to-all-start.1 = ((bf16[16,128,128]{2,1,0:T(8,128)(2,1)}), bf16[16,128,128]{2,1,0:T(8,128)(2,1)S(1)}, u32[]{:S(2)}, u32[]{:S(2)}) async-start(bf16[16,128,128]{2,1,0:T(8,128)(2,1)} %get-tuple-element.32), calls=%async_computation.1 | async-start | bytes 1048576 | tf_op jit(solution)/shard_map/all_to_all | solution.py:283
  18.7 0.0 copy-start.1
  18.7 2.4 %reshape_squeeze.7 = s32[4,16,8,2,128]{4,3,2,1,0:T(2,128)} reshape(s32[1,4,32768]{2,1,0:T(4,128)} %param.12) | data formatting | bytes 1048576 | tf_op jit(solution)/shard_map/reshape;squeeze | solution.py:269
  21.2 0.0 copy-done
  21.2 0.9 %constant_dynamic-slice_fusion = s32[4,16,1,2,128]{4,3,2,1,0:T(2,128)S(1)} fusion(s32[4,16,8,2,128]{4,3,2,1,0:T(2,128)} %reshape_squeeze.7, s32[]{:T(128)S(6)} %select_n.61), kind=kLoop, calls=%fused_computation.41 | loop fusion | bytes 131076 | tf_op jit(solution)/shard_map/jit(dynamic_index_in_dim)/dynamic_slice | solution.py:271
  22.0 0.1 fusion.5
  22.2 0.0 collective-permute-done.2.g2
  22.2 0.0 collective-permute-done.1.x2
  22.3 0.8 collective-permute-start.3
  23.1 0.1 collective-permute-start.4
  23.2 0.5 collective-permute-start.8
  23.7 0.4 collective-permute-done.3
  24.1 0.4 collective-permute-start.5
  24.4 0.0 collective-permute-done.4
  24.4 0.2 collective-permute-start.6
  24.6 0.8 collective-permute-done.5
  25.4 0.4 collective-permute-done.6
  25.8 0.0 collective-permute-done.7.g1
  25.9 0.0 collective-permute-done.8.g3
  25.9 0.0 collective-permute-done.x1
  25.9 0.0 copy-done.1
  25.9 2.6 %weight_part.1 = bf16[2048,512]{1,0:T(8,128)(2,1)} custom-call(bf16[128,2048]{1,0:T(8,128)(2,1)S(1)} %copy-done.1, bf16[128,2048]{1,0:T(8,128)(2,1)S(1)} %collective-permute-done.x1, bf16[128,2048]{1,0:T(8,128)(2,1)S(1)} %collective-permute-done.1.x2, bf16[128,2048]{1,0:T(8,128)(2,1)S(1)} %pad_maximum_fusion.x3, bf16[128,1024]{1,0:T(8,128)(2,1)S(1)} %get-tuple-element.27.g0, ...), custom_call_target="tpu_custom_call" | custom-call | tf_op jit(solution)/shard_map/weight_part/pallas_call | solution.py:148
  28.5 0.5 all-to-all-done.1
  29.0 6.4 %all-to-all-start = ((bf16[16,128,512]{2,1,0:T(8,128)(2,1)}), bf16[16,128,512]{2,1,0:T(8,128)(2,1)S(1)}, u32[]{:S(2)}, u32[]{:S(2)}) async-start(bf16[16,128,512]{2,1,0:T(8,128)(2,1)} %bitcast.4), calls=%async_computation | async-start | bytes 4194304 | tf_op jit(solution)/shard_map/all_to_all | solution.py:286
  35.5 0.7 collective-permute-start.9
  36.2 3.7 %table_own.1.refs_0_ = f32[2048,128]{1,0:T(8,128)S(1)} custom-call(s32[4,4096]{1,0:T(4,128)S(1)} %pad_add_fusion.ids_ref, bf16[2048,128]{1,0:T(8,128)(2,1)S(1)} %bitcast.58), custom_call_target="tpu_custom_call" | custom-call | tf_op jit(solution)/shard_map/table_own/pallas_call | solution.py:210
  40.0 0.0 collective-permute-done.9.x_ref
  40.0 3.8 %table_other.1 = bf16[2048,128]{1,0:T(8,128)(2,1)S(1)} custom-call(s32[4,4096]{1,0:T(4,128)S(1)} %pad_add_fusion.ids_ref, bf16[2048,128]{1,0:T(8,128)(2,1)S(1)} %collective-permute-done.9.x_ref, f32[2048,128]{1,0:T(8,128)S(1)} %table_own.1.refs_0_), custom_call_target="tpu_custom_call" | custom-call | tf_op jit(solution)/shard_map/table_other/pallas_call | solution.py:210
  43.7 0.1 dynamic-slice_bitcast_fusion
  43.8 6.7 %collective-permute-start.10 = (bf16[256,128]{1,0:T(8,128)(2,1)S(1)}, bf16[256,128]{1,0:T(8,128)(2,1)S(1)}, u32[]{:S(2)}, u32[]{:S(2)}) collective-permute-start(bf16[256,128]{1,0:T(8,128)(2,1)S(1)} %get-tuple-element.50), channel_id=1, source_target_pairs={{0,8},{1,9},{2,10},{3,11},{4,12},{5,13},{6,14},{7,15},{8,0},{9,1},... | collective-permute-start | bytes 196616 | tf_op jit(solution)/shard_map/ppermute | solution.py:41
  50.5 1.6 %collective-permute-start.11 = (bf16[256,128]{1,0:T(8,128)(2,1)S(1)}, bf16[256,128]{1,0:T(8,128)(2,1)S(1)}, u32[]{:S(2)}, u32[]{:S(2)}) collective-permute-start(bf16[256,128]{1,0:T(8,128)(2,1)S(1)} %get-tuple-element.49), channel_id=1, source_target_pairs={{0,6},{1,7},{2,8},{3,9},{4,10},{5,11},{6,12},{7,13},{8,14},{9,15},... | collective-permute-start | bytes 196616 | tf_op jit(solution)/shard_map/ppermute | solution.py:41
  52.2 2.8 %collective-permute-start.12 = (bf16[256,128]{1,0:T(8,128)(2,1)S(1)}, bf16[256,128]{1,0:T(8,128)(2,1)S(1)}, u32[]{:S(2)}, u32[]{:S(2)}) collective-permute-start(bf16[256,128]{1,0:T(8,128)(2,1)S(1)} %get-tuple-element.48), channel_id=1, source_target_pairs={{0,10},{1,11},{2,12},{3,13},{4,14},{5,15},{6,0},{7,1},{8,2},{9,3},... | collective-permute-start | bytes 196616 | tf_op jit(solution)/shard_map/ppermute | solution.py:41
  55.0 1.2 %collective-permute-start.13 = (bf16[256,128]{1,0:T(8,128)(2,1)S(1)}, bf16[256,128]{1,0:T(8,128)(2,1)S(1)}, u32[]{:S(2)}, u32[]{:S(2)}) collective-permute-start(bf16[256,128]{1,0:T(8,128)(2,1)S(1)} %get-tuple-element.47), channel_id=1, source_target_pairs={{0,4},{1,5},{2,6},{3,7},{4,8},{5,9},{6,10},{7,11},{8,12},{9,13},{1... | collective-permute-start | bytes 196616 | tf_op jit(solution)/shard_map/ppermute | solution.py:41
  56.2 2.4 %collective-permute-start.14 = (bf16[256,128]{1,0:T(8,128)(2,1)S(1)}, bf16[256,128]{1,0:T(8,128)(2,1)S(1)}, u32[]{:S(2)}, u32[]{:S(2)}) collective-permute-start(bf16[256,128]{1,0:T(8,128)(2,1)S(1)} %get-tuple-element.46), channel_id=1, source_target_pairs={{0,12},{1,13},{2,14},{3,15},{4,0},{5,1},{6,2},{7,3},{8,4},{9,5},{1... | collective-permute-start | bytes 196616 | tf_op jit(solution)/shard_map/ppermute | solution.py:41
  58.6 0.0 collective-permute-done.10.refs_1_
  58.6 0.7 collective-permute-start.15
  59.3 1.3 %collective-permute-done.11.refs_2_ = bf16[256,128]{1,0:T(8,128)(2,1)S(1)} collective-permute-done((bf16[256,128]{1,0:T(8,128)(2,1)S(1)}, bf16[256,128]{1,0:T(8,128)(2,1)S(1)}, u32[]{:S(2)}, u32[]{:S(2)}) %collective-permute-start.11) | collective-permute-done | bytes 65568 | tf_op jit(solution)/shard_map/ppermute | solution.py:41
  60.6 0.7 collective-permute-start.16
  61.3 0.0 collective-permute-done.12.refs_3_
  61.3 0.0 collective-permute-done.13.refs_4_
  61.3 2.2 %collective-permute-done.14.refs_5_ = bf16[256,128]{1,0:T(8,128)(2,1)S(1)} collective-permute-done((bf16[256,128]{1,0:T(8,128)(2,1)S(1)}, bf16[256,128]{1,0:T(8,128)(2,1)S(1)}, u32[]{:S(2)}, u32[]{:S(2)}) %collective-permute-start.14) | collective-permute-done | bytes 65568 | tf_op jit(solution)/shard_map/ppermute | solution.py:41
  63.5 0.0 collective-permute-done.15.refs_6_
  63.5 2.1 %collective-permute-done.16.refs_7_ = bf16[256,128]{1,0:T(8,128)(2,1)S(1)} collective-permute-done((bf16[256,128]{1,0:T(8,128)(2,1)S(1)}, bf16[256,128]{1,0:T(8,128)(2,1)S(1)}, u32[]{:S(2)}, u32[]{:S(2)}) %collective-permute-start.16) | collective-permute-done | bytes 65568 | tf_op jit(solution)/shard_map/ppermute | solution.py:41
  65.6 0.0 all-to-all-done.x_ref
  65.6 0.3 sum_blocks.1
  65.9 18.3 %all_to_all.19.w_ref = bf16[16,8,512]{2,1,0:T(8,128)(2,1)S(1)} all-to-all(bf16[16,8,512]{2,1,0:T(8,128)(2,1)S(1)} %bitcast.60), channel_id=1, replica_groups=mesh['hst'=16,'chip'=16] {'chip'}, dimensions={0} | all-to-all | bytes 262144 | tf_op jit(solution)/shard_map/all_to_all | solution.py:301
  84.2 0.7 last_sums.1
  (7 shorter events, 0.1 us)
Async XLA Ops:
  0.6 20.5 %copy-start = (s32[1,32768]{1,0:T(1,128)S(1)}, s32[1,32768]{1,0:T(1,128)}, u32[]{:S(2)}) copy-start(s32[1,32768]{1,0:T(1,128)} %param.13) | copy-start | bytes 393220
  0.6 21.6 %collective-permute-start.1 = (bf16[128,2048]{1,0:T(8,128)(2,1)}, bf16[128,2048]{1,0:T(8,128)(2,1)S(1)}, u32[]{:S(2)}, u32[]{:S(2)}) collective-permute-start(bf16[128,2048]{1,0:T(8,128)(2,1)} %x0.1), channel_id=1, source_target_pairs={{0,2},{1,3},{2,0},{3,1},{4,6},{5,7},{6,4},{7,5},{8,10},{9,11},{10,... | collective-permute-start | bytes 1572872 | tf_op jit(solution)/shard_map/ppermute | solution.py:37
  3.2 22.7 %collective-permute-start = (bf16[128,2048]{1,0:T(8,128)(2,1)}, bf16[128,2048]{1,0:T(8,128)(2,1)S(1)}, u32[]{:S(2)}, u32[]{:S(2)}) collective-permute-start(bf16[128,2048]{1,0:T(8,128)(2,1)} %x0.1), channel_id=1, source_target_pairs={{0,1},{1,0},{2,3},{3,2},{4,5},{5,4},{6,7},{7,6},{8,9},{9,8},{10,11... | collective-permute-start | bytes 1572872 | tf_op jit(solution)/shard_map/ppermute | solution.py:33
  11.7 10.5 %collective-permute-start.2 = (bf16[128,1024]{1,0:T(8,128)(2,1)S(1)}, bf16[128,1024]{1,0:T(8,128)(2,1)S(1)}, u32[]{:S(2)}, u32[]{:S(2)}) collective-permute-start(bf16[128,1024]{1,0:T(8,128)(2,1)S(1)} %get-tuple-element.23), channel_id=1, source_target_pairs={{0,2},{1,3},{2,0},{3,1},{4,6},{5,7},{6,4},{7,5},{8,10},{9,11},{10,... | collective-permute-start | bytes 786440 | tf_op jit(solution)/shard_map/ppermute | solution.py:37
  13.4 12.5 %collective-permute-start.7 = (bf16[128,1024]{1,0:T(8,128)(2,1)S(1)}, bf16[128,1024]{1,0:T(8,128)(2,1)S(1)}, u32[]{:S(2)}, u32[]{:S(2)}) collective-permute-start(bf16[128,1024]{1,0:T(8,128)(2,1)S(1)} %get-tuple-element.27.g0), channel_id=1, source_target_pairs={{0,1},{1,0},{2,3},{3,2},{4,5},{5,4},{6,7},{7,6},{8,9},{9,8},{10,11... | collective-permute-start | bytes 786440 | tf_op jit(solution)/shard_map/ppermute | solution.py:33
  13.7 15.4 %all-to-all-start.1 = ((bf16[16,128,128]{2,1,0:T(8,128)(2,1)}), bf16[16,128,128]{2,1,0:T(8,128)(2,1)S(1)}, u32[]{:S(2)}, u32[]{:S(2)}) async-start(bf16[16,128,128]{2,1,0:T(8,128)(2,1)} %get-tuple-element.32), calls=%async_computation.1 | async-start | bytes 1048576 | tf_op jit(solution)/shard_map/all_to_all | solution.py:283
  18.7 7.2 %copy-start.1 = (bf16[128,2048]{1,0:T(8,128)(2,1)S(1)}, bf16[128,2048]{1,0:T(8,128)(2,1)}, u32[]{:S(2)}) copy-start(bf16[128,2048]{1,0:T(8,128)(2,1)} %x0.1) | copy-start | bytes 1572868
  22.3 1.8 %collective-permute-start.3 = (bf16[32,2048]{1,0:T(8,128)(2,1)S(1)}, bf16[32,2048]{1,0:T(8,128)(2,1)S(1)}, u32[]{:S(2)}, u32[]{:S(2)}) collective-permute-start(bf16[32,2048]{1,0:T(8,128)(2,1)S(1)} %get-tuple-element.52), channel_id=1, source_target_pairs={{0,1},{1,0},{2,3},{3,2},{4,5},{5,4},{6,7},{7,6},{8,9},{9,8},{10,11... | collective-permute-start | bytes 393224 | tf_op jit(solution)/shard_map/ppermute | solution.py:33
  23.1 1.4 %collective-permute-start.4 = (bf16[32,2048]{1,0:T(8,128)(2,1)S(1)}, bf16[32,2048]{1,0:T(8,128)(2,1)S(1)}, u32[]{:S(2)}, u32[]{:S(2)}) collective-permute-start(bf16[32,2048]{1,0:T(8,128)(2,1)S(1)} %get-tuple-element.55), channel_id=1, source_target_pairs={{0,1},{1,0},{2,3},{3,2},{4,5},{5,4},{6,7},{7,6},{8,9},{9,8},{10,11... | collective-permute-start | bytes 393224 | tf_op jit(solution)/shard_map/ppermute | solution.py:33
  23.2 2.6 %collective-permute-start.8 = (bf16[128,1024]{1,0:T(8,128)(2,1)S(1)}, bf16[128,1024]{1,0:T(8,128)(2,1)S(1)}, u32[]{:S(2)}, u32[]{:S(2)}) collective-permute-start(bf16[128,1024]{1,0:T(8,128)(2,1)S(1)} %collective-permute-done.2.g2), channel_id=1, source_target_pairs={{0,1},{1,0},{2,3},{3,2},{4,5},{5,4},{6,7},{7,6},{8,9},{9,8},{10,11... | collective-permute-start | bytes 786440 | tf_op jit(solution)/shard_map/ppermute | solution.py:33
  24.1 1.3 %collective-permute-start.5 = (bf16[32,2048]{1,0:T(8,128)(2,1)S(1)}, bf16[32,2048]{1,0:T(8,128)(2,1)S(1)}, u32[]{:S(2)}, u32[]{:S(2)}) collective-permute-start(bf16[32,2048]{1,0:T(8,128)(2,1)S(1)} %get-tuple-element.54), channel_id=1, source_target_pairs={{0,1},{1,0},{2,3},{3,2},{4,5},{5,4},{6,7},{7,6},{8,9},{9,8},{10,11... | collective-permute-start | bytes 393224 | tf_op jit(solution)/shard_map/ppermute | solution.py:33
  24.4 1.3 %collective-permute-start.6 = (bf16[32,2048]{1,0:T(8,128)(2,1)S(1)}, bf16[32,2048]{1,0:T(8,128)(2,1)S(1)}, u32[]{:S(2)}, u32[]{:S(2)}) collective-permute-start(bf16[32,2048]{1,0:T(8,128)(2,1)S(1)} %get-tuple-element.53), channel_id=1, source_target_pairs={{0,1},{1,0},{2,3},{3,2},{4,5},{5,4},{6,7},{7,6},{8,9},{9,8},{10,11... | collective-permute-start | bytes 393224 | tf_op jit(solution)/shard_map/ppermute | solution.py:33
  29.0 36.6 %all-to-all-start = ((bf16[16,128,512]{2,1,0:T(8,128)(2,1)}), bf16[16,128,512]{2,1,0:T(8,128)(2,1)S(1)}, u32[]{:S(2)}, u32[]{:S(2)}) async-start(bf16[16,128,512]{2,1,0:T(8,128)(2,1)} %bitcast.4), calls=%async_computation | async-start | bytes 4194304 | tf_op jit(solution)/shard_map/all_to_all | solution.py:286
  35.5 4.5 %collective-permute-start.9 = (bf16[2048,128]{1,0:T(8,128)(2,1)S(1)}, bf16[2048,128]{1,0:T(8,128)(2,1)S(1)}, u32[]{:S(2)}, u32[]{:S(2)}) collective-permute-start(bf16[2048,128]{1,0:T(8,128)(2,1)S(1)} %bitcast.57), channel_id=1, source_target_pairs={{0,1},{1,0},{2,3},{3,2},{4,5},{5,4},{6,7},{7,6},{8,9},{9,8},{10,11... | collective-permute-start | bytes 1572872 | tf_op jit(solution)/shard_map/ppermute | solution.py:33
  43.8 14.8 %collective-permute-start.10 = (bf16[256,128]{1,0:T(8,128)(2,1)S(1)}, bf16[256,128]{1,0:T(8,128)(2,1)S(1)}, u32[]{:S(2)}, u32[]{:S(2)}) collective-permute-start(bf16[256,128]{1,0:T(8,128)(2,1)S(1)} %get-tuple-element.50), channel_id=1, source_target_pairs={{0,8},{1,9},{2,10},{3,11},{4,12},{5,13},{6,14},{7,15},{8,0},{9,1},... | collective-permute-start | bytes 196616 | tf_op jit(solution)/shard_map/ppermute | solution.py:41
  50.5 10.1 %collective-permute-start.11 = (bf16[256,128]{1,0:T(8,128)(2,1)S(1)}, bf16[256,128]{1,0:T(8,128)(2,1)S(1)}, u32[]{:S(2)}, u32[]{:S(2)}) collective-permute-start(bf16[256,128]{1,0:T(8,128)(2,1)S(1)} %get-tuple-element.49), channel_id=1, source_target_pairs={{0,6},{1,7},{2,8},{3,9},{4,10},{5,11},{6,12},{7,13},{8,14},{9,15},... | collective-permute-start | bytes 196616 | tf_op jit(solution)/shard_map/ppermute | solution.py:41
  52.2 9.1 %collective-permute-start.12 = (bf16[256,128]{1,0:T(8,128)(2,1)S(1)}, bf16[256,128]{1,0:T(8,128)(2,1)S(1)}, u32[]{:S(2)}, u32[]{:S(2)}) collective-permute-start(bf16[256,128]{1,0:T(8,128)(2,1)S(1)} %get-tuple-element.48), channel_id=1, source_target_pairs={{0,10},{1,11},{2,12},{3,13},{4,14},{5,15},{6,0},{7,1},{8,2},{9,3},... | collective-permute-start | bytes 196616 | tf_op jit(solution)/shard_map/ppermute | solution.py:41
  55.0 6.3 %collective-permute-start.13 = (bf16[256,128]{1,0:T(8,128)(2,1)S(1)}, bf16[256,128]{1,0:T(8,128)(2,1)S(1)}, u32[]{:S(2)}, u32[]{:S(2)}) collective-permute-start(bf16[256,128]{1,0:T(8,128)(2,1)S(1)} %get-tuple-element.47), channel_id=1, source_target_pairs={{0,4},{1,5},{2,6},{3,7},{4,8},{5,9},{6,10},{7,11},{8,12},{9,13},{1... | collective-permute-start | bytes 196616 | tf_op jit(solution)/shard_map/ppermute | solution.py:41
  56.2 7.3 %collective-permute-start.14 = (bf16[256,128]{1,0:T(8,128)(2,1)S(1)}, bf16[256,128]{1,0:T(8,128)(2,1)S(1)}, u32[]{:S(2)}, u32[]{:S(2)}) collective-permute-start(bf16[256,128]{1,0:T(8,128)(2,1)S(1)} %get-tuple-element.46), channel_id=1, source_target_pairs={{0,12},{1,13},{2,14},{3,15},{4,0},{5,1},{6,2},{7,3},{8,4},{9,5},{1... | collective-permute-start | bytes 196616 | tf_op jit(solution)/shard_map/ppermute | solution.py:41
  58.6 4.9 %collective-permute-start.15 = (bf16[256,128]{1,0:T(8,128)(2,1)S(1)}, bf16[256,128]{1,0:T(8,128)(2,1)S(1)}, u32[]{:S(2)}, u32[]{:S(2)}) collective-permute-start(bf16[256,128]{1,0:T(8,128)(2,1)S(1)} %get-tuple-element.45), channel_id=1, source_target_pairs={{0,2},{1,3},{2,4},{3,5},{4,6},{5,7},{6,8},{7,9},{8,10},{9,11},{10,... | collective-permute-start | bytes 196616 | tf_op jit(solution)/shard_map/ppermute | solution.py:41
  60.6 5.0 %collective-permute-start.16 = (bf16[256,128]{1,0:T(8,128)(2,1)S(1)}, bf16[256,128]{1,0:T(8,128)(2,1)S(1)}, u32[]{:S(2)}, u32[]{:S(2)}) collective-permute-start(bf16[256,128]{1,0:T(8,128)(2,1)S(1)} %get-tuple-element.44), channel_id=1, source_target_pairs={{0,14},{1,15},{2,0},{3,1},{4,2},{5,3},{6,4},{7,5},{8,6},{9,7},{10,... | collective-permute-start | bytes 196616 | tf_op jit(solution)/shard_map/ppermute | solution.py:41

commit v6 on v5

--- a/solution.py
+++ b/solution.py
@@ -10,6 +10,7 @@
 NX, NY, NZ, NC = 4, 4, 8, 2
 AXES = ("hst", "chip")
 ROWS_DEV = 256
+FRONT_BLOCKS = (256, 256, 512, 512, 512)
 LOCAL_ROWS = NZ * ROWS_DEV
 VMEM = pl.BlockSpec(memory_space=pltpu.VMEM)
 HBM = pl.BlockSpec(memory_space=pltpu.MemorySpace.HBM)
@@ -55,8 +56,8 @@
 
 def front_kernel(map_hbm, top_hbm, gh_hbm, w_hbm, b_hbm, keep_ref, give_ref, out_ref, map_ref, top_ref, gh_ref, w_ref, b_ref, gp_ref, acc_ref, sems):
     hidden = gh_ref.shape[1]
-    blocks = sems.shape[0] - 4
-    block = hidden // blocks
+    ends = [sum(FRONT_BLOCKS[: j + 1]) for j in range(len(FRONT_BLOCKS))]
+    spans = [slice(end - size, end) for end, size in zip(ends, FRONT_BLOCKS)]
     small = [
         pltpu.make_async_copy(src, dst, sems.at[k])
         for k, (src, dst) in enumerate(
@@ -65,21 +66,20 @@
     ]
     large = [
         pltpu.make_async_copy(
-            w_hbm.at[:, pl.ds(j * block, block)],
-            w_ref.at[:, pl.ds(j * block, block)],
+            w_hbm.at[:, span],
+            w_ref.at[:, span],
             sems.at[4 + j],
         )
-        for j in range(blocks)
+        for j, span in enumerate(spans)
     ]
     for copy in small[:1] + large[:1] + small[1:] + large[1:]:
         copy.start()
-    for j in range(blocks):
-        cols = slice(j * block, (j + 1) * block)
+    def cotangent(j):
+        cols = spans[j]
         if j == 0:
             small[0].wait()
         large[j].wait()
-        w = w_ref[:, cols]
-        pre = jnp.dot(top_ref[...], w, preferred_element_type=jnp.float32)
+        pre = jnp.dot(top_ref[...], w_ref[:, cols], preferred_element_type=jnp.float32)
         if j == 0:
             for copy in small[1:]:
                 copy.wait()
@@ -87,11 +87,23 @@
         sig = 1.0 / (1.0 + jnp.exp(-pre))
         grad = (f32(gh_ref[:, cols]) * sig * (1.0 + pre * (1.0 - sig))).astype(jnp.bfloat16)
         gp_ref[:, cols] = grad
-        part = lax.dot_general(grad, w, (((1,), (1,)), ((), ())), preferred_element_type=jnp.float32)
+        return grad
+
+    def back(j, grad):
+        part = lax.dot_general(
+            grad, w_ref[:, spans[j]], (((1,), (1,)), ((), ())), preferred_element_type=jnp.float32
+        )
         if j == 0:
             acc_ref[...] = part
         else:
             acc_ref[...] += part
+
+    grad = cotangent(0)
+    for j in range(1, len(spans)):
+        ahead = cotangent(j)
+        back(j - 1, grad)
+        grad = ahead
+    back(len(spans) - 1, grad)
     bit = lax.rem(lax.div(lax.axis_index("chip"), NC), 2)
     half = hidden // 2
     keep_ref[...] = gp_ref[:, pl.ds(pl.multiple_of(bit * half, half), half)]
@@ -102,7 +114,7 @@
         out_ref[s] = acc_ref[:, pl.ds(first, slw)].astype(jnp.bfloat16)
 
 
-def front(slice_map, top_input, grad_hidden, w_in, b_in, blocks=4):
+def front(slice_map, top_input, grad_hidden, w_in, b_in):
     b_dev, width = top_input.shape
     hidden = grad_hidden.shape[1]
     slices = slice_map.shape[0]
@@ -124,7 +136,7 @@
             pltpu.VMEM((1, hidden), jnp.float32),
             pltpu.VMEM((b_dev, hidden), jnp.bfloat16),
             pltpu.VMEM((b_dev, width), jnp.float32),
-            pltpu.SemaphoreType.DMA((4 + blocks,)),
+            pltpu.SemaphoreType.DMA((4 + len(FRONT_BLOCKS),)),
         ],
         compiler_params=params(20),
         name="front",
@@ -277,7 +289,6 @@
     near = lax.dynamic_index_in_dim(local, core, 2, keepdims=False).reshape(slots, -1)
     far = lax.dynamic_index_in_dim(local, 1 - core, 2, keepdims=False).reshape(slots, -1)
     local = jnp.concatenate([near, far], axis=1)
-    grads, local = lax.optimization_barrier((grads, local))
     part = weight_part((top_input, top_core, top_pair, top_both), grads)
 
     received = lax.all_to_all(ordered, "hst", split_axis=0, concat_axis=1, tiled=True)[0]

time: 85.3 us -> 84.7 us (level)
  waiting for transfers between devices: 7.63 us -> 9.5 us
  local copies, waits for them, and re-layouts: 3.45 us -> 1.78 us
  blocking collectives: 18.3 us -> 16.8 us
  starting transfers between devices: 35.8 us -> 36.7 us
    ppermute x8, starting transfers between devices: 3.93 us -> 7.21 us  [core_swap(): lax.ppermute(value, AXES, permutation(lambda x, y, z, c: (x, y, z, 1 - c)))]
    ppermute x2, starting transfers between devices: 4.23 us -> 2.67 us  [pair_swap(): lax.ppermute(value, AXES, permutation(lambda x, y, z, c: (x, y, z ^ 1, c)))]
    all_to_all x1, blocking collectives: 18.3 us -> 16.8 us  [body(): lax.all_to_all(summed.reshape(NZ * NC, rows_out, quart), 'chip', split_ax...]
    ppermute x2, waiting for transfers between devices: 0.01 us -> 1.08 us  [pair_swap(): lax.ppermute(value, AXES, permutation(lambda x, y, z, c: (x, y, z ^ 1, c)))]
    another operation x1, local copies, waits for them, and re-layouts: 2.44 us -> 1.57 us  [body(): ids = lookup_ids[0].reshape(slots, NX * NY, NZ, NC, b_dev)]
  transfers between devices with their start and end apart: 19 -> 19, of which waited for: 7 -> 10; matrix products, arithmetic and copies ran while one was open for 4% -> 2% of each run, Pallas kernels for 21% -> 21%
where the time goes in v6:
time: 84.7 us; the launch traced here: 84.4 us
  starting transfers between devices  36.7 us (43%)
  Pallas kernels  18.6 us (22%)
  blocking collectives  16.8 us (20%)
  waiting for transfers between devices  9.5 us (11%)
  local copies, waits for them, and re-layouts  1.78 us (2%)
  between operations  0.91 us (1%)
    all_to_all x1, blocking collectives, body(): lax.all_to_all(summed.reshape(NZ * NC, rows_out, quart), 'chip', split_ax...  16.8 us
    ppermute x7, starting transfers between devices, z_shift(): lax.ppermute(value, AXES, permutation(lambda x, y, z, c: (x, y, (z + d) %...  16.2 us
    pallas_call x2, Pallas kernels, table_partial(): pl.pallas_call(functools.partial(table_kernel, 256, 512, first), out_shap...  7.51 us
    pallas_call x1, Pallas kernels, front(): pl.pallas_call(front_kernel, in_specs=[HBM] * 5, out_specs=[VMEM] * 3, ou...  7.41 us
    ppermute x8, starting transfers between devices, core_swap(): lax.ppermute(value, AXES, permutation(lambda x, y, z, c: (x, y, z, 1 - c)))  7.21 us
    all_to_all x1, starting transfers between devices, body(): lax.all_to_all(part.reshape(NX * NY, width // (NX * NY), quart), 'hst', s...  5.64 us
    ppermute x7, waiting for transfers between devices, z_shift(): lax.ppermute(value, AXES, permutation(lambda x, y, z, c: (x, y, (z + d) %...  5.61 us
    all_to_all x1, starting transfers between devices, body(): lax.all_to_all(ordered, 'hst', split_axis=0, concat_axis=1, tiled=True)[0]  5.02 us
  transfers between devices with their start and end apart: 19, of which 10 were waited for; matrix products, arithmetic and copies ran while one was open for 2% of the time, Pallas kernels for 21%

profile of v6, /device:TPU:1, one launch (start us, length us, event | category | flops | bytes accessed | tf_op | source)
XLA Modules:
  0.0 84.4 jit_solution(12442098986873889840)
XLA Ops:
  0.6 0.0 copy-start
  0.6 2.6 %collective-permute-start.1 = (bf16[128,2048]{1,0:T(8,128)(2,1)}, bf16[128,2048]{1,0:T(8,128)(2,1)S(1)}, u32[]{:S(2)}, u32[]{:S(2)}) collective-permute-start(bf16[128,2048]{1,0:T(8,128)(2,1)} %x0.1), channel_id=1, source_target_pairs={{0,2},{1,3},{2,0},{3,1},{4,6},{5,7},{6,4},{7,5},{8,10},{9,11},{10,... | collective-permute-start | bytes 1572872 | tf_op jit(solution)/shard_map/ppermute | solution.py:38
  3.2 0.0 copy-start.1
  3.2 7.4 %front.1 = (bf16[128,1024]{1,0:T(8,128)(2,1)S(1)}, bf16[128,1024]{1,0:T(8,128)(2,1)S(1)}, bf16[16,128,128]{2,1,0:T(8,128)(2,1)}) custom-call(s32[16]{0:T(128)} %map_hbm.1, bf16[128,2048]{1,0:T(8,128)(2,1)} %x0.1, bf16[128,2048]{1,0:T(8,128)(2,1)} %gh_hbm.1, bf16[2048,2048]{1,0:T(8,128)(2,1)} %w_hbm.1, f32[1,2048]{1,0:T(1,128)} %bitcast.62), custom_call_target="tpu_custom_call" | custom-call | tf_op jit(solution)/shard_map/front/pallas_call | solution.py:122
  10.6 0.1 collective-permute-start.2
  10.7 0.0 copy-done.1
  10.7 2.8 %collective-permute-start = (bf16[128,2048]{1,0:T(8,128)(2,1)S(1)}, bf16[128,2048]{1,0:T(8,128)(2,1)S(1)}, u32[]{:S(2)}, u32[]{:S(2)}) collective-permute-start(bf16[128,2048]{1,0:T(8,128)(2,1)S(1)} %copy-done.1), channel_id=1, source_target_pairs={{0,1},{1,0},{2,3},{3,2},{4,5},{5,4},{6,7},{7,6},{8,9},{9,8},{10,11... | collective-permute-start | bytes 1572872 | tf_op jit(solution)/shard_map/ppermute | solution.py:34
  13.5 5.0 %all-to-all-start.1 = ((bf16[16,128,128]{2,1,0:T(8,128)(2,1)}), bf16[16,128,128]{2,1,0:T(8,128)(2,1)S(1)}, u32[]{:S(2)}, u32[]{:S(2)}) async-start(bf16[16,128,128]{2,1,0:T(8,128)(2,1)} %get-tuple-element.22), calls=%async_computation.1 | async-start | bytes 1048576 | tf_op jit(solution)/shard_map/all_to_all | solution.py:294
  18.5 1.1 %collective-permute-done.2.g2 = bf16[128,1024]{1,0:T(8,128)(2,1)S(1)} collective-permute-done((bf16[128,1024]{1,0:T(8,128)(2,1)S(1)}, bf16[128,1024]{1,0:T(8,128)(2,1)S(1)}, u32[]{:S(2)}, u32[]{:S(2)}) %collective-permute-start.2) | collective-permute-done | bytes 262176 | tf_op jit(solution)/shard_map/ppermute | solution.py:38
  19.6 0.0 collective-permute-done.1.x2
  19.7 2.4 %collective-permute-start.3 = (bf16[32,2048]{1,0:T(8,128)(2,1)S(1)}, bf16[32,2048]{1,0:T(8,128)(2,1)S(1)}, u32[]{:S(2)}, u32[]{:S(2)}) collective-permute-start(bf16[32,2048]{1,0:T(8,128)(2,1)S(1)} %get-tuple-element.42), channel_id=1, source_target_pairs={{0,1},{1,0},{2,3},{3,2},{4,5},{5,4},{6,7},{7,6},{8,9},{9,8},{10,11... | collective-permute-start | bytes 393224 | tf_op jit(solution)/shard_map/ppermute | solution.py:34
  22.0 0.1 collective-permute-start.4
  22.1 0.4 collective-permute-start.5
  22.5 0.1 collective-permute-start.6
  22.6 0.4 collective-permute-done.3
  23.0 0.4 collective-permute-start.7
  23.4 0.0 collective-permute-done.4
  23.4 0.2 collective-permute-start.8
  23.6 0.0 collective-permute-done.5
  23.6 0.3 collective-permute-done.6
  23.9 0.6 collective-permute-done.7.g1
  24.6 0.0 collective-permute-done.x1
  24.6 0.4 collective-permute-done.8.g3
  24.9 2.6 %weight_part.1 = bf16[2048,512]{1,0:T(8,128)(2,1)} custom-call(bf16[128,2048]{1,0:T(8,128)(2,1)S(1)} %copy-done.1, bf16[128,2048]{1,0:T(8,128)(2,1)S(1)} %collective-permute-done.x1, bf16[128,2048]{1,0:T(8,128)(2,1)S(1)} %collective-permute-done.1.x2, bf16[128,2048]{1,0:T(8,128)(2,1)S(1)} %pad_maximum_fusion.x3, bf16[128,1024]{1,0:T(8,128)(2,1)S(1)} %get-tuple-element.20.g0, ...), custom_call_target="tpu_custom_call" | custom-call | tf_op jit(solution)/shard_map/weight_part/pallas_call | solution.py:160
  27.6 1.1 %all-to-all-done.1 = bf16[16,128,128]{2,1,0:T(8,128)(2,1)S(1)} async-done(((bf16[16,128,128]{2,1,0:T(8,128)(2,1)}), bf16[16,128,128]{2,1,0:T(8,128)(2,1)S(1)}, u32[]{:S(2)}, u32[]{:S(2)}) %all-to-all-start.1) | async-done | bytes 524320 | tf_op jit(solution)/shard_map/all_to_all | solution.py:294
  28.7 5.6 %all-to-all-start = ((bf16[16,128,512]{2,1,0:T(8,128)(2,1)}), bf16[16,128,512]{2,1,0:T(8,128)(2,1)S(1)}, u32[]{:S(2)}, u32[]{:S(2)}) async-start(bf16[16,128,512]{2,1,0:T(8,128)(2,1)} %bitcast.1), calls=%async_computation | async-start | bytes 4194304 | tf_op jit(solution)/shard_map/all_to_all | solution.py:297
  34.3 1.6 %reshape_squeeze.7 = s32[4,16,8,2,128]{4,3,2,1,0:T(2,128)S(1)} reshape(s32[1,4,32768]{2,1,0:T(4,128)} %param.12) | data formatting | bytes 1048576 | tf_op jit(solution)/shard_map/reshape;squeeze | solution.py:281
  35.9 0.0 copy-done
  36.0 0.1 fusion.5
  36.2 0.9 %collective-permute-start.9 = (bf16[2048,128]{1,0:T(8,128)(2,1)S(1)}, bf16[2048,128]{1,0:T(8,128)(2,1)S(1)}, u32[]{:S(2)}, u32[]{:S(2)}) collective-permute-start(bf16[2048,128]{1,0:T(8,128)(2,1)S(1)} %bitcast.57), channel_id=1, source_target_pairs={{0,1},{1,0},{2,3},{3,2},{4,5},{5,4},{6,7},{7,6},{8,9},{9,8},{10,11... | collective-permute-start | bytes 1572872 | tf_op jit(solution)/shard_map/ppermute | solution.py:34
  37.2 3.8 %table_own.1.refs_0_ = f32[2048,128]{1,0:T(8,128)S(1)} custom-call(s32[4,4096]{1,0:T(4,128)S(1)} %bitcast_dynamic-update-slice_fusion.ids_ref, bf16[2048,128]{1,0:T(8,128)(2,1)S(1)} %bitcast.58), custom_call_target="tpu_custom_call" | custom-call | tf_op jit(solution)/shard_map/table_own/pallas_call | solution.py:222
  41.0 0.0 collective-permute-done.9.x_ref
  41.0 3.8 %table_other.1 = bf16[2048,128]{1,0:T(8,128)(2,1)S(1)} custom-call(s32[4,4096]{1,0:T(4,128)S(1)} %bitcast_dynamic-update-slice_fusion.ids_ref, bf16[2048,128]{1,0:T(8,128)(2,1)S(1)} %collective-permute-done.9.x_ref, f32[2048,128]{1,0:T(8,128)S(1)} %table_own.1.refs_0_), custom_call_target="tpu_custom_call" | custom-call | tf_op jit(solution)/shard_map/table_other/pallas_call | solution.py:222
  44.8 0.1 dynamic-slice_bitcast_fusion
  44.8 6.8 %collective-permute-start.10 = (bf16[256,128]{1,0:T(8,128)(2,1)S(1)}, bf16[256,128]{1,0:T(8,128)(2,1)S(1)}, u32[]{:S(2)}, u32[]{:S(2)}) collective-permute-start(bf16[256,128]{1,0:T(8,128)(2,1)S(1)} %get-tuple-element.40), channel_id=1, source_target_pairs={{0,8},{1,9},{2,10},{3,11},{4,12},{5,13},{6,14},{7,15},{8,0},{9,1},... | collective-permute-start | bytes 196616 | tf_op jit(solution)/shard_map/ppermute | solution.py:42
  51.6 1.6 %collective-permute-start.11 = (bf16[256,128]{1,0:T(8,128)(2,1)S(1)}, bf16[256,128]{1,0:T(8,128)(2,1)S(1)}, u32[]{:S(2)}, u32[]{:S(2)}) collective-permute-start(bf16[256,128]{1,0:T(8,128)(2,1)S(1)} %get-tuple-element.39), channel_id=1, source_target_pairs={{0,6},{1,7},{2,8},{3,9},{4,10},{5,11},{6,12},{7,13},{8,14},{9,15},... | collective-permute-start | bytes 196616 | tf_op jit(solution)/shard_map/ppermute | solution.py:42
  53.3 2.8 %collective-permute-start.12 = (bf16[256,128]{1,0:T(8,128)(2,1)S(1)}, bf16[256,128]{1,0:T(8,128)(2,1)S(1)}, u32[]{:S(2)}, u32[]{:S(2)}) collective-permute-start(bf16[256,128]{1,0:T(8,128)(2,1)S(1)} %get-tuple-element.38), channel_id=1, source_target_pairs={{0,10},{1,11},{2,12},{3,13},{4,14},{5,15},{6,0},{7,1},{8,2},{9,3},... | collective-permute-start | bytes 196616 | tf_op jit(solution)/shard_map/ppermute | solution.py:42
  56.1 1.2 %collective-permute-start.13 = (bf16[256,128]{1,0:T(8,128)(2,1)S(1)}, bf16[256,128]{1,0:T(8,128)(2,1)S(1)}, u32[]{:S(2)}, u32[]{:S(2)}) collective-permute-start(bf16[256,128]{1,0:T(8,128)(2,1)S(1)} %get-tuple-element.37), channel_id=1, source_target_pairs={{0,4},{1,5},{2,6},{3,7},{4,8},{5,9},{6,10},{7,11},{8,12},{9,13},{1... | collective-permute-start | bytes 196616 | tf_op jit(solution)/shard_map/ppermute | solution.py:42
  57.3 2.4 %collective-permute-start.14 = (bf16[256,128]{1,0:T(8,128)(2,1)S(1)}, bf16[256,128]{1,0:T(8,128)(2,1)S(1)}, u32[]{:S(2)}, u32[]{:S(2)}) collective-permute-start(bf16[256,128]{1,0:T(8,128)(2,1)S(1)} %get-tuple-element.36), channel_id=1, source_target_pairs={{0,12},{1,13},{2,14},{3,15},{4,0},{5,1},{6,2},{7,3},{8,4},{9,5},{1... | collective-permute-start | bytes 196616 | tf_op jit(solution)/shard_map/ppermute | solution.py:42
  59.7 0.0 collective-permute-done.10.refs_1_
  59.7 0.7 collective-permute-start.15
  60.4 1.4 %collective-permute-done.11.refs_2_ = bf16[256,128]{1,0:T(8,128)(2,1)S(1)} collective-permute-done((bf16[256,128]{1,0:T(8,128)(2,1)S(1)}, bf16[256,128]{1,0:T(8,128)(2,1)S(1)}, u32[]{:S(2)}, u32[]{:S(2)}) %collective-permute-start.11) | collective-permute-done | bytes 65568 | tf_op jit(solution)/shard_map/ppermute | solution.py:42
  61.8 0.6 collective-permute-start.16
  62.4 0.0 collective-permute-done.12.refs_3_
  62.4 0.6 collective-permute-done.13.refs_4_
  63.0 1.9 %collective-permute-done.14.refs_5_ = bf16[256,128]{1,0:T(8,128)(2,1)S(1)} collective-permute-done((bf16[256,128]{1,0:T(8,128)(2,1)S(1)}, bf16[256,128]{1,0:T(8,128)(2,1)S(1)}, u32[]{:S(2)}, u32[]{:S(2)}) %collective-permute-start.14) | collective-permute-done | bytes 65568 | tf_op jit(solution)/shard_map/ppermute | solution.py:42
  64.9 0.0 collective-permute-done.15.refs_6_
  64.9 1.7 %collective-permute-done.16.refs_7_ = bf16[256,128]{1,0:T(8,128)(2,1)S(1)} collective-permute-done((bf16[256,128]{1,0:T(8,128)(2,1)S(1)}, bf16[256,128]{1,0:T(8,128)(2,1)S(1)}, u32[]{:S(2)}, u32[]{:S(2)}) %collective-permute-start.16) | collective-permute-done | bytes 65568 | tf_op jit(solution)/shard_map/ppermute | solution.py:42
  66.6 0.0 all-to-all-done.x_ref
  66.6 0.3 sum_blocks.1
  66.9 16.8 %all_to_all.19.w_ref = bf16[16,8,512]{2,1,0:T(8,128)(2,1)S(1)} all-to-all(bf16[16,8,512]{2,1,0:T(8,128)(2,1)S(1)} %bitcast.60), channel_id=1, replica_groups=mesh['hst'=16,'chip'=16] {'chip'}, dimensions={0} | all-to-all | bytes 262144 | tf_op jit(solution)/shard_map/all_to_all | solution.py:312
  83.7 0.7 last_sums.1
  (8 shorter events, 0.2 us)
Async XLA Ops:
  0.6 35.3 %copy-start = (s32[1,32768]{1,0:T(1,128)S(1)}, s32[1,32768]{1,0:T(1,128)}, u32[]{:S(2)}) copy-start(s32[1,32768]{1,0:T(1,128)} %param.13) | copy-start | bytes 393220
  0.6 19.0 %collective-permute-start.1 = (bf16[128,2048]{1,0:T(8,128)(2,1)}, bf16[128,2048]{1,0:T(8,128)(2,1)S(1)}, u32[]{:S(2)}, u32[]{:S(2)}) collective-permute-start(bf16[128,2048]{1,0:T(8,128)(2,1)} %x0.1), channel_id=1, source_target_pairs={{0,2},{1,3},{2,0},{3,1},{4,6},{5,7},{6,4},{7,5},{8,10},{9,11},{10,... | collective-permute-start | bytes 1572872 | tf_op jit(solution)/shard_map/ppermute | solution.py:38
  3.2 7.5 %copy-start.1 = (bf16[128,2048]{1,0:T(8,128)(2,1)S(1)}, bf16[128,2048]{1,0:T(8,128)(2,1)}, u32[]{:S(2)}) copy-start(bf16[128,2048]{1,0:T(8,128)(2,1)} %x0.1) | copy-start | bytes 1572868
  10.6 9.0 %collective-permute-start.2 = (bf16[128,1024]{1,0:T(8,128)(2,1)S(1)}, bf16[128,1024]{1,0:T(8,128)(2,1)S(1)}, u32[]{:S(2)}, u32[]{:S(2)}) collective-permute-start(bf16[128,1024]{1,0:T(8,128)(2,1)S(1)} %get-tuple-element.18), channel_id=1, source_target_pairs={{0,2},{1,3},{2,0},{3,1},{4,6},{5,7},{6,4},{7,5},{8,10},{9,11},{10,... | collective-permute-start | bytes 786440 | tf_op jit(solution)/shard_map/ppermute | solution.py:38
  10.7 13.8 %collective-permute-start = (bf16[128,2048]{1,0:T(8,128)(2,1)S(1)}, bf16[128,2048]{1,0:T(8,128)(2,1)S(1)}, u32[]{:S(2)}, u32[]{:S(2)}) collective-permute-start(bf16[128,2048]{1,0:T(8,128)(2,1)S(1)} %copy-done.1), channel_id=1, source_target_pairs={{0,1},{1,0},{2,3},{3,2},{4,5},{5,4},{6,7},{7,6},{8,9},{9,8},{10,11... | collective-permute-start | bytes 1572872 | tf_op jit(solution)/shard_map/ppermute | solution.py:34
  13.5 15.2 %all-to-all-start.1 = ((bf16[16,128,128]{2,1,0:T(8,128)(2,1)}), bf16[16,128,128]{2,1,0:T(8,128)(2,1)S(1)}, u32[]{:S(2)}, u32[]{:S(2)}) async-start(bf16[16,128,128]{2,1,0:T(8,128)(2,1)} %get-tuple-element.22), calls=%async_computation.1 | async-start | bytes 1048576 | tf_op jit(solution)/shard_map/all_to_all | solution.py:294
  19.7 3.4 %collective-permute-start.3 = (bf16[32,2048]{1,0:T(8,128)(2,1)S(1)}, bf16[32,2048]{1,0:T(8,128)(2,1)S(1)}, u32[]{:S(2)}, u32[]{:S(2)}) collective-permute-start(bf16[32,2048]{1,0:T(8,128)(2,1)S(1)} %get-tuple-element.42), channel_id=1, source_target_pairs={{0,1},{1,0},{2,3},{3,2},{4,5},{5,4},{6,7},{7,6},{8,9},{9,8},{10,11... | collective-permute-start | bytes 393224 | tf_op jit(solution)/shard_map/ppermute | solution.py:34
  22.0 1.4 %collective-permute-start.4 = (bf16[32,2048]{1,0:T(8,128)(2,1)S(1)}, bf16[32,2048]{1,0:T(8,128)(2,1)S(1)}, u32[]{:S(2)}, u32[]{:S(2)}) collective-permute-start(bf16[32,2048]{1,0:T(8,128)(2,1)S(1)} %get-tuple-element.45), channel_id=1, source_target_pairs={{0,1},{1,0},{2,3},{3,2},{4,5},{5,4},{6,7},{7,6},{8,9},{9,8},{10,11... | collective-permute-start | bytes 393224 | tf_op jit(solution)/shard_map/ppermute | solution.py:34
  22.1 1.4 %collective-permute-start.5 = (bf16[32,2048]{1,0:T(8,128)(2,1)S(1)}, bf16[32,2048]{1,0:T(8,128)(2,1)S(1)}, u32[]{:S(2)}, u32[]{:S(2)}) collective-permute-start(bf16[32,2048]{1,0:T(8,128)(2,1)S(1)} %get-tuple-element.44), channel_id=1, source_target_pairs={{0,1},{1,0},{2,3},{3,2},{4,5},{5,4},{6,7},{7,6},{8,9},{9,8},{10,11... | collective-permute-start | bytes 393224 | tf_op jit(solution)/shard_map/ppermute | solution.py:34
  22.5 1.3 %collective-permute-start.6 = (bf16[32,2048]{1,0:T(8,128)(2,1)S(1)}, bf16[32,2048]{1,0:T(8,128)(2,1)S(1)}, u32[]{:S(2)}, u32[]{:S(2)}) collective-permute-start(bf16[32,2048]{1,0:T(8,128)(2,1)S(1)} %get-tuple-element.43), channel_id=1, source_target_pairs={{0,1},{1,0},{2,3},{3,2},{4,5},{5,4},{6,7},{7,6},{8,9},{9,8},{10,11... | collective-permute-start | bytes 393224 | tf_op jit(solution)/shard_map/ppermute | solution.py:34
  23.0 1.5 %collective-permute-start.7 = (bf16[128,1024]{1,0:T(8,128)(2,1)S(1)}, bf16[128,1024]{1,0:T(8,128)(2,1)S(1)}, u32[]{:S(2)}, u32[]{:S(2)}) collective-permute-start(bf16[128,1024]{1,0:T(8,128)(2,1)S(1)} %get-tuple-element.20.g0), channel_id=1, source_target_pairs={{0,1},{1,0},{2,3},{3,2},{4,5},{5,4},{6,7},{7,6},{8,9},{9,8},{10,11... | collective-permute-start | bytes 786440 | tf_op jit(solution)/shard_map/ppermute | solution.py:34
  23.4 1.5 %collective-permute-start.8 = (bf16[128,1024]{1,0:T(8,128)(2,1)S(1)}, bf16[128,1024]{1,0:T(8,128)(2,1)S(1)}, u32[]{:S(2)}, u32[]{:S(2)}) collective-permute-start(bf16[128,1024]{1,0:T(8,128)(2,1)S(1)} %collective-permute-done.2.g2), channel_id=1, source_target_pairs={{0,1},{1,0},{2,3},{3,2},{4,5},{5,4},{6,7},{7,6},{8,9},{9,8},{10,11... | collective-permute-start | bytes 786440 | tf_op jit(solution)/shard_map/ppermute | solution.py:34
  28.7 37.9 %all-to-all-start = ((bf16[16,128,512]{2,1,0:T(8,128)(2,1)}), bf16[16,128,512]{2,1,0:T(8,128)(2,1)S(1)}, u32[]{:S(2)}, u32[]{:S(2)}) async-start(bf16[16,128,512]{2,1,0:T(8,128)(2,1)} %bitcast.1), calls=%async_computation | async-start | bytes 4194304 | tf_op jit(solution)/shard_map/all_to_all | solution.py:297
  36.2 4.8 %collective-permute-start.9 = (bf16[2048,128]{1,0:T(8,128)(2,1)S(1)}, bf16[2048,128]{1,0:T(8,128)(2,1)S(1)}, u32[]{:S(2)}, u32[]{:S(2)}) collective-permute-start(bf16[2048,128]{1,0:T(8,128)(2,1)S(1)} %bitcast.57), channel_id=1, source_target_pairs={{0,1},{1,0},{2,3},{3,2},{4,5},{5,4},{6,7},{7,6},{8,9},{9,8},{10,11... | collective-permute-start | bytes 1572872 | tf_op jit(solution)/shard_map/ppermute | solution.py:34
  44.8 14.9 %collective-permute-start.10 = (bf16[256,128]{1,0:T(8,128)(2,1)S(1)}, bf16[256,128]{1,0:T(8,128)(2,1)S(1)}, u32[]{:S(2)}, u32[]{:S(2)}) collective-permute-start(bf16[256,128]{1,0:T(8,128)(2,1)S(1)} %get-tuple-element.40), channel_id=1, source_target_pairs={{0,8},{1,9},{2,10},{3,11},{4,12},{5,13},{6,14},{7,15},{8,0},{9,1},... | collective-permute-start | bytes 196616 | tf_op jit(solution)/shard_map/ppermute | solution.py:42
  51.6 10.2 %collective-permute-start.11 = (bf16[256,128]{1,0:T(8,128)(2,1)S(1)}, bf16[256,128]{1,0:T(8,128)(2,1)S(1)}, u32[]{:S(2)}, u32[]{:S(2)}) collective-permute-start(bf16[256,128]{1,0:T(8,128)(2,1)S(1)} %get-tuple-element.39), channel_id=1, source_target_pairs={{0,6},{1,7},{2,8},{3,9},{4,10},{5,11},{6,12},{7,13},{8,14},{9,15},... | collective-permute-start | bytes 196616 | tf_op jit(solution)/shard_map/ppermute | solution.py:42
  53.3 9.1 %collective-permute-start.12 = (bf16[256,128]{1,0:T(8,128)(2,1)S(1)}, bf16[256,128]{1,0:T(8,128)(2,1)S(1)}, u32[]{:S(2)}, u32[]{:S(2)}) collective-permute-start(bf16[256,128]{1,0:T(8,128)(2,1)S(1)} %get-tuple-element.38), channel_id=1, source_target_pairs={{0,10},{1,11},{2,12},{3,13},{4,14},{5,15},{6,0},{7,1},{8,2},{9,3},... | collective-permute-start | bytes 196616 | tf_op jit(solution)/shard_map/ppermute | solution.py:42
  56.1 6.9 %collective-permute-start.13 = (bf16[256,128]{1,0:T(8,128)(2,1)S(1)}, bf16[256,128]{1,0:T(8,128)(2,1)S(1)}, u32[]{:S(2)}, u32[]{:S(2)}) collective-permute-start(bf16[256,128]{1,0:T(8,128)(2,1)S(1)} %get-tuple-element.37), channel_id=1, source_target_pairs={{0,4},{1,5},{2,6},{3,7},{4,8},{5,9},{6,10},{7,11},{8,12},{9,13},{1... | collective-permute-start | bytes 196616 | tf_op jit(solution)/shard_map/ppermute | solution.py:42
  57.3 7.6 %collective-permute-start.14 = (bf16[256,128]{1,0:T(8,128)(2,1)S(1)}, bf16[256,128]{1,0:T(8,128)(2,1)S(1)}, u32[]{:S(2)}, u32[]{:S(2)}) collective-permute-start(bf16[256,128]{1,0:T(8,128)(2,1)S(1)} %get-tuple-element.36), channel_id=1, source_target_pairs={{0,12},{1,13},{2,14},{3,15},{4,0},{5,1},{6,2},{7,3},{8,4},{9,5},{1... | collective-permute-start | bytes 196616 | tf_op jit(solution)/shard_map/ppermute | solution.py:42
  59.7 5.2 %collective-permute-start.15 = (bf16[256,128]{1,0:T(8,128)(2,1)S(1)}, bf16[256,128]{1,0:T(8,128)(2,1)S(1)}, u32[]{:S(2)}, u32[]{:S(2)}) collective-permute-start(bf16[256,128]{1,0:T(8,128)(2,1)S(1)} %get-tuple-element.35), channel_id=1, source_target_pairs={{0,2},{1,3},{2,4},{3,5},{4,6},{5,7},{6,8},{7,9},{8,10},{9,11},{10,... | collective-permute-start | bytes 196616 | tf_op jit(solution)/shard_map/ppermute | solution.py:42
  61.8 4.8 %collective-permute-start.16 = (bf16[256,128]{1,0:T(8,128)(2,1)S(1)}, bf16[256,128]{1,0:T(8,128)(2,1)S(1)}, u32[]{:S(2)}, u32[]{:S(2)}) collective-permute-start(bf16[256,128]{1,0:T(8,128)(2,1)S(1)} %get-tuple-element.34), channel_id=1, source_target_pairs={{0,14},{1,15},{2,0},{3,1},{4,2},{5,3},{6,4},{7,5},{8,6},{9,7},{10,... | collective-permute-start | bytes 196616 | tf_op jit(solution)/shard_map/ppermute | solution.py:42

commit v7 on v6

--- a/solution.py
+++ b/solution.py
@@ -270,9 +270,9 @@
     pair = pair_swap(give)
 
     top_pair, pair = lax.optimization_barrier((top_pair, pair))
-    piece = b_dev // 4
+    piece = b_dev // 2
     top_both = jnp.concatenate(
-        [core_swap(top_pair[k * piece : (k + 1) * piece]) for k in range(4)], axis=0
+        [core_swap(top_pair[k * piece : (k + 1) * piece]) for k in range(2)], axis=0
     )
 
     grads = (keep, core_swap(keep), pair, core_swap(pair))

time: 84.7 us -> 94.8 us (1.12)
  waiting for transfers between devices: 9.5 us -> 22.8 us
  blocking collectives: 16.8 us -> 12.3 us
  other arithmetic: 0.16 us -> 1.11 us
    ppermute x7, waiting for transfers between devices: 5.61 us -> 10.8 us  [z_shift(): lax.ppermute(value, AXES, permutation(lambda x, y, z, c: (x, y, (z + d) %...]
    ppermute x2, waiting for transfers between devices: 1.08 us -> 6.11 us  [pair_swap(): lax.ppermute(value, AXES, permutation(lambda x, y, z, c: (x, y, z ^ 1, c)))]
    all_to_all x1, blocking collectives: 16.8 us -> 12.3 us  [body(): lax.all_to_all(summed.reshape(NZ * NC, rows_out, quart), 'chip', split_ax...]
    all_to_all x1, waiting for transfers between devices: 1.12 us -> 5.4 us  [body(): lax.all_to_all(ordered, 'hst', split_axis=0, concat_axis=1, tiled=True)[0]]
    all_to_all x1, starting transfers between devices: 5.64 us -> 3.72 us  [body(): lax.all_to_all(part.reshape(NX * NY, width // (NX * NY), quart), 'hst', s...]
    all_to_all x1, starting transfers between devices: 5.02 us -> 6.75 us  [body(): lax.all_to_all(ordered, 'hst', split_axis=0, concat_axis=1, tiled=True)[0]]
    ppermute x8 -> x6, starting transfers between devices: 7.21 us -> 8.49 us  [core_swap(): lax.ppermute(value, AXES, permutation(lambda x, y, z, c: (x, y, z, 1 - c)))]
    ppermute x8 -> x6, waiting for transfers between devices: 1.69 us -> 0.44 us  [core_swap(): lax.ppermute(value, AXES, permutation(lambda x, y, z, c: (x, y, z, 1 - c)))]
  transfers between devices with their start and end apart: 19 -> 17, of which waited for: 10 -> 7; matrix products, arithmetic and copies ran while one was open for 2% -> 3% of each run, Pallas kernels for 21% -> 19%
where the time goes in v7:
time: 94.8 us; the launch traced here: 94.5 us
  starting transfers between devices  37 us (39%)
  waiting for transfers between devices  22.8 us (24%)
  Pallas kernels  18.5 us (20%)
  blocking collectives  12.3 us (13%)
  local copies, waits for them, and re-layouts  1.78 us (2%)
  other arithmetic  1.11 us (1%)
    ppermute x7, starting transfers between devices, z_shift(): lax.ppermute(value, AXES, permutation(lambda x, y, z, c: (x, y, (z + d) %...  15.4 us
    all_to_all x1, blocking collectives, body(): lax.all_to_all(summed.reshape(NZ * NC, rows_out, quart), 'chip', split_ax...  12.3 us
    ppermute x7, waiting for transfers between devices, z_shift(): lax.ppermute(value, AXES, permutation(lambda x, y, z, c: (x, y, (z + d) %...  10.8 us
    ppermute x6, starting transfers between devices, core_swap(): lax.ppermute(value, AXES, permutation(lambda x, y, z, c: (x, y, z, 1 - c)))  8.49 us
    pallas_call x2, Pallas kernels, table_partial(): pl.pallas_call(functools.partial(table_kernel, 256, 512, first), out_shap...  7.51 us
    pallas_call x1, Pallas kernels, front(): pl.pallas_call(front_kernel, in_specs=[HBM] * 5, out_specs=[VMEM] * 3, ou...  7.4 us
    all_to_all x1, starting transfers between devices, body(): lax.all_to_all(ordered, 'hst', split_axis=0, concat_axis=1, tiled=True)[0]  6.75 us
    ppermute x2, waiting for transfers between devices, pair_swap(): lax.ppermute(value, AXES, permutation(lambda x, y, z, c: (x, y, z ^ 1, c)))  6.11 us
  transfers between devices with their start and end apart: 17, of which 7 were waited for; matrix products, arithmetic and copies ran while one was open for 3% of the time, Pallas kernels for 19%

profile of v7, /device:TPU:1, one launch (start us, length us, event | category | flops | bytes accessed | tf_op | source)
XLA Modules:
  0.0 94.5 jit_solution(2763745497424878868)
XLA Ops:
  0.6 0.0 copy-start
  0.6 2.6 %collective-permute-start.1 = (bf16[128,2048]{1,0:T(8,128)(2,1)}, bf16[128,2048]{1,0:T(8,128)(2,1)S(1)}, u32[]{:S(2)}, u32[]{:S(2)}) collective-permute-start(bf16[128,2048]{1,0:T(8,128)(2,1)} %x0.1), channel_id=1, source_target_pairs={{0,2},{1,3},{2,0},{3,1},{4,6},{5,7},{6,4},{7,5},{8,10},{9,11},{10,... | collective-permute-start | bytes 1572872 | tf_op jit(solution)/shard_map/ppermute | solution.py:38
  3.2 0.0 copy-start.1
  3.2 7.4 %front.1 = (bf16[128,1024]{1,0:T(8,128)(2,1)S(1)}, bf16[128,1024]{1,0:T(8,128)(2,1)S(1)}, bf16[16,128,128]{2,1,0:T(8,128)(2,1)}) custom-call(s32[16]{0:T(128)} %map_hbm.1, bf16[128,2048]{1,0:T(8,128)(2,1)} %x0.1, bf16[128,2048]{1,0:T(8,128)(2,1)} %gh_hbm.1, bf16[2048,2048]{1,0:T(8,128)(2,1)} %w_hbm.1, f32[1,2048]{1,0:T(1,128)} %bitcast.62), custom_call_target="tpu_custom_call" | custom-call | tf_op jit(solution)/shard_map/front/pallas_call | solution.py:122
  10.6 0.1 collective-permute-start.2
  10.7 0.0 copy-done.1
  10.7 2.8 %collective-permute-start = (bf16[128,2048]{1,0:T(8,128)(2,1)S(1)}, bf16[128,2048]{1,0:T(8,128)(2,1)S(1)}, u32[]{:S(2)}, u32[]{:S(2)}) collective-permute-start(bf16[128,2048]{1,0:T(8,128)(2,1)S(1)} %copy-done.1), channel_id=1, source_target_pairs={{0,1},{1,0},{2,3},{3,2},{4,5},{5,4},{6,7},{7,6},{8,9},{9,8},{10,11... | collective-permute-start | bytes 1572872 | tf_op jit(solution)/shard_map/ppermute | solution.py:34
  13.5 6.1 %collective-permute-done.2.g2 = bf16[128,1024]{1,0:T(8,128)(2,1)S(1)} collective-permute-done((bf16[128,1024]{1,0:T(8,128)(2,1)S(1)}, bf16[128,1024]{1,0:T(8,128)(2,1)S(1)}, u32[]{:S(2)}, u32[]{:S(2)}) %collective-permute-start.2) | collective-permute-done | bytes 262176 | tf_op jit(solution)/shard_map/ppermute | solution.py:38
  19.6 0.0 collective-permute-done.1.x2
  19.7 2.4 %collective-permute-start.3 = (bf16[64,2048]{1,0:T(8,128)(2,1)S(1)}, bf16[64,2048]{1,0:T(8,128)(2,1)S(1)}, u32[]{:S(2)}, u32[]{:S(2)}) collective-permute-start(bf16[64,2048]{1,0:T(8,128)(2,1)S(1)} %get-tuple-element.42), channel_id=1, source_target_pairs={{0,1},{1,0},{2,3},{3,2},{4,5},{5,4},{6,7},{7,6},{8,9},{9,8},{10,11... | collective-permute-start | bytes 786440 | tf_op jit(solution)/shard_map/ppermute | solution.py:34
  22.0 0.1 collective-permute-start.4
  22.1 6.8 %all-to-all-start.1 = ((bf16[16,128,128]{2,1,0:T(8,128)(2,1)}), bf16[16,128,128]{2,1,0:T(8,128)(2,1)S(1)}, u32[]{:S(2)}, u32[]{:S(2)}) async-start(bf16[16,128,128]{2,1,0:T(8,128)(2,1)} %get-tuple-element.22), calls=%async_computation.1 | async-start | bytes 1048576 | tf_op jit(solution)/shard_map/all_to_all | solution.py:294
  28.9 0.8 collective-permute-start.5
  29.7 0.1 collective-permute-start.6
  29.8 0.0 collective-permute-done.3
  29.8 0.0 collective-permute-done.4
  29.8 1.0 %pad_maximum_fusion.x3 = bf16[128,2048]{1,0:T(8,128)(2,1)S(1)} fusion(bf16[64,2048]{1,0:T(8,128)(2,1)} %collective-permute-done.4, bf16[64,2048]{1,0:T(8,128)(2,1)S(1)} %collective-permute-done.3), kind=kLoop, calls=%fused_computation | loop fusion | flops 1048576 | bytes 1048576 | tf_op jit(solution)/shard_map/concatenate | solution.py:274
  30.8 0.1 collective-permute-done.5.g1
  30.8 0.0 collective-permute-done.x1
  30.8 0.4 collective-permute-done.6.g3
  31.2 2.6 %weight_part.1 = bf16[2048,512]{1,0:T(8,128)(2,1)} custom-call(bf16[128,2048]{1,0:T(8,128)(2,1)S(1)} %copy-done.1, bf16[128,2048]{1,0:T(8,128)(2,1)S(1)} %collective-permute-done.x1, bf16[128,2048]{1,0:T(8,128)(2,1)S(1)} %collective-permute-done.1.x2, bf16[128,2048]{1,0:T(8,128)(2,1)S(1)} %pad_maximum_fusion.x3, bf16[128,1024]{1,0:T(8,128)(2,1)S(1)} %get-tuple-element.20.g0, ...), custom_call_target="tpu_custom_call" | custom-call | tf_op jit(solution)/shard_map/weight_part/pallas_call | solution.py:160
  33.8 5.4 %all-to-all-done.1 = bf16[16,128,128]{2,1,0:T(8,128)(2,1)S(1)} async-done(((bf16[16,128,128]{2,1,0:T(8,128)(2,1)}), bf16[16,128,128]{2,1,0:T(8,128)(2,1)S(1)}, u32[]{:S(2)}, u32[]{:S(2)}) %all-to-all-start.1) | async-done | bytes 524320 | tf_op jit(solution)/shard_map/all_to_all | solution.py:294
  39.2 3.7 %all-to-all-start = ((bf16[16,128,512]{2,1,0:T(8,128)(2,1)}), bf16[16,128,512]{2,1,0:T(8,128)(2,1)S(1)}, u32[]{:S(2)}, u32[]{:S(2)}) async-start(bf16[16,128,512]{2,1,0:T(8,128)(2,1)} %bitcast.1), calls=%async_computation | async-start | bytes 4194304 | tf_op jit(solution)/shard_map/all_to_all | solution.py:297
  43.0 1.6 %reshape_squeeze.7 = s32[4,16,8,2,128]{4,3,2,1,0:T(2,128)S(1)} reshape(s32[1,4,32768]{2,1,0:T(4,128)} %param.12) | data formatting | bytes 1048576 | tf_op jit(solution)/shard_map/reshape;squeeze | solution.py:281
  44.6 0.0 copy-done
  44.7 0.1 fusion.5
  44.8 2.4 %collective-permute-start.7 = (bf16[2048,128]{1,0:T(8,128)(2,1)S(1)}, bf16[2048,128]{1,0:T(8,128)(2,1)S(1)}, u32[]{:S(2)}, u32[]{:S(2)}) collective-permute-start(bf16[2048,128]{1,0:T(8,128)(2,1)S(1)} %bitcast.57), channel_id=1, source_target_pairs={{0,1},{1,0},{2,3},{3,2},{4,5},{5,4},{6,7},{7,6},{8,9},{9,8},{10,11... | collective-permute-start | bytes 1572872 | tf_op jit(solution)/shard_map/ppermute | solution.py:34
  47.3 3.7 %table_own.1.refs_0_ = f32[2048,128]{1,0:T(8,128)S(1)} custom-call(s32[4,4096]{1,0:T(4,128)S(1)} %bitcast_dynamic-update-slice_fusion.ids_ref, bf16[2048,128]{1,0:T(8,128)(2,1)S(1)} %bitcast.58), custom_call_target="tpu_custom_call" | custom-call | tf_op jit(solution)/shard_map/table_own/pallas_call | solution.py:222
  51.1 0.0 collective-permute-done.7.x_ref
  51.1 3.8 %table_other.1 = bf16[2048,128]{1,0:T(8,128)(2,1)S(1)} custom-call(s32[4,4096]{1,0:T(4,128)S(1)} %bitcast_dynamic-update-slice_fusion.ids_ref, bf16[2048,128]{1,0:T(8,128)(2,1)S(1)} %collective-permute-done.7.x_ref, f32[2048,128]{1,0:T(8,128)S(1)} %table_own.1.refs_0_), custom_call_target="tpu_custom_call" | custom-call | tf_op jit(solution)/shard_map/table_other/pallas_call | solution.py:222
  54.9 0.1 dynamic-slice_bitcast_fusion
  54.9 6.4 %collective-permute-start.10 = (bf16[256,128]{1,0:T(8,128)(2,1)S(1)}, bf16[256,128]{1,0:T(8,128)(2,1)S(1)}, u32[]{:S(2)}, u32[]{:S(2)}) collective-permute-start(bf16[256,128]{1,0:T(8,128)(2,1)S(1)} %get-tuple-element.38), channel_id=1, source_target_pairs={{0,10},{1,11},{2,12},{3,13},{4,14},{5,15},{6,0},{7,1},{8,2},{9,3},... | collective-permute-start | bytes 196616 | tf_op jit(solution)/shard_map/ppermute | solution.py:42
  61.3 1.2 %collective-permute-start.11 = (bf16[256,128]{1,0:T(8,128)(2,1)S(1)}, bf16[256,128]{1,0:T(8,128)(2,1)S(1)}, u32[]{:S(2)}, u32[]{:S(2)}) collective-permute-start(bf16[256,128]{1,0:T(8,128)(2,1)S(1)} %get-tuple-element.37), channel_id=1, source_target_pairs={{0,4},{1,5},{2,6},{3,7},{4,8},{5,9},{6,10},{7,11},{8,12},{9,13},{1... | collective-permute-start | bytes 196616 | tf_op jit(solution)/shard_map/ppermute | solution.py:42
  62.5 2.4 %collective-permute-start.12 = (bf16[256,128]{1,0:T(8,128)(2,1)S(1)}, bf16[256,128]{1,0:T(8,128)(2,1)S(1)}, u32[]{:S(2)}, u32[]{:S(2)}) collective-permute-start(bf16[256,128]{1,0:T(8,128)(2,1)S(1)} %get-tuple-element.36), channel_id=1, source_target_pairs={{0,12},{1,13},{2,14},{3,15},{4,0},{5,1},{6,2},{7,3},{8,4},{9,5},{1... | collective-permute-start | bytes 196616 | tf_op jit(solution)/shard_map/ppermute | solution.py:42
  64.9 0.7 collective-permute-start.13
  65.6 1.9 %collective-permute-start.14 = (bf16[256,128]{1,0:T(8,128)(2,1)S(1)}, bf16[256,128]{1,0:T(8,128)(2,1)S(1)}, u32[]{:S(2)}, u32[]{:S(2)}) collective-permute-start(bf16[256,128]{1,0:T(8,128)(2,1)S(1)} %get-tuple-element.34), channel_id=1, source_target_pairs={{0,14},{1,15},{2,0},{3,1},{4,2},{5,3},{6,4},{7,5},{8,6},{9,7},{10,... | collective-permute-start | bytes 196616 | tf_op jit(solution)/shard_map/ppermute | solution.py:42
  67.5 0.0 collective-permute-done.10.refs_3_
  67.5 0.9 collective-permute-start.8
  68.5 0.2 collective-permute-done.11.refs_4_
  68.7 1.8 %collective-permute-start.9 = (bf16[256,128]{1,0:T(8,128)(2,1)S(1)}, bf16[256,128]{1,0:T(8,128)(2,1)S(1)}, u32[]{:S(2)}, u32[]{:S(2)}) collective-permute-start(bf16[256,128]{1,0:T(8,128)(2,1)S(1)} %get-tuple-element.39), channel_id=1, source_target_pairs={{0,6},{1,7},{2,8},{3,9},{4,10},{5,11},{6,12},{7,13},{8,14},{9,15},... | collective-permute-start | bytes 196616 | tf_op jit(solution)/shard_map/ppermute | solution.py:42
  70.5 0.0 collective-permute-done.12.refs_5_
  70.5 0.0 collective-permute-done.13.refs_6_
  70.5 0.0 collective-permute-done.14.refs_7_
  70.5 4.2 %collective-permute-done.8.refs_1_ = bf16[256,128]{1,0:T(8,128)(2,1)S(1)} collective-permute-done((bf16[256,128]{1,0:T(8,128)(2,1)S(1)}, bf16[256,128]{1,0:T(8,128)(2,1)S(1)}, u32[]{:S(2)}, u32[]{:S(2)}) %collective-permute-start.8) | collective-permute-done | bytes 65568 | tf_op jit(solution)/shard_map/ppermute | solution.py:42
  74.7 6.4 %collective-permute-done.9.refs_2_ = bf16[256,128]{1,0:T(8,128)(2,1)S(1)} collective-permute-done((bf16[256,128]{1,0:T(8,128)(2,1)S(1)}, bf16[256,128]{1,0:T(8,128)(2,1)S(1)}, u32[]{:S(2)}, u32[]{:S(2)}) %collective-permute-start.9) | collective-permute-done | bytes 65568 | tf_op jit(solution)/shard_map/ppermute | solution.py:42
  81.1 0.0 all-to-all-done.x_ref
  81.1 0.3 sum_blocks.1
  81.4 12.3 %all_to_all.19.w_ref = bf16[16,8,512]{2,1,0:T(8,128)(2,1)S(1)} all-to-all(bf16[16,8,512]{2,1,0:T(8,128)(2,1)S(1)} %bitcast.60), channel_id=1, replica_groups=mesh['hst'=16,'chip'=16] {'chip'}, dimensions={0} | all-to-all | bytes 262144 | tf_op jit(solution)/shard_map/all_to_all | solution.py:312
  93.7 0.7 last_sums.1
  (7 shorter events, 0.1 us)
Async XLA Ops:
  0.6 43.9 %copy-start = (s32[1,32768]{1,0:T(1,128)S(1)}, s32[1,32768]{1,0:T(1,128)}, u32[]{:S(2)}) copy-start(s32[1,32768]{1,0:T(1,128)} %param.13) | copy-start | bytes 393220
  0.6 19.0 %collective-permute-start.1 = (bf16[128,2048]{1,0:T(8,128)(2,1)}, bf16[128,2048]{1,0:T(8,128)(2,1)S(1)}, u32[]{:S(2)}, u32[]{:S(2)}) collective-permute-start(bf16[128,2048]{1,0:T(8,128)(2,1)} %x0.1), channel_id=1, source_target_pairs={{0,2},{1,3},{2,0},{3,1},{4,6},{5,7},{6,4},{7,5},{8,10},{9,11},{10,... | collective-permute-start | bytes 1572872 | tf_op jit(solution)/shard_map/ppermute | solution.py:38
  3.2 7.5 %copy-start.1 = (bf16[128,2048]{1,0:T(8,128)(2,1)S(1)}, bf16[128,2048]{1,0:T(8,128)(2,1)}, u32[]{:S(2)}) copy-start(bf16[128,2048]{1,0:T(8,128)(2,1)} %x0.1) | copy-start | bytes 1572868
  10.6 9.0 %collective-permute-start.2 = (bf16[128,1024]{1,0:T(8,128)(2,1)S(1)}, bf16[128,1024]{1,0:T(8,128)(2,1)S(1)}, u32[]{:S(2)}, u32[]{:S(2)}) collective-permute-start(bf16[128,1024]{1,0:T(8,128)(2,1)S(1)} %get-tuple-element.18), channel_id=1, source_target_pairs={{0,2},{1,3},{2,0},{3,1},{4,6},{5,7},{6,4},{7,5},{8,10},{9,11},{10,... | collective-permute-start | bytes 786440 | tf_op jit(solution)/shard_map/ppermute | solution.py:38
  10.7 20.1 %collective-permute-start = (bf16[128,2048]{1,0:T(8,128)(2,1)S(1)}, bf16[128,2048]{1,0:T(8,128)(2,1)S(1)}, u32[]{:S(2)}, u32[]{:S(2)}) collective-permute-start(bf16[128,2048]{1,0:T(8,128)(2,1)S(1)} %copy-done.1), channel_id=1, source_target_pairs={{0,1},{1,0},{2,3},{3,2},{4,5},{5,4},{6,7},{7,6},{8,9},{9,8},{10,11... | collective-permute-start | bytes 1572872 | tf_op jit(solution)/shard_map/ppermute | solution.py:34
  19.7 10.1 %collective-permute-start.3 = (bf16[64,2048]{1,0:T(8,128)(2,1)S(1)}, bf16[64,2048]{1,0:T(8,128)(2,1)S(1)}, u32[]{:S(2)}, u32[]{:S(2)}) collective-permute-start(bf16[64,2048]{1,0:T(8,128)(2,1)S(1)} %get-tuple-element.42), channel_id=1, source_target_pairs={{0,1},{1,0},{2,3},{3,2},{4,5},{5,4},{6,7},{7,6},{8,9},{9,8},{10,11... | collective-permute-start | bytes 786440 | tf_op jit(solution)/shard_map/ppermute | solution.py:34
  22.0 7.7 %collective-permute-start.4 = (bf16[64,2048]{1,0:T(8,128)(2,1)S(1)}, bf16[64,2048]{1,0:T(8,128)(2,1)}, u32[]{:S(2)}, u32[]{:S(2)}) collective-permute-start(bf16[64,2048]{1,0:T(8,128)(2,1)S(1)} %get-tuple-element.43), channel_id=1, source_target_pairs={{0,1},{1,0},{2,3},{3,2},{4,5},{5,4},{6,7},{7,6},{8,9},{9,8},{10,11... | collective-permute-start | bytes 786440 | tf_op jit(solution)/shard_map/ppermute | solution.py:34
  22.1 17.1 %all-to-all-start.1 = ((bf16[16,128,128]{2,1,0:T(8,128)(2,1)}), bf16[16,128,128]{2,1,0:T(8,128)(2,1)S(1)}, u32[]{:S(2)}, u32[]{:S(2)}) async-start(bf16[16,128,128]{2,1,0:T(8,128)(2,1)} %get-tuple-element.22), calls=%async_computation.1 | async-start | bytes 1048576 | tf_op jit(solution)/shard_map/all_to_all | solution.py:294
  28.9 1.9 %collective-permute-start.5 = (bf16[128,1024]{1,0:T(8,128)(2,1)S(1)}, bf16[128,1024]{1,0:T(8,128)(2,1)S(1)}, u32[]{:S(2)}, u32[]{:S(2)}) collective-permute-start(bf16[128,1024]{1,0:T(8,128)(2,1)S(1)} %get-tuple-element.20.g0), channel_id=1, source_target_pairs={{0,1},{1,0},{2,3},{3,2},{4,5},{5,4},{6,7},{7,6},{8,9},{9,8},{10,11... | collective-permute-start | bytes 786440 | tf_op jit(solution)/shard_map/ppermute | solution.py:34
  29.7 1.5 %collective-permute-start.6 = (bf16[128,1024]{1,0:T(8,128)(2,1)S(1)}, bf16[128,1024]{1,0:T(8,128)(2,1)S(1)}, u32[]{:S(2)}, u32[]{:S(2)}) collective-permute-start(bf16[128,1024]{1,0:T(8,128)(2,1)S(1)} %collective-permute-done.2.g2), channel_id=1, source_target_pairs={{0,1},{1,0},{2,3},{3,2},{4,5},{5,4},{6,7},{7,6},{8,9},{9,8},{10,11... | collective-permute-start | bytes 786440 | tf_op jit(solution)/shard_map/ppermute | solution.py:34
  39.2 41.9 %all-to-all-start = ((bf16[16,128,512]{2,1,0:T(8,128)(2,1)}), bf16[16,128,512]{2,1,0:T(8,128)(2,1)S(1)}, u32[]{:S(2)}, u32[]{:S(2)}) async-start(bf16[16,128,512]{2,1,0:T(8,128)(2,1)} %bitcast.1), calls=%async_computation | async-start | bytes 4194304 | tf_op jit(solution)/shard_map/all_to_all | solution.py:297
  44.8 6.3 %collective-permute-start.7 = (bf16[2048,128]{1,0:T(8,128)(2,1)S(1)}, bf16[2048,128]{1,0:T(8,128)(2,1)S(1)}, u32[]{:S(2)}, u32[]{:S(2)}) collective-permute-start(bf16[2048,128]{1,0:T(8,128)(2,1)S(1)} %bitcast.57), channel_id=1, source_target_pairs={{0,1},{1,0},{2,3},{3,2},{4,5},{5,4},{6,7},{7,6},{8,9},{9,8},{10,11... | collective-permute-start | bytes 1572872 | tf_op jit(solution)/shard_map/ppermute | solution.py:34
  54.9 12.6 %collective-permute-start.10 = (bf16[256,128]{1,0:T(8,128)(2,1)S(1)}, bf16[256,128]{1,0:T(8,128)(2,1)S(1)}, u32[]{:S(2)}, u32[]{:S(2)}) collective-permute-start(bf16[256,128]{1,0:T(8,128)(2,1)S(1)} %get-tuple-element.38), channel_id=1, source_target_pairs={{0,10},{1,11},{2,12},{3,13},{4,14},{5,15},{6,0},{7,1},{8,2},{9,3},... | collective-permute-start | bytes 196616 | tf_op jit(solution)/shard_map/ppermute | solution.py:42
  61.3 7.4 %collective-permute-start.11 = (bf16[256,128]{1,0:T(8,128)(2,1)S(1)}, bf16[256,128]{1,0:T(8,128)(2,1)S(1)}, u32[]{:S(2)}, u32[]{:S(2)}) collective-permute-start(bf16[256,128]{1,0:T(8,128)(2,1)S(1)} %get-tuple-element.37), channel_id=1, source_target_pairs={{0,4},{1,5},{2,6},{3,7},{4,8},{5,9},{6,10},{7,11},{8,12},{9,13},{1... | collective-permute-start | bytes 196616 | tf_op jit(solution)/shard_map/ppermute | solution.py:42
  62.5 8.1 %collective-permute-start.12 = (bf16[256,128]{1,0:T(8,128)(2,1)S(1)}, bf16[256,128]{1,0:T(8,128)(2,1)S(1)}, u32[]{:S(2)}, u32[]{:S(2)}) collective-permute-start(bf16[256,128]{1,0:T(8,128)(2,1)S(1)} %get-tuple-element.36), channel_id=1, source_target_pairs={{0,12},{1,13},{2,14},{3,15},{4,0},{5,1},{6,2},{7,3},{8,4},{9,5},{1... | collective-permute-start | bytes 196616 | tf_op jit(solution)/shard_map/ppermute | solution.py:42
  64.9 5.7 %collective-permute-start.13 = (bf16[256,128]{1,0:T(8,128)(2,1)S(1)}, bf16[256,128]{1,0:T(8,128)(2,1)S(1)}, u32[]{:S(2)}, u32[]{:S(2)}) collective-permute-start(bf16[256,128]{1,0:T(8,128)(2,1)S(1)} %get-tuple-element.35), channel_id=1, source_target_pairs={{0,2},{1,3},{2,4},{3,5},{4,6},{5,7},{6,8},{7,9},{8,10},{9,11},{10,... | collective-permute-start | bytes 196616 | tf_op jit(solution)/shard_map/ppermute | solution.py:42
  65.6 4.9 %collective-permute-start.14 = (bf16[256,128]{1,0:T(8,128)(2,1)S(1)}, bf16[256,128]{1,0:T(8,128)(2,1)S(1)}, u32[]{:S(2)}, u32[]{:S(2)}) collective-permute-start(bf16[256,128]{1,0:T(8,128)(2,1)S(1)} %get-tuple-element.34), channel_id=1, source_target_pairs={{0,14},{1,15},{2,0},{3,1},{4,2},{5,3},{6,4},{7,5},{8,6},{9,7},{10,... | collective-permute-start | bytes 196616 | tf_op jit(solution)/shard_map/ppermute | solution.py:42
  67.5 7.2 %collective-permute-start.8 = (bf16[256,128]{1,0:T(8,128)(2,1)S(1)}, bf16[256,128]{1,0:T(8,128)(2,1)S(1)}, u32[]{:S(2)}, u32[]{:S(2)}) collective-permute-start(bf16[256,128]{1,0:T(8,128)(2,1)S(1)} %get-tuple-element.40), channel_id=1, source_target_pairs={{0,8},{1,9},{2,10},{3,11},{4,12},{5,13},{6,14},{7,15},{8,0},{9,1},... | collective-permute-start | bytes 196616 | tf_op jit(solution)/shard_map/ppermute | solution.py:42
  68.7 12.4 %collective-permute-start.9 = (bf16[256,128]{1,0:T(8,128)(2,1)S(1)}, bf16[256,128]{1,0:T(8,128)(2,1)S(1)}, u32[]{:S(2)}, u32[]{:S(2)}) collective-permute-start(bf16[256,128]{1,0:T(8,128)(2,1)S(1)} %get-tuple-element.39), channel_id=1, source_target_pairs={{0,6},{1,7},{2,8},{3,9},{4,10},{5,11},{6,12},{7,13},{8,14},{9,15},... | collective-permute-start | bytes 196616 | tf_op jit(solution)/shard_map/ppermute | solution.py:42
